TPU v7x, 32 devices: a whole 2x2x4 slice. The times are simulated.
32 devices in a mesh: dp: 4 (over y, x), fsdp: 8 (over z, core).
Axes of the slice: x: 2, y: 2, z: 4, core: 2. Of those that a mesh axis runs over, the one named last changes fastest.
Arguments:
- tokens: bfloat16 [384, 256, 512], P(('dp', 'fsdp')), may hold values from -6 to 6
- lengths: int32 [384], P(('dp', 'fsdp')), may hold values from 64 to 250, as said below
- cotangent: bfloat16 [384, 256, 512], P(('dp', 'fsdp')), may hold values from -6 to 6
- qkv_weight: float32 [512, 1536], P(('dp', 'fsdp')), may hold values from -0.25 to 0.25
- out_weight: float32 [512, 512], P(('dp', 'fsdp')), may hold values from -2 to 2
- up_weight: float32 [512, 2048], P(('dp', 'fsdp')), may hold values from -0.25 to 0.25
- down_weight: float32 [2048, 512], P(('dp', 'fsdp')), may hold values from -0.125 to 0.125
- gains: float32 [2, 512], P(None, ('dp', 'fsdp')), may hold values from 0.1 to 1.9
- biases: float32 [6, 512], P(None, ('dp', 'fsdp')), may hold values from -1 to 1
- up_bias: float32 [2048], P(('dp', 'fsdp')), may hold values from -1 to 1
Outputs:
- output: bfloat16 [384, 256, 512], P(('dp', 'fsdp'))
- tokens_grad: bfloat16 [384, 256, 512], P(('dp', 'fsdp'))
- qkv_grad: float32 [512, 1536], P(('dp', 'fsdp'))
- out_grad: float32 [512, 512], P(('dp', 'fsdp'))
- up_grad: float32 [512, 2048], P(('dp', 'fsdp'))
- down_grad: float32 [2048, 512], P(('dp', 'fsdp'))
- gains_grad: float32 [2, 512], P(None, ('dp', 'fsdp'))
- biases_grad: float32 [6, 512], P(None, ('dp', 'fsdp'))
- up_bias_grad: float32 [2048], P(('dp', 'fsdp'))
Inputs may be any that keep to these rules, and one draw needn't show every extreme that they name: `lengths`: each length is 64, 128 or 250, and each of the three occurs.
All inputs are finite; a program needn't handle non-finite values.
Results may differ from a plain program's by a relative error of at most 0.012.
The roundings to bfloat16 on the way count: a program that leaves them out, or rounds other values in their place, can miss the bound.
Values may be sent and summed in bfloat16 or wider, within the bound.
A program may use at most 128 MiB of HBM per device.

v0:
```python
import math

import jax
import jax.numpy as jnp
from jax import lax
from jax.sharding import PartitionSpec as P

HEADS = 8


EPSILON = 1e-05
CONTRACT_ROWS = (((0,), (0,)), ((), ()))
CONTRACT_COLS = (((1,), (1,)), ((), ()))


def normalize(values):
    center = values - jnp.mean(values, -1, keepdims=True)
    inverse = lax.rsqrt(jnp.mean(center * center, -1, keepdims=True) + EPSILON)
    return (center * inverse, inverse)


def normalize_back(grad_norm, normed, inverse, gain):
    scaled = grad_norm * gain
    return inverse * (
        scaled
        - jnp.mean(scaled, -1, keepdims=True)
        - normed * jnp.mean(scaled * normed, -1, keepdims=True)
    )


def add_all(totals, increments):
    return tuple((total + extra for total, extra in zip(totals, increments)))


def forward(token_part, length_part, params):
    qkv_w, out_w, up_w, down_w, gains, biases, up_b = params
    gain_f = gains.astype(jnp.float32)
    bias_f = biases.astype(jnp.float32)
    up_bias_f = up_b.astype(jnp.float32)
    group, seq_len, model_width = token_part.shape
    rows = group * seq_len
    head_size = model_width // HEADS
    score_scale = head_size ** (-0.5)
    inputs = token_part.astype(jnp.float32).reshape(rows, model_width)
    normed_one, inverse_one = normalize(inputs)
    act_one = (normed_one * gain_f[0] + bias_f[0]).astype(jnp.bfloat16)
    joined = jnp.dot(act_one, qkv_w, preferred_element_type=jnp.float32)
    queries = (
        (joined[:, :model_width] + bias_f[1])
        .astype(jnp.bfloat16)
        .reshape(group, seq_len, HEADS, head_size)
    )
    key_rows = (
        joined[:, model_width : 2 * model_width]
        .astype(jnp.bfloat16)
        .reshape(group, seq_len, HEADS, head_size)
    )
    values = (
        (joined[:, 2 * model_width :] + bias_f[2])
        .astype(jnp.bfloat16)
        .reshape(group, seq_len, HEADS, head_size)
    )
    scores = (
        jnp.einsum("bqhd,bkhd->bhqk", queries, key_rows, preferred_element_type=jnp.float32)
        * score_scale
    )
    key_valid = (jnp.arange(seq_len)[None, :] < length_part[:, None])[:, None, None, :]
    logits = jnp.where(key_valid, scores, -1e30)
    highest = jnp.max(logits, -1, keepdims=True)
    exponent = jnp.exp(logits - highest)
    attn_probs = exponent / jnp.sum(exponent, -1, keepdims=True)
    probs_low = attn_probs.astype(jnp.bfloat16)
    context = jnp.einsum("bhqk,bkhd->bqhd", probs_low, values, preferred_element_type=jnp.float32)
    context = context.reshape(rows, model_width).astype(jnp.bfloat16)
    residual = inputs + jnp.dot(context, out_w, preferred_element_type=jnp.float32) + bias_f[3]
    normed_two, inverse_two = normalize(residual)
    act_two = (normed_two * gain_f[1] + bias_f[4]).astype(jnp.bfloat16)
    preact = jnp.dot(act_two, up_w, preferred_element_type=jnp.float32) + up_bias_f
    hidden = jax.nn.gelu(preact, approximate=True).astype(jnp.bfloat16)
    result = residual + jnp.dot(hidden, down_w, preferred_element_type=jnp.float32) + bias_f[5]
    saved = (
        normed_one,
        inverse_one,
        act_one,
        queries,
        key_rows,
        values,
        attn_probs,
        probs_low,
        context,
        normed_two,
        inverse_two,
        act_two,
        preact,
        hidden,
    )
    return (saved, result.astype(jnp.bfloat16).reshape(group, seq_len, model_width))


def backward(saved, grad_part, params):
    qkv_w, out_w, up_w, down_w, gains, biases, up_b = params
    (
        normed_one,
        inverse_one,
        act_one,
        queries,
        key_rows,
        values,
        attn_probs,
        probs_low,
        context,
        normed_two,
        inverse_two,
        act_two,
        preact,
        hidden,
    ) = saved
    gain_f = gains.astype(jnp.float32)
    group, seq_len, model_width = grad_part.shape
    rows = group * seq_len
    head_size = model_width // HEADS
    score_scale = head_size ** (-0.5)
    grad_low = grad_part.reshape(rows, model_width)
    grad_full = grad_low.astype(jnp.float32)
    grad_down_b = jnp.sum(grad_full, 0)
    grad_down = lax.dot_general(hidden, grad_low, CONTRACT_ROWS, preferred_element_type=jnp.float32)
    grad_hidden = lax.dot_general(
        grad_low, down_w, CONTRACT_COLS, preferred_element_type=jnp.float32
    )
    unused, gelu_back = jax.vjp(lambda value_in: jax.nn.gelu(value_in, approximate=True), preact)
    grad_preact = gelu_back(grad_hidden)[0].astype(jnp.bfloat16)
    grad_up_b = jnp.sum(grad_preact, 0, dtype=jnp.float32)
    grad_up = lax.dot_general(
        act_two, grad_preact, CONTRACT_ROWS, preferred_element_type=jnp.float32
    )
    grad_act_two = lax.dot_general(
        grad_preact, up_w, CONTRACT_COLS, preferred_element_type=jnp.float32
    )
    grad_gain_two = jnp.sum(grad_act_two * normed_two, 0)
    grad_shift_two = jnp.sum(grad_act_two, 0)
    grad_resid = grad_full + normalize_back(grad_act_two, normed_two, inverse_two, gain_f[1])
    grad_attn = grad_resid.astype(jnp.bfloat16)
    grad_out_b = jnp.sum(grad_attn, 0, dtype=jnp.float32)
    grad_out = lax.dot_general(
        context, grad_attn, CONTRACT_ROWS, preferred_element_type=jnp.float32
    )
    grad_context = lax.dot_general(
        grad_attn, out_w, CONTRACT_COLS, preferred_element_type=jnp.float32
    )
    grad_context = grad_context.astype(jnp.bfloat16).reshape(group, seq_len, HEADS, head_size)
    grad_values = jnp.einsum(
        "bhqk,bqhd->bkhd", probs_low, grad_context, preferred_element_type=jnp.float32
    )
    grad_probs = jnp.einsum(
        "bqhd,bkhd->bhqk", grad_context, values, preferred_element_type=jnp.float32
    )
    grad_scores = attn_probs * (grad_probs - jnp.sum(attn_probs * grad_probs, -1, keepdims=True))
    grad_scores = grad_scores.astype(jnp.bfloat16)
    grad_queries = (
        jnp.einsum("bhqk,bkhd->bqhd", grad_scores, key_rows, preferred_element_type=jnp.float32)
        * score_scale
    )
    grad_keys = (
        jnp.einsum("bhqk,bqhd->bkhd", grad_scores, queries, preferred_element_type=jnp.float32)
        * score_scale
    )
    grad_joined = jnp.concatenate(
        [
            grad_queries.reshape(rows, model_width),
            grad_keys.reshape(rows, model_width),
            grad_values.reshape(rows, model_width),
        ],
        1,
    ).astype(jnp.bfloat16)
    grad_query_b = jnp.sum(grad_joined[:, :model_width], 0, dtype=jnp.float32)
    grad_value_b = jnp.sum(grad_joined[:, 2 * model_width :], 0, dtype=jnp.float32)
    grad_qkv = lax.dot_general(
        act_one, grad_joined, CONTRACT_ROWS, preferred_element_type=jnp.float32
    )
    grad_act_one = lax.dot_general(
        grad_joined, qkv_w, CONTRACT_COLS, preferred_element_type=jnp.float32
    )
    grad_gain_one = jnp.sum(grad_act_one * normed_one, 0)
    grad_shift_one = jnp.sum(grad_act_one, 0)
    grad_tokens = grad_resid + normalize_back(grad_act_one, normed_one, inverse_one, gain_f[0])
    grad_tokens = grad_tokens.astype(jnp.bfloat16).reshape(group, seq_len, model_width)
    grad_gains = jnp.stack([grad_gain_one, grad_gain_two])
    grad_biases = jnp.stack(
        [grad_shift_one, grad_query_b, grad_value_b, grad_out_b, grad_shift_two, grad_down_b]
    )
    return (
        grad_tokens,
        (grad_qkv, grad_out, grad_up, grad_down, grad_gains, grad_biases, grad_up_b),
    )


def per_device(
    tokens,
    lengths,
    cotangent,
    qkv_weight,
    out_weight,
    up_weight,
    down_weight,
    gains,
    biases,
    up_bias,
):
    seq_dev, seq_len, model_width = tokens.shape
    group = math.gcd(seq_dev, 4)
    blocks = seq_dev // group
    token_blocks = tokens.reshape(blocks, group, seq_len, model_width)
    length_blocks = lengths.reshape(blocks, group)
    grad_blocks = cotangent.reshape(blocks, group, seq_len, model_width)
    first = (
        lax.all_gather(qkv_weight.astype(jnp.bfloat16), ("dp", "fsdp"), axis=0, tiled=True),
        lax.all_gather(out_weight.astype(jnp.bfloat16), ("dp", "fsdp"), axis=0, tiled=True),
        lax.all_gather(up_weight.astype(jnp.bfloat16), ("dp", "fsdp"), axis=0, tiled=True),
        lax.all_gather(down_weight.astype(jnp.bfloat16), ("dp", "fsdp"), axis=0, tiled=True),
        lax.all_gather(gains.astype(jnp.bfloat16), ("dp", "fsdp"), axis=1, tiled=True),
        lax.all_gather(biases.astype(jnp.bfloat16), ("dp", "fsdp"), axis=1, tiled=True),
        lax.all_gather(up_bias.astype(jnp.bfloat16), ("dp", "fsdp"), axis=0, tiled=True),
    )
    zero_grads = tuple((jnp.zeros(whole.shape, jnp.float32) for whole in first))

    def forward_only(carried, element):
        token_part, length_part = element
        saved, result = forward(token_part, length_part, first)
        return (carried, result)

    carried, results = lax.scan(
        forward_only, jnp.zeros((), jnp.float32), (token_blocks, length_blocks)
    )
    second = (
        lax.all_gather(qkv_weight.astype(jnp.bfloat16), ("dp", "fsdp"), axis=0, tiled=True),
        lax.all_gather(out_weight.astype(jnp.bfloat16), ("dp", "fsdp"), axis=0, tiled=True),
        lax.all_gather(up_weight.astype(jnp.bfloat16), ("dp", "fsdp"), axis=0, tiled=True),
        lax.all_gather(down_weight.astype(jnp.bfloat16), ("dp", "fsdp"), axis=0, tiled=True),
        lax.all_gather(gains.astype(jnp.bfloat16), ("dp", "fsdp"), axis=1, tiled=True),
        lax.all_gather(biases.astype(jnp.bfloat16), ("dp", "fsdp"), axis=1, tiled=True),
        lax.all_gather(up_bias.astype(jnp.bfloat16), ("dp", "fsdp"), axis=0, tiled=True),
    )

    def backward_only(totals, element):
        token_part, length_part, grad_part = element
        saved, unused = forward(token_part, length_part, second)
        token_grad, weight_grads = backward(saved, grad_part, second)
        return (add_all(totals, weight_grads), token_grad)

    totals, token_grads = lax.scan(
        backward_only, zero_grads, (token_blocks, length_blocks, grad_blocks)
    )
    shards = (
        lax.psum_scatter(totals[0], ("dp", "fsdp"), scatter_dimension=0, tiled=True),
        lax.psum_scatter(totals[1], ("dp", "fsdp"), scatter_dimension=0, tiled=True),
        lax.psum_scatter(totals[2], ("dp", "fsdp"), scatter_dimension=0, tiled=True),
        lax.psum_scatter(totals[3], ("dp", "fsdp"), scatter_dimension=0, tiled=True),
        lax.psum_scatter(totals[4], ("dp", "fsdp"), scatter_dimension=1, tiled=True),
        lax.psum_scatter(totals[5], ("dp", "fsdp"), scatter_dimension=1, tiled=True),
        lax.psum_scatter(totals[6], ("dp", "fsdp"), scatter_dimension=0, tiled=True),
    )
    return (
        results.reshape(seq_dev, seq_len, model_width),
        token_grads.reshape(seq_dev, seq_len, model_width),
        shards[0],
        shards[1],
        shards[2],
        shards[3],
        shards[4],
        shards[5],
        shards[6],
    )


def solution(mesh):
    placed = (
        P(("dp", "fsdp"), None, None),
        P(("dp", "fsdp")),
        P(("dp", "fsdp"), None, None),
        P(("dp", "fsdp"), None),
        P(("dp", "fsdp"), None),
        P(("dp", "fsdp"), None),
        P(("dp", "fsdp"), None),
        P(None, ("dp", "fsdp")),
        P(None, ("dp", "fsdp")),
        P(("dp", "fsdp")),
    )
    return jax.shard_map(
        per_device,
        mesh=mesh,
        in_specs=placed,
        out_specs=(
            P(("dp", "fsdp"), None, None),
            P(("dp", "fsdp"), None, None),
            P(("dp", "fsdp"), None),
            P(("dp", "fsdp"), None),
            P(("dp", "fsdp"), None),
            P(("dp", "fsdp"), None),
            P(None, ("dp", "fsdp")),
            P(None, ("dp", "fsdp")),
            P(("dp", "fsdp")),
        ),
        check_vma=False,
    )
```

profile of v0, /device:TPU:0, one launch (start us, length us, event | category | flops | bytes accessed | tf_op | source)
XLA Modules:
  0.0 1329.6 jit_solution(17472043329100366465)
XLA Ops:
  14.2 43.0 %all-gather = bf16[32,16,2]{1,2,0:T(2,128)(2,1)S(1)} all-gather(bf16[1,16,2]{1,2,0:T(2,128)(2,1)S(1)} %convert_bitcast_fusion.1), channel_id=1, replica_groups=mesh['dp'=4,'fsdp'=8] {'dp','fsdp'}, dimensions={0}, use_global_device_ids=true | all-gather | bytes 2112 | tf_op jit(solution)/shard_map/all_gather | solution.py:220
  58.8 36.8 %all-gather.1 = bf16[32,16,6]{1,2,0:T(8,128)(2,1)S(1)} all-gather(bf16[1,16,6]{1,2,0:T(8,128)(2,1)S(1)} %convert_bitcast_fusion), channel_id=1, replica_groups=mesh['dp'=4,'fsdp'=8] {'dp','fsdp'}, dimensions={0}, use_global_device_ids=true | all-gather | bytes 6336 | tf_op jit(solution)/shard_map/all_gather | solution.py:221
  96.0 39.7 %all-reduce = bf16[2048]{0:T(1024)(128)(2,1)S(1)} all-reduce(bf16[2048]{0:T(1024)(128)(2,1)S(1)} %dynamic-update-slice), channel_id=1, replica_groups=mesh['dp'=4,'fsdp'=8] {'dp','fsdp'}, use_global_device_ids=true, to_apply=%add | all-reduce | flops 2048 | bytes 8192
  135.7 45.0 %all_gather.31 = bf16[512,512]{1,0:T(8,128)(2,1)} all-gather(bf16[16,512]{1,0:T(8,128)(2,1)S(1)} %convert_element_type.249), channel_id=1, replica_groups=mesh['dp'=4,'fsdp'=8] {'dp','fsdp'}, dimensions={0}, use_global_device_ids=true | all-gather | bytes 540672 | tf_op jit(solution)/shard_map/all_gather | solution.py:217
  180.8 7.4 all-gather.10.cloned.1.call-done
  190.1 341.8 %while.38 = (s32[]{:T(128)}, f32[512,1536]{1,0:T(8,128)}, f32[512,512]{1,0:T(8,128)}, f32[512,2048]{1,0:T(8,128)}, f32[2048,512]{1,0:T(8,128)}, /*index=5*/f32[2...) while((s32[]{:T(128)}, f32[512,1536]{1,0:T(8,128)}, ...), condition=%wide.region_29.30_spmd.clone, body=%wide.region_8.29_spmd.clone.sunk | while | flops 18944106496 | bytes 413778720 | solution.py:250
  219.0 7.9 fusion.289
  241.9 8.3 convert_reduce_fusion.15
  328.1 7.9 fusion.289
  345.7 7.1 select_add_fusion.9
  352.8 8.1 convert_reduce_fusion.15
  438.8 7.9 fusion.289
  456.3 7.1 select_add_fusion.9
  463.4 8.2 convert_reduce_fusion.15
  538.5 117.7 %while.37 = (s32[]{:T(128)}, bf16[3,4,256,512]{3,2,1,0:T(8,128)(2,1)}, bf16[3,4,256,512]{3,2,1,0:T(8,128)(2,1)}, bf16[2,512]{1,0:T(2,128)(2,1)S(1)}, bf16[6,512]...) while((s32[]{:T(128)}, ...), condition=%wide.region_7.8_spmd, body=%wide.region_0.7_spmd.sunk | while | flops 7033852928 | bytes 98797848 | solution.py:231
  569.3 7.3 add_convert_fusion.12
  608.6 7.3 add_convert_fusion.12
  647.8 7.3 add_convert_fusion.12
  656.2 38.9 %all-reduce.1 = f32[2048]{0:T(1024)S(1)} all-reduce(f32[2048]{0:T(1024)S(1)} %copy-done.18), channel_id=8, replica_groups=mesh['dp'=4,'fsdp'=8] {'dp','fsdp'}, use_global_device_ids=true, to_apply=%region_36.37.clone | all-reduce | flops 2048 | bytes 16384
  697.0 100.3 %reduce-scatter.21.cloned.1.call-done = f32[16,6]{1,0:T(8,128)} async-done(((f32[512,6]{1,0:T(8,128)}), f32[16,6]{1,0:T(8,128)}) %reduce-scatter.21.cloned.1.call-update) | async-done | bytes 400
  798.6 132.4 %reduce-scatter.13.cloned.1.call-done = f32[16,512]{1,0:T(8,128)} async-done(((f32[512,512]{1,0:T(8,128)}), f32[16,512]{1,0:T(8,128)}) %reduce-scatter.13.cloned.1.call-update) | async-done | bytes 32784 | tf_op jit(solution)/shard_map/reduce_scatter | solution.py:255
  931.1 104.7 %reduce-scatter.11.cloned.1.call-done = f32[16,1536]{1,0:T(8,128)} async-done(((f32[512,1536]{1,0:T(8,128)}), f32[16,1536]{1,0:T(8,128)}) %reduce-scatter.11.cloned.1.call-update) | async-done | bytes 98320 | tf_op jit(solution)/shard_map/reduce_scatter | solution.py:254
  1035.8 144.6 %reduce-scatter.15.cloned.1.call-done = f32[16,2048]{1,0:T(8,128)} async-done(((f32[512,2048]{1,0:T(8,128)}), f32[16,2048]{1,0:T(8,128)}) %reduce-scatter.15.cloned.1.call-update) | async-done | bytes 131088 | tf_op jit(solution)/shard_map/reduce_scatter | solution.py:256
  1180.5 142.4 %reduce-scatter.17.cloned.1.call-done = f32[64,512]{1,0:T(8,128)} async-done(((f32[2048,512]{1,0:T(8,128)}), f32[64,512]{1,0:T(8,128)}) %reduce-scatter.17.cloned.1.call-update) | async-done | bytes 131088 | tf_op jit(solution)/shard_map/reduce_scatter | solution.py:257
  (459 shorter events, 381.5 us)
Async XLA Ops:
  7.2 173.6 %all-gather.6.cloned.1.call-start = ((), (), s32[]{:S(2)}) async-start(), calls=%async_computation.6 | async-start | bytes 1622016 | tf_op jit(solution)/shard_map/all_gather | solution.py:216
  8.8 172.0 %all-gather.8.cloned.1.call-start = ((), (), s32[]{:S(2)}) async-start(), calls=%async_computation.7 | async-start | bytes 2162688 | tf_op jit(solution)/shard_map/all_gather | solution.py:218
  10.4 177.8 %all-gather.10.cloned.1.call-start = ((), (), s32[]{:S(2)}) async-start(), calls=%async_computation.8 | async-start | bytes 2162688 | tf_op jit(solution)/shard_map/all_gather | solution.py:219
  12.0 683.7 %reduce-scatter.19.cloned.1.call-start = ((), (), s32[]{:S(2)}) async-start(), calls=%async_computation.13 | async-start | bytes 270336
  218.9 7.9 copy-start.7
  236.5 5.4 copy-start.20
  271.6 5.8 slice-start.1
  288.9 6.5 copy-start.16
  328.1 7.9 copy-start.7
  345.7 7.1 copy-start.20
  382.2 5.0 slice-start
  382.3 5.8 slice-start.1
  399.5 6.5 copy-start.16
  438.7 7.9 copy-start.7
  456.3 7.1 copy-start.20
  492.9 5.0 slice-start
  492.9 5.8 slice-start.1
  510.4 6.5 copy-start.16
  532.8 264.5 %reduce-scatter.21.cloned.1.call-start = ((), (), s32[]{:S(2)}) async-start(), calls=%async_computation.14 | async-start | bytes 270336
  533.7 397.4 %reduce-scatter.13.cloned.1.call-start = ((), (), s32[]{:S(2)}) async-start(), calls=%async_computation.10 | async-start | bytes 1081344 | tf_op jit(solution)/shard_map/reduce_scatter | solution.py:255
  534.3 501.5 %reduce-scatter.11.cloned.1.call-start = ((), (), s32[]{:S(2)}) async-start(), calls=%async_computation.9 | async-start | bytes 3244032 | tf_op jit(solution)/shard_map/reduce_scatter | solution.py:254
  535.0 645.4 %reduce-scatter.15.cloned.1.call-start = ((), (), s32[]{:S(2)}) async-start(), calls=%async_computation.11 | async-start | bytes 4325376 | tf_op jit(solution)/shard_map/reduce_scatter | solution.py:256
  535.8 787.0 %reduce-scatter.17.cloned.1.call-start = ((), (), s32[]{:S(2)}) async-start(), calls=%async_computation.12 | async-start | bytes 4325376 | tf_op jit(solution)/shard_map/reduce_scatter | solution.py:257
  538.5 117.7 %copy-start.18 = (f32[2048]{0:T(1024)S(1)}, f32[2048]{0:T(1024)}, u32[]{:S(2)}) copy-start(f32[2048]{0:T(1024)} %copy-done.17) | copy-start | bytes 24580
  (50 other events, 97.0 us)
Sparse Core Ops, SparseCore 0:
  11.6 57.8 all-gather.5
  73.0 55.8 all-gather.7
  132.4 55.6 all-gather.9
  532.9 132.3 reduce-scatter.18
  667.4 129.7 reduce-scatter.20
  799.9 131.0 reduce-scatter.12
  938.0 97.8 reduce-scatter.10
  1038.8 141.6 reduce-scatter.14
  1183.4 139.3 reduce-scatter.16
where the time goes:
time: 1340 us; the launch traced here: 1330 us
  waiting for transfers between devices  635 us (47%)
  matrix products  234 us (17%)
  blocking collectives  204 us (15%)
  local copies, waits for them, and re-layouts  150 us (11%)
  other arithmetic  79 us (6%)
  between operations  14.2 us (1%)
  loops' own time  14 us (1%)
    reduce_scatter x1, waiting for transfers between devices, per_device(): lax.psum_scatter(totals[2], ('dp', 'fsdp'), scatter_dimension=0, tiled=True)  145 us
    reduce_scatter x1, waiting for transfers between devices, per_device(): lax.psum_scatter(totals[3], ('dp', 'fsdp'), scatter_dimension=0, tiled=True)  142 us
    reduce_scatter x1, waiting for transfers between devices, per_device(): lax.psum_scatter(totals[1], ('dp', 'fsdp'), scatter_dimension=0, tiled=True)  132 us
    reduce_scatter x1, waiting for transfers between devices, per_device(): lax.psum_scatter(totals[0], ('dp', 'fsdp'), scatter_dimension=0, tiled=True)  105 us
    unnamed x11, waiting for transfers between devices  103 us
    unnamed x2, blocking collectives  78.6 us
    all_gather x1, blocking collectives, per_device(): lax.all_gather(out_weight.astype(jnp.bfloat16), ('dp', 'fsdp'), axis=0, t...  45 us
    all_gather x1, blocking collectives, per_device(): lax.all_gather(gains.astype(jnp.bfloat16), ('dp', 'fsdp'), axis=1, tiled=...  43 us
  transfers between devices with their start and end apart: 9, of which 6 were waited for; matrix products, arithmetic and copies ran while one was open for 10% of the time, Pallas kernels for 0%

commit v1 on v0

v1 whole, which is shorter than its diff:
```python
import functools

import jax
import jax.numpy as jnp
from jax import lax
from jax.experimental import pallas as pl
from jax.experimental.pallas import tpu as pltpu
from jax.sharding import PartitionSpec as P

F32, BF = jnp.float32, jnp.bfloat16
MESH = pl.DeviceIdType.MESH
HEADS = 8
EPS = 1e-5
C0 = 0.7978845608028654
C1 = C0 * 0.044715
LANES = 128
NN = (((1,), (0,)), ((), ()))
NT = (((1,), (1,)), ((), ()))
TN = (((0,), (0,)), ((), ()))
VMEM_LIMIT = 60 * 2**20


def dot(a, b, dims=NN):
    return lax.dot_general(a, b, dims, preferred_element_type=F32)


def lane_sums(v):
    total = v[:, :LANES]
    for at in range(LANES, v.shape[1], LANES):
        total = total + v[:, at : at + LANES]
    return total


def normalize(v):
    center = v - jnp.mean(v, 0, keepdims=True)
    inverse = lax.rsqrt(jnp.mean(center * center, 0, keepdims=True) + EPS)
    return center * inverse, inverse


def normalize_back(grad, normed, inverse, gain):
    scaled = grad * gain
    return inverse * (
        scaled
        - jnp.mean(scaled, 0, keepdims=True)
        - normed * jnp.mean(scaled * normed, 0, keepdims=True)
    )


class Place:
    def __init__(self, n_dp, n_z):
        self.n_dp, self.n_z = n_dp, n_z
        self.dp = lax.axis_index("dp")
        fsdp = lax.axis_index("fsdp")
        self.fsdp, self.z, self.core = fsdp, fsdp // 2, fsdp % 2
        self.slot = self.dp * n_z + self.z
        self.mate = (self.dp, self.z * 2 + 1 - self.core)

    def z_of(self, k):
        return lax.rem(self.z + k, self.n_z)

    def dp_of(self, k):
        return lax.rem(self.dp + k, self.n_dp)

    def z_peer(self, k):
        return (self.dp, self.z_of(k) * 2 + self.core)

    def dp_peer(self, k):
        return (self.dp_of(k), self.fsdp)

    def greet(self):
        barrier = pltpu.get_barrier_semaphore()
        peers = [self.mate]
        peers += [self.z_peer(k) for k in range(1, self.n_z)]
        peers += [self.dp_peer(k) for k in range(1, self.n_dp)]
        for peer in peers:
            pl.semaphore_signal(barrier, inc=1, device_id=peer, device_id_type=MESH)
        pl.semaphore_wait(barrier, len(peers))


class Gather:
    def __init__(self, place, own, whole, send, recv):
        self.p, self.own, self.whole, self.send, self.recv = place, own, whole, send, recv

    def put(self, src, slot, core, peer, at):
        pltpu.make_async_remote_copy(
            src_ref=src,
            dst_ref=self.whole.at[slot, core],
            send_sem=self.send.at[at],
            recv_sem=self.recv.at[slot, core],
            device_id=peer,
            device_id_type=MESH,
        ).start()

    def landed(self, slot, core):
        there = self.whole.at[slot, core]
        pltpu.make_async_copy(there, there, self.recv.at[slot, core]).wait()

    def start(self):
        p, at = self.p, 0
        peers = [p.z_peer(k) for k in range(1, p.n_z)]
        peers += [p.dp_peer(k) for k in range(1, p.n_dp)]
        for peer in peers + [p.mate]:
            self.put(self.own, p.slot, p.core, peer, at)
            at += 1

    def along_z(self):
        p = self.p
        at = p.n_z + p.n_dp - 1
        for k in range(1, p.n_z):
            slot = p.dp * p.n_z + p.z_of(k)
            self.landed(slot, p.core)
            for peer in [p.dp_peer(m) for m in range(1, p.n_dp)] + [p.mate]:
                self.put(self.whole.at[slot, p.core], slot, p.core, peer, at)
                at += 1

    def over_dp(self):
        p = self.p
        at = p.n_z + p.n_dp - 1 + (p.n_z - 1) * p.n_dp
        for k in range(0, p.n_z):
            for m in range(1, p.n_dp):
                slot = p.dp_of(m) * p.n_z + p.z_of(k)
                self.landed(slot, p.core)
                self.put(self.whole.at[slot, p.core], slot, p.core, p.mate, at)
                at += 1

    def finish(self):
        p = self.p
        for k in range(0, p.n_z):
            for m in range(0, p.n_dp):
                self.landed(p.dp_of(m) * p.n_z + p.z_of(k), 1 - p.core)
        for at in range(self.sends(p.n_dp, p.n_z)):
            pltpu.make_async_copy(self.own, self.own, self.send.at[at]).wait()

    @staticmethod
    def sends(n_dp, n_z):
        return 2 * n_dp * n_z - 1


def attention_kernel(
    mesh_sizes, gathers, lengths, x_ref, *refs
):
    n_dp, n_z = mesh_sizes
    if gathers:
        (qkv_s, wo_s, wu_s, wd_s, gains_s, biases_s, upb_s,
         qkv_ref, probs_ref, ct_ref, r1_ref, a1_ref, xt_ref, early_ref, wu_ref, wd_ref,
         wqkv_t, wo_t, early, early_own, wu_own, wd_own, small, sems, rems, local) = refs
    else:
        (early_in,
         qkv_ref, probs_ref, ct_ref, r1_ref, a1_ref, xt_ref,
         wqkv_t, wo_t, early) = refs
    step = pl.program_id(0)
    d = x_ref.shape[2]

    if gathers:
        place = Place(n_dp, n_z)
        first = Gather(place, early_own, early, sems.at[0], rems.at[0])
        up = Gather(place, wu_own, wu_ref, sems.at[1], rems.at[1])
        down = Gather(place, wd_own, wd_ref, sems.at[2], rems.at[2])
        own_up = pltpu.make_async_copy(wu_own, wu_ref.at[place.slot, place.core], local.at[0])
        own_down = pltpu.make_async_copy(wd_own, wd_ref.at[place.slot, place.core], local.at[1])
        out_early = pltpu.make_async_copy(early, early_ref, local.at[2])

        @pl.when(step == 0)
        def _():
            place.greet()
            rows = qkv_s.shape[0]
            small[...] = jnp.zeros_like(small)
            small[0:2, :rows] = gains_s[...]
            small[2:8, :rows] = biases_s[...]
            small[8:12, :rows] = upb_s[...]
            early_own[:, : 3 * d] = qkv_s[...].astype(BF)
            early_own[:, 3 * d : 4 * d] = wo_s[...].astype(BF)
            early_own[:, 4 * d :] = small[...].T[:rows].astype(BF)
            wu_own[...] = wu_s[...].astype(BF)
            wd_own[...] = wd_s[...].astype(BF)
            first.start()
            early[place.slot, place.core] = early_own[...]
            first.along_z()
            first.over_dp()
            first.finish()
            own_up.start()
            own_down.start()
            out_early.start()

        for each, at in ((up, 1), (down, 2)):
            pl.when(step == at)(each.start)
            pl.when(step == at + 2)(each.along_z)
            pl.when(step == at + 4)(each.over_dp)
            pl.when(step == at + 6)(each.finish)

        @pl.when(step == 10)
        def _():
            own_up.wait()
            own_down.wait()
            out_early.wait()
    else:

        @pl.when(step == 0)
        def _():
            early[...] = early_in[...].reshape(early.shape)

    @pl.when(step == 0)
    def _():
        whole = early[...].reshape(d, 4 * d + LANES)
        wqkv_t[...] = whole[:, : 3 * d].T
        wo_t[...] = whole[:, 3 * d : 4 * d].T

    column = early[..., 4 * d :].reshape(d, LANES).astype(F32)
    xt = x_ref[0].T
    xt_ref[...] = xt
    x = xt.astype(F32)
    seq = x.shape[1]
    head = d // HEADS
    normed, _ = normalize(x)
    a1 = (normed * column[:, 0:1] + column[:, 2:3]).astype(BF)
    a1_ref[...] = a1
    scale = head**-0.5
    query = (dot(wqkv_t[0:d], a1) + column[:, 3:4]).astype(BF)
    qkv_ref[0:d] = (query.astype(F32) * scale).astype(BF)
    qkv_ref[d : 2 * d] = dot(wqkv_t[d : 2 * d], a1).astype(BF)
    qkv_ref[2 * d :] = (dot(wqkv_t[2 * d :], a1) + column[:, 4:5]).astype(BF)
    valid = lax.broadcasted_iota(jnp.int32, (seq, seq), 0) < lengths[step]
    for h in range(HEADS):
        at = h * head
        scores = dot(qkv_ref[d + at : d + at + head], qkv_ref[at : at + head], TN)
        scores = jnp.where(valid, scores, -1e30)
        exponent = jnp.exp(scores - jnp.max(scores, 0, keepdims=True))
        probs = (exponent * (1.0 / jnp.sum(exponent, 0, keepdims=True))).astype(BF)
        probs_ref[0, h] = probs
        ct_ref[at : at + head] = dot(qkv_ref[2 * d + at : 2 * d + at + head], probs).astype(BF)
    r1_ref[...] = x + dot(wo_t[...], ct_ref[...]) + column[:, 5:6]


def forward_kernel(
    r1_ref, g_ref, column_ref, wu_ref, wd_ref, out_ref, dr1_ref, dwu_ref, dwd_ref, small_ref,
    wu_t, wd_t, gt, a2, total_out, total_a2, total_wu, total_wd, sums, sums_up, up_bias, *, block,
):
    step = pl.program_id(0)
    d, tokens = r1_ref.shape
    hidden = wd_ref.shape[0]
    n_dev = dwd_ref.shape[0] * 2
    rows = d // n_dev
    seqs, seq = g_ref.shape[:2]
    column = column_ref[...].astype(F32)

    @pl.when(step == 0)
    def _():
        wu_t[...] = wu_ref[...].T
        wd_t[...] = wd_ref[...].T
        total_wu[...] = jnp.zeros_like(total_wu)
        total_wd[...] = jnp.zeros_like(total_wd)
        sums[...] = jnp.zeros_like(sums)
        sums_up[...] = jnp.zeros_like(sums_up)
        for r in range(hidden // d):
            up_bias[:, r * rows : (r + 1) * rows, :] = jnp.broadcast_to(
                column[:, 8 + r : 9 + r].reshape(n_dev, rows, 1), (n_dev, rows, LANES)
            )

    for s in range(seqs):
        gt[:, seq * s : seq * (s + 1)] = g_ref[s].T
    r1 = r1_ref[...]
    normed, inverse = normalize(r1)
    a2[...] = (normed * column[:, 1:2] + column[:, 6:7]).astype(BF)
    total_out[...] = r1 + column[:, 7:8]
    total_a2[...] = jnp.zeros_like(total_a2)
    per = block // (hidden // n_dev)

    def body(j, _):
        at = pl.ds(pl.multiple_of(j * block, block), block)
        bias = up_bias[pl.ds(j * per, per)].reshape(block, LANES)[:, 0:1]
        u = dot(wu_t[at, :], a2[...]) + bias
        dh = dot(wd_ref[at, :], gt[...])
        square = u * u
        half = 0.5 + 0.5 * jnp.tanh(u * (C0 + C1 * square))
        h = u * half
        h_low = h.astype(BF)
        slope = half + h * (1.0 - half) * (2 * C0 + 6 * C1 * square)
        du = (dh * slope).astype(BF)
        total_out[...] += dot(wd_t[:, at], h_low)
        total_a2[...] += dot(wu_ref[:, at], du)
        total_wd[at, :] += dot(h_low, gt[...], NT)
        total_wu[:, at] += dot(a2[...], du, NT)
        sums_up[at, :] += lane_sums(du.astype(F32))
        return 0

    lax.fori_loop(0, hidden // block, body, 0)
    for s in range(seqs):
        out_ref[s] = total_out[:, seq * s : seq * (s + 1)].astype(BF).T
    da2 = total_a2[...]
    g = gt[...].astype(F32)
    dr1_ref[...] = g + normalize_back(da2, normed, inverse, column[:, 1:2])
    sums[0] += lane_sums(da2 * normed)
    sums[1] += lane_sums(da2)
    sums[2] += lane_sums(g)

    @pl.when(step == pl.num_programs(0) - 1)
    def _():
        dwu_ref[...] = total_wu[...].astype(BF).reshape(dwu_ref.shape)
        dwd_ref[...] = total_wd[...].astype(BF).reshape(dwd_ref.shape)
        lane = lax.broadcasted_iota(jnp.int32, (d, LANES), 1)
        small = jnp.zeros((d, LANES), F32)
        for s, at in ((0, 1), (1, 6), (2, 7)):
            small = jnp.where(lane == at, jnp.sum(sums[s], 1, keepdims=True), small)
        up = jnp.sum(sums_up[...], 1, keepdims=True).reshape(n_dev, hidden // n_dev, 1)
        for r in range(hidden // d):
            part = up[:, r * rows : (r + 1) * rows].reshape(d, 1)
            small = jnp.where(lane == 8 + r, part, small)
        small_ref[...] = small


class Scatter:
    def __init__(self, place, part, result, bufs, send, recv):
        self.p, self.part, self.result = place, part, result
        self.mine, self.got1, self.sum1, self.got2, self.sum2, self.got3 = bufs
        self.send, self.recv = send, recv

    @staticmethod
    def scratch(n_dp, n_z, rows, width, kind):
        return [
            pltpu.VMEM((n_dp * n_z, rows, width), kind),
            pltpu.VMEM((n_dp * n_z, rows, width), kind),
            pltpu.VMEM((n_dp * n_z, rows, width), kind),
            pltpu.VMEM((n_dp - 1, n_z, rows, width), kind),
            pltpu.VMEM((n_z, rows, width), kind),
            pltpu.VMEM((n_z - 1, rows, width), kind),
        ]

    @staticmethod
    def sems(n_dp, n_z):
        return n_dp + n_z

    def copy(self, src, dst, at, peer):
        return pltpu.make_async_remote_copy(
            src_ref=src,
            dst_ref=dst,
            send_sem=self.send.at[at],
            recv_sem=self.recv.at[at],
            device_id=peer,
            device_id_type=MESH,
        )

    def to_mate(self):
        p = self.p
        return self.copy(self.part.at[:, 1 - p.core], self.got1, 0, p.mate)

    def own(self):
        p = self.p
        return pltpu.make_async_copy(
            self.part.at[:, p.core], self.mine, self.send.at[p.n_dp + p.n_z - 1]
        )

    def over_dp(self):
        p = self.p
        return [
            self.copy(
                self.sum1.at[pl.ds(p.dp_of(k) * p.n_z, p.n_z)], self.got2.at[k - 1], k, p.dp_peer(k)
            )
            for k in range(1, p.n_dp)
        ]

    def along_z(self):
        p = self.p
        return [
            self.copy(
                self.sum2.at[p.z_of(k)], self.got3.at[k - 1], p.n_dp - 1 + k, p.z_peer(k)
            )
            for k in range(1, p.n_z)
        ]

    def step1(self):
        self.to_mate().start()
        self.own().start()

    def step2(self):
        self.own().wait()
        self.to_mate().wait()

        def add(s, _):
            self.sum1[s] = (self.mine[s].astype(F32) + self.got1[s].astype(F32)).astype(
                self.sum1.dtype
            )
            return 0

        lax.fori_loop(0, self.p.n_dp * self.p.n_z, add, 0)
        for copy in self.over_dp():
            copy.start()

    def step3(self):
        for copy in self.over_dp():
            copy.wait()

        def add(s, _):
            total = self.sum1[self.p.dp * self.p.n_z + s].astype(F32)
            for k in range(self.p.n_dp - 1):
                total = total + self.got2[k, s].astype(F32)
            self.sum2[s] = total.astype(self.sum2.dtype)
            return 0

        lax.fori_loop(0, self.p.n_z, add, 0)
        for copy in self.along_z():
            copy.start()

    def step4(self):
        for copy in self.along_z():
            copy.wait()
        total = self.sum2[self.p.z].astype(F32)
        for k in range(self.p.n_z - 1):
            total = total + self.got3[k].astype(F32)
        self.result[...] = total


def backward_kernel(mesh_sizes, scatters, *refs):
    n_dp, n_z = mesh_sizes
    (dr1_ref, xt_ref, a1_ref, ct_ref, qkv_ref, probs_ref, early_ref, part_ref) = refs[:8]
    refs = refs[8:]
    if scatters:
        (dwu_ref, dwd_ref, tg_ref,
         gqkv_ref, gout_ref, gup_ref, gdown_ref, ggains_ref, gbiases_ref, gupb_ref,
         total_qkv, total_out, dp_s, dc_s, sums, part_qkv, part_out, part_small, turn, small_own) = refs[:20]
        buffers, (send, recv) = refs[20:-2], refs[-2:]
    else:
        tg_ref, gqkv_ref, gout_ref, gsmall_ref, total_qkv, total_out, dp_s, dc_s, sums = refs
    step = pl.program_id(0)
    last = pl.num_programs(0) - 1
    d, seq = dr1_ref.shape
    head = d // HEADS
    column = early_ref[:, 4 * d :].astype(F32)

    if scatters:
        place = Place(n_dp, n_z)
        pieces = [
            Scatter(place, part, result, buffers[6 * i : 6 * i + 6], send.at[i], recv.at[i])
            for i, (part, result) in enumerate(
                (
                    (dwd_ref, gdown_ref),
                    (dwu_ref, gup_ref),
                    (part_qkv, gqkv_ref),
                    (part_out, gout_ref),
                    (part_small, small_own),
                )
            )
        ]
        pl.when(step == 0)(place.greet)
        for piece, at in ((pieces[0], 0), (pieces[1], 1)):
            pl.when(step == at)(piece.step1)
            pl.when(step == at + 2)(piece.step2)
            pl.when(step == at + 5)(piece.step3)
            pl.when(step == at + 8)(piece.step4)

    @pl.when(step == 0)
    def _():
        total_qkv[...] = jnp.zeros_like(total_qkv)
        total_out[...] = jnp.zeros_like(total_out)
        sums[...] = jnp.zeros_like(sums)

    dr1 = dr1_ref[...]
    do = dr1.astype(BF)
    total_out[...] += dot(ct_ref[...], do, NT)
    dc_s[...] = dot(early_ref[:, 3 * d : 4 * d], do).astype(BF)
    scale = head**-0.5
    for h in range(HEADS):
        q = slice(h * head, (h + 1) * head)
        k = slice(d + h * head, d + (h + 1) * head)
        v = slice(2 * d + h * head, 2 * d + (h + 1) * head)
        dc = dc_s[q]
        probs = probs_ref[0, h]
        delta = jnp.sum(dc.astype(F32) * ct_ref[q].astype(F32), 0, keepdims=True)
        ds = (probs.astype(F32) * (dot(qkv_ref[v], dc, TN) - delta)).astype(BF)
        dp_s[v] = dot(dc, probs, NT).astype(BF)
        dp_s[k] = dot(qkv_ref[q], ds, NT).astype(BF)
        dp_s[q] = (dot(qkv_ref[k], ds) * scale).astype(BF)
    total_qkv[...] += dot(a1_ref[...], dp_s[...], NT)
    da1 = dot(early_ref[:, : 3 * d], dp_s[...])
    normed, inverse = normalize(xt_ref[...].astype(F32))
    tg_ref[0] = (dr1 + normalize_back(da1, normed, inverse, column[:, 0:1])).astype(BF).T
    sums[0] += lane_sums(da1 * normed)
    sums[1] += lane_sums(da1)
    sums[2] += lane_sums(dp_s[0:d].astype(F32))
    sums[3] += lane_sums(dp_s[2 * d :].astype(F32))
    sums[4] += lane_sums(do.astype(F32))

    @pl.when(step == last)
    def _():
        lane = lax.broadcasted_iota(jnp.int32, (d, LANES), 1)
        small = part_ref[...]
        for s, at in enumerate((0, 2, 3, 4, 5)):
            small = jnp.where(lane == at, jnp.sum(sums[s], 1, keepdims=True), small)
        if not scatters:
            gqkv_ref[...] = total_qkv[...]
            gout_ref[...] = total_out[...]
            gsmall_ref[...] = small
            return
        part_qkv[...] = total_qkv[...].astype(BF).reshape(part_qkv.shape)
        part_out[...] = total_out[...].astype(BF).reshape(part_out.shape)
        part_small[...] = small.reshape(part_small.shape)
        for piece in pieces[2:]:
            piece.step1()
        for piece in pieces[2:]:
            piece.step2()
        for piece in pieces[2:]:
            piece.step3()
        for piece in pieces[2:]:
            piece.step4()
        rows = small_own.shape[0]
        turn[...] = jnp.zeros_like(turn)
        turn[:rows] = small_own[...]
        turned = turn[...].T
        ggains_ref[...] = turned[0:2, :rows]
        gbiases_ref[...] = turned[2:8, :rows]
        gupb_ref[...] = turned[8:12, :rows]


def per_device(n_dp, n_fsdp, tokens, lengths, cotangent, qkv_w, out_w, up_w, down_w, gains, biases, up_bias):
    seqs, seq, d = tokens.shape
    n_z, n_dev = n_fsdp // 2, n_dp * n_fsdp
    rows, rows_down = qkv_w.shape[0], down_w.shape[0]
    hidden = up_w.shape[1]
    slots = n_dp * n_z
    count = seqs * seq
    wide = 4 * d + LANES
    direct = rows % 16 == 0
    axes = ("dp", "fsdp")
    cut = n_dev if direct else 32
    quarter = hidden // d
    up_rows = up_bias.reshape(quarter, rows)

    def whole(shape):
        return pl.BlockSpec(shape, lambda i: (0,) * len(shape), pipeline_mode=pl.Buffered(1))

    def lanes(height, width=seq):
        return pl.BlockSpec((height, width), lambda i: (0, i))

    anywhere = pl.BlockSpec(memory_space=pl.ANY)
    smem = pl.BlockSpec(memory_space=pltpu.SMEM)
    seq_block = pl.BlockSpec((1, seq, d), lambda i: (i, 0, 0))
    probs_block = pl.BlockSpec((1, HEADS, seq, seq), lambda i: (i, 0, 0, 0))

    def shape(dims, kind):
        return jax.ShapeDtypeStruct(dims, kind)

    acts_specs = [lanes(3 * d), probs_block, lanes(d), lanes(d), lanes(d), lanes(d)]
    acts_shapes = [
        shape((3 * d, count), BF),
        shape((seqs, HEADS, seq, seq), BF),
        shape((d, count), BF),
        shape((d, count), F32),
        shape((d, count), BF),
        shape((d, count), BF),
    ]
    turned = [pltpu.VMEM((3 * d, d), BF), pltpu.VMEM((d, d), BF), pltpu.VMEM((slots, 2, rows, wide), BF)]
    if direct:
        n_sends = Gather.sends(n_dp, n_z)
        shards = (qkv_w, out_w, up_w, down_w, gains, biases, up_rows)
        acts = pl.pallas_call(
            functools.partial(attention_kernel, (n_dp, n_z), True),
            grid=(seqs,),
            in_specs=[smem, seq_block] + [whole(s.shape) for s in shards],
            out_specs=acts_specs + [anywhere] * 3,
            out_shape=acts_shapes
            + [
                shape((slots, 2, rows, wide), BF),
                shape((slots, 2, rows, hidden), BF),
                shape((slots, 2, rows_down, d), BF),
            ],
            scratch_shapes=turned
            + [
                pltpu.VMEM((rows, wide), BF),
                pltpu.VMEM((rows, hidden), BF),
                pltpu.VMEM((rows_down, d), BF),
                pltpu.VMEM((LANES, LANES), F32),
                pltpu.SemaphoreType.DMA((3, n_sends)),
                pltpu.SemaphoreType.DMA((3, slots, 2)),
                pltpu.SemaphoreType.DMA((3,)),
            ],
            compiler_params=pltpu.CompilerParams(
                vmem_limit_bytes=VMEM_LIMIT, collective_id=0, has_side_effects=True
            ),
            name="attention_forward",
        )(lengths, tokens, *shards)
        qkv, probs, ct, r1, a1, xt, early, wu, wd = acts
        early = early.reshape(d, wide)
        wu, wd = wu.reshape(d, hidden), wd.reshape(hidden, d)
    else:
        early = jnp.concatenate([qkv_w, out_w, gains.T, biases.T], 1).astype(BF)
        early = lax.all_gather(early, axes, axis=0, tiled=True)
        up_all = lax.all_gather(up_bias.astype(BF), axes, axis=0, tiled=True)
        up_all = up_all.reshape(cut, quarter, d // cut).swapaxes(1, 2).reshape(d, quarter)
        early = jnp.concatenate([early, up_all], 1)
        early = jnp.pad(early, ((0, 0), (0, wide - early.shape[1])))
        wu = lax.all_gather(up_w.astype(BF), axes, axis=0, tiled=True)
        wd = lax.all_gather(down_w.astype(BF), axes, axis=0, tiled=True)
        turned[2] = pltpu.VMEM((d, wide), BF)
        qkv, probs, ct, r1, a1, xt = pl.pallas_call(
            functools.partial(attention_kernel, (n_dp, n_z), False),
            grid=(seqs,),
            in_specs=[smem, seq_block, whole(early.shape)],
            out_specs=acts_specs,
            out_shape=acts_shapes,
            scratch_shapes=turned,
            compiler_params=pltpu.CompilerParams(vmem_limit_bytes=VMEM_LIMIT),
            name="attention_forward",
        )(lengths, tokens, early)

    group = 2 if seqs % 2 == 0 else 1
    chunk = group * seq
    block = 512
    tail = 4 * d // LANES
    out, dr1, dwu, dwd, small = pl.pallas_call(
        functools.partial(forward_kernel, block=block),
        grid=(count // chunk,),
        in_specs=[
            lanes(d, chunk),
            pl.BlockSpec((group, seq, d), lambda i: (i, 0, 0)),
            pl.BlockSpec((d, LANES), lambda i: (0, tail), pipeline_mode=pl.Buffered(1)),
            whole((d, hidden)),
            whole((hidden, d)),
        ],
        out_specs=[
            pl.BlockSpec((group, seq, d), lambda i: (i, 0, 0)),
            lanes(d, chunk),
            whole((cut // 2, 2, d // cut, hidden)),
            whole((cut // 2, 2, hidden // cut, d)),
            whole((d, LANES)),
        ],
        out_shape=[
            shape(tokens.shape, BF),
            shape((d, count), F32),
            shape((cut // 2, 2, d // cut, hidden), BF),
            shape((cut // 2, 2, hidden // cut, d), BF),
            shape((d, LANES), F32),
        ],
        scratch_shapes=[
            pltpu.VMEM((hidden, d), BF),
            pltpu.VMEM((d, hidden), BF),
            pltpu.VMEM((d, chunk), BF),
            pltpu.VMEM((d, chunk), BF),
            pltpu.VMEM((d, chunk), F32),
            pltpu.VMEM((d, chunk), F32),
            pltpu.VMEM((d, hidden), F32),
            pltpu.VMEM((hidden, d), F32),
            pltpu.VMEM((3, d, LANES), F32),
            pltpu.VMEM((hidden, LANES), F32),
            pltpu.VMEM((cut, hidden // cut, LANES), F32),
        ],
        compiler_params=pltpu.CompilerParams(vmem_limit_bytes=VMEM_LIMIT),
        name="feed_forward",
    )(r1, cotangent, early, wu, wd)

    acts_in = [lanes(d), lanes(d), lanes(d), lanes(d), lanes(3 * d), probs_block, whole((d, wide)), whole((d, LANES))]
    base = [
        pltpu.VMEM((d, 3 * d), F32),
        pltpu.VMEM((d, d), F32),
        pltpu.VMEM((3 * d, seq), BF),
        pltpu.VMEM((d, seq), BF),
        pltpu.VMEM((5, d, LANES), F32),
    ]
    if direct:
        n_sems = Scatter.sems(n_dp, n_z)
        plan = ((rows_down, d, BF), (rows, hidden, BF), (rows, 3 * d, BF), (rows, d, BF), (rows, LANES, F32))
        outs = [(rows, 3 * d), (rows, d), (rows, hidden), (rows_down, d), gains.shape, biases.shape, up_rows.shape]
        scratch = list(base)
        for height, width, kind in plan[2:]:
            scratch.append(pltpu.VMEM((slots, 2, height, width), kind))
        scratch += [pltpu.VMEM((LANES, LANES), F32), pltpu.VMEM((rows, LANES), F32)]
        for height, width, kind in plan:
            scratch += Scatter.scratch(n_dp, n_z, height, width, kind)
        scratch += [pltpu.SemaphoreType.DMA((len(plan), n_sems))] * 2
        token_grad, gqkv, gout, gup, gdown, ggains, gbiases, gupb = pl.pallas_call(
            functools.partial(backward_kernel, (n_dp, n_z), True),
            grid=(seqs,),
            in_specs=acts_in + [anywhere, anywhere],
            out_specs=[seq_block] + [whole(o) for o in outs],
            out_shape=[shape(tokens.shape, BF)] + [shape(o, F32) for o in outs],
            scratch_shapes=scratch,
            compiler_params=pltpu.CompilerParams(
                vmem_limit_bytes=VMEM_LIMIT, collective_id=1, has_side_effects=True
            ),
            name="attention_backward",
        )(dr1, xt, a1, ct, qkv, probs, early, small, dwu, dwd)
        return out, token_grad, gqkv, gout, gup, gdown, ggains, gbiases, gupb.reshape(-1)

    token_grad, gqkv, gout, gsmall = pl.pallas_call(
        functools.partial(backward_kernel, (n_dp, n_z), False),
        grid=(seqs,),
        in_specs=acts_in,
        out_specs=[seq_block, whole((d, 3 * d)), whole((d, d)), whole((d, LANES))],
        out_shape=[shape(tokens.shape, BF), shape((d, 3 * d), F32), shape((d, d), F32), shape((d, LANES), F32)],
        scratch_shapes=base,
        compiler_params=pltpu.CompilerParams(vmem_limit_bytes=VMEM_LIMIT),
        name="attention_backward",
    )(dr1, xt, a1, ct, qkv, probs, early, small)

    def scatter(term):
        return lax.psum_scatter(term.astype(F32), axes, scatter_dimension=0, tiled=True)

    up_sums = gsmall[:, 8 : 8 + quarter].reshape(cut, d // cut, quarter).swapaxes(1, 2)
    gsmall = scatter(gsmall[:, :8]).T
    return (
        out,
        token_grad,
        scatter(gqkv),
        scatter(gout),
        scatter(dwu.reshape(d, hidden)),
        scatter(dwd.reshape(hidden, d)),
        gsmall[:2],
        gsmall[2:8],
        scatter(up_sums.reshape(hidden)),
    )


def solution(mesh):
    axes = ("dp", "fsdp")
    rows, cols, flat = P(axes, None), P(None, axes), P(axes)
    data = P(axes, None, None)
    return jax.shard_map(
        functools.partial(per_device, mesh.shape["dp"], mesh.shape["fsdp"]),
        mesh=mesh,
        in_specs=(data, flat, data, rows, rows, rows, rows, cols, cols, flat),
        out_specs=(data, data, rows, rows, rows, rows, cols, cols, flat),
        check_vma=False,
    )
```

time: 1340 us -> 250 us (0.19)
  waiting for transfers between devices: 635 us -> 0 us
  Pallas kernels: 0 us -> 239 us
  matrix products: 234 us -> 0 us
  blocking collectives: 204 us -> 0 us
  local copies, waits for them, and re-layouts: 150 us -> 10.1 us
  other arithmetic: 79 us -> 0 us
  loops' own time: 14 us -> 0 us
  between operations: 14.2 us -> 0.69 us
    reduce_scatter x4 -> x0, waiting for transfers between devices: 524 us -> none  [the longest x1 145 us: per_device(): lax.psum_scatter(totals[2], ('dp', 'fsdp'), scatter_dimension=0, tiled=True)]
    pallas_call x0 -> x3, Pallas kernels: none -> 239 us  [the longest x1 86.4 us: per_device(): pl.pallas_call(functools.partial(backward_kernel, (n_dp, n_z), True), gri...]
    dot_general x63 -> x0, matrix products: 210 us -> none  [the longest x3 24.6 us: backward(): lax.dot_general(grad_low, down_w, CONTRACT_COLS, preferred_element_type=j...]
    all_gather x3 -> x0, blocking collectives: 125 us -> none  [the longest x1 45 us: per_device(): lax.all_gather(out_weight.astype(jnp.bfloat16), ('dp', 'fsdp'), axis=0, t...]
    unnamed x11 -> x0, waiting for transfers between devices: 103 us -> none
    reshape x34 -> x2, local copies, waits for them, and re-layouts: 83.4 us -> 2.53 us  [the longest x1 1.32 us: per_device(): up_rows = up_bias.reshape(quarter, rows)]
    unnamed x2 -> x0, blocking collectives: 78.6 us -> none
    convert_element_type x29 -> x0, other arithmetic: 40.9 us -> none  [the longest x6 10 us: forward(): act_one = (normed_one * gain_f[0] + bias_f[0]).astype(jnp.bfloat16)]
  transfers between devices with their start and end apart: 9 -> 0, of which waited for: 6 -> 0; matrix products, arithmetic and copies ran while one was open for 10% -> 0% of each run, Pallas kernels for 0% -> 0%
where the time goes in v1:
time: 250 us; the launch traced here: 249 us
  Pallas kernels  239 us (96%)
  local copies, waits for them, and re-layouts  10.1 us (4%)
    pallas_call x1, Pallas kernels, per_device(): pl.pallas_call(functools.partial(backward_kernel, (n_dp, n_z), True), gri...  86.4 us
    pallas_call x1, Pallas kernels, per_device(): pl.pallas_call(functools.partial(attention_kernel, (n_dp, n_z), True), gr...  82 us
    pallas_call x1, Pallas kernels, per_device(): pl.pallas_call(functools.partial(forward_kernel, block=block), grid=(coun...  70.2 us
    unnamed x19, local copies, waits for them, and re-layouts  7.55 us

profile of v1, /device:TPU:0, one launch (start us, length us, event | category | flops | bytes accessed | tf_op | source)
XLA Modules:
  0.0 249.4 jit_solution(12801143805327659562)
XLA Ops:
  0.6 1.3 reshape.33.refs_6_
  2.0 82.0 %attention_forward.1 = (bf16[1536,3072]{1,0:T(8,128)(2,1)}, bf16[12,8,256,256]{3,2,1,0:T(8,128)(2,1)}, bf16[512,3072]{1,0:T(8,128)(2,1)}, f32[512,3072]{1,0:T(8,...) custom-call(s32[12]{0:T(128)} %lengths.1, ...), custom_call_target="tpu_custom_call" | custom-call | tf_op jit(solution)/shard_map/attention_forward/pallas_call | solution.py:554
  84.0 70.2 %feed_forward.1 = (bf16[12,256,512]{2,1,0:T(8,128)(2,1)}, f32[512,3072]{1,0:T(8,128)}, bf16[16,2,16,2048]{3,2,1,0:T(8,128)(2,1)}, bf16[16,2,64,512]{3,2,1,0:T(8,128)(2,1)}, f32[512,128]{1,0:T(8,128)}) custom-call(f32[512,3072]{1,0:T(8,128)} %get-tuple-element.31.r1_ref, bf16[12,256,512]{2,1,0:T(8,128)(2,1)} %g_ref.1, bf16[512,2176]{1,0:T(8,128)(2,1)} %bitcast.3, ...), custom_call_target="tpu_custom_call" | custom-call | tf_op jit(solution)/shard_map/feed_forward/pallas_call | solution.py:608
  154.2 86.4 %attention_backward.1 = (bf16[12,256,512]{2,1,0:T(8,128)(2,1)}, f32[16,1536]{1,0:T(8,128)}, f32[16,512]{1,0:T(8,128)}, f32[16,2048]{1,0:T(8,128)}, f32[64,512]{1...) custom-call(f32[512,3072]{1,0:T(8,128)} %get-tuple-element.36.refs_0_, ...), custom_call_target="tpu_custom_call" | custom-call | tf_op jit(solution)/shard_map/attention_backward/pallas_call | solution.py:668
  240.6 1.2 reshape.37
  241.8 0.0 copy-start.2
  241.8 0.0 copy-start.3
  241.8 0.0 copy-start.1
  241.8 0.0 copy-start
  241.8 0.0 copy-start.5
  241.8 0.0 copy-start.4
  241.8 3.8 %copy.26 = bf16[12,256,512]{2,1,0:T(8,128)(2,1)} copy(bf16[12,256,512]{2,1,0:T(8,128)(2,1)} %get-tuple-element.63) | data formatting | bytes 6291456
  245.7 0.0 copy-done.2
  245.7 0.6 copy.27
  246.3 0.0 copy-done.3
  246.3 0.6 copy.28
  246.9 0.0 copy-done.1
  246.9 0.7 copy.29
  247.6 0.0 copy-done
  247.6 0.7 copy.30
  248.2 0.0 copy-done.5
  248.2 0.6 copy.31
  248.8 0.0 copy-done.4
  248.8 0.6 copy.32
Async XLA Ops:
  241.8 3.8 %copy-start.2 = (f32[16,1536]{1,0:T(8,128)S(1)}, f32[16,1536]{1,0:T(8,128)}, u32[]{:S(2)}) copy-start(f32[16,1536]{1,0:T(8,128)} %get-tuple-element.64) | copy-start | bytes 294916
  241.8 4.5 %copy-start.3 = (f32[16,512]{1,0:T(8,128)S(1)}, f32[16,512]{1,0:T(8,128)}, u32[]{:S(2)}) copy-start(f32[16,512]{1,0:T(8,128)} %get-tuple-element.65) | copy-start | bytes 98308
  241.8 5.1 %copy-start.1 = (f32[16,2048]{1,0:T(8,128)S(1)}, f32[16,2048]{1,0:T(8,128)}, u32[]{:S(2)}) copy-start(f32[16,2048]{1,0:T(8,128)} %get-tuple-element.66) | copy-start | bytes 393220
  241.8 5.7 %copy-start = (f32[64,512]{1,0:T(8,128)S(1)}, f32[64,512]{1,0:T(8,128)}, u32[]{:S(2)}) copy-start(f32[64,512]{1,0:T(8,128)} %get-tuple-element.67) | copy-start | bytes 393220
  241.8 6.4 %copy-start.5 = (f32[2,16]{1,0:T(2,128)S(1)}, f32[2,16]{1,0:T(2,128)}, u32[]{:S(2)}) copy-start(f32[2,16]{1,0:T(2,128)} %get-tuple-element.68) | copy-start | bytes 388
  241.8 7.0 %copy-start.4 = (f32[6,16]{1,0:T(8,128)S(1)}, f32[6,16]{1,0:T(8,128)}, u32[]{:S(2)}) copy-start(f32[6,16]{1,0:T(8,128)} %get-tuple-element.69) | copy-start | bytes 1156

commit v2 on v1

v2 whole, which is shorter than its diff:
```python
import functools

import jax
import jax.numpy as jnp
from jax import lax
from jax.experimental import pallas as pl
from jax.experimental.pallas import tpu as pltpu
from jax.sharding import PartitionSpec as P

F32, BF = jnp.float32, jnp.bfloat16
MESH = pl.DeviceIdType.MESH
HEADS = 8
EPS = 1e-5
C0 = 0.7978845608028654
C1 = C0 * 0.044715
LANES = 128
NN = (((1,), (0,)), ((), ()))
NT = (((1,), (1,)), ((), ()))
TN = (((0,), (0,)), ((), ()))
VMEM_LIMIT = 60 * 2**20


def dot(a, b, dims=NN):
    return lax.dot_general(a, b, dims, preferred_element_type=F32)


def lane_sums(v):
    total = v[:, :LANES]
    for at in range(LANES, v.shape[1], LANES):
        total = total + v[:, at : at + LANES]
    return total


def normalize(v):
    center = v - jnp.mean(v, 0, keepdims=True)
    inverse = lax.rsqrt(jnp.mean(center * center, 0, keepdims=True) + EPS)
    return center * inverse, inverse


def normalize_back(grad, normed, inverse, gain):
    scaled = grad * gain
    return inverse * (
        scaled
        - jnp.mean(scaled, 0, keepdims=True)
        - normed * jnp.mean(scaled * normed, 0, keepdims=True)
    )


class Place:
    def __init__(self, n_dp, n_z):
        self.n_dp, self.n_z = n_dp, n_z
        self.dp = lax.axis_index("dp")
        fsdp = lax.axis_index("fsdp")
        self.fsdp, self.z, self.core = fsdp, fsdp // 2, fsdp % 2
        self.slot = self.dp * n_z + self.z
        self.mate = (self.dp, self.z * 2 + 1 - self.core)

    def z_of(self, k):
        return lax.rem(self.z + k, self.n_z)

    def dp_of(self, k):
        return lax.rem(self.dp + k, self.n_dp)

    def z_peer(self, k):
        return (self.dp, self.z_of(k) * 2 + self.core)

    def dp_peer(self, k):
        return (self.dp_of(k), self.fsdp)

    def greet(self):
        barrier = pltpu.get_barrier_semaphore()
        peers = [self.mate]
        peers += [self.z_peer(k) for k in range(1, self.n_z)]
        peers += [self.dp_peer(k) for k in range(1, self.n_dp)]
        for peer in peers:
            pl.semaphore_signal(barrier, inc=1, device_id=peer, device_id_type=MESH)
        pl.semaphore_wait(barrier, len(peers))


class Gather:
    def __init__(self, place, own, whole, send, recv):
        self.p, self.own, self.whole, self.send, self.recv = place, own, whole, send, recv

    def put(self, src, slot, core, peer, at):
        pltpu.make_async_remote_copy(
            src_ref=src,
            dst_ref=self.whole.at[slot, core],
            send_sem=self.send.at[at],
            recv_sem=self.recv.at[slot, core],
            device_id=peer,
            device_id_type=MESH,
        ).start()

    def landed(self, slot, core):
        there = self.whole.at[slot, core]
        pltpu.make_async_copy(there, there, self.recv.at[slot, core]).wait()

    def start(self):
        p, at = self.p, 0
        peers = [p.z_peer(k) for k in range(1, p.n_z)]
        peers += [p.dp_peer(k) for k in range(1, p.n_dp)]
        for peer in peers + [p.mate]:
            self.put(self.own, p.slot, p.core, peer, at)
            at += 1

    def along_z(self):
        p = self.p
        at = p.n_z + p.n_dp - 1
        for k in range(1, p.n_z):
            slot = p.dp * p.n_z + p.z_of(k)
            self.landed(slot, p.core)
            for peer in [p.dp_peer(m) for m in range(1, p.n_dp)] + [p.mate]:
                self.put(self.whole.at[slot, p.core], slot, p.core, peer, at)
                at += 1

    def over_dp(self):
        p = self.p
        at = p.n_z + p.n_dp - 1 + (p.n_z - 1) * p.n_dp
        for k in range(0, p.n_z):
            for m in range(1, p.n_dp):
                slot = p.dp_of(m) * p.n_z + p.z_of(k)
                self.landed(slot, p.core)
                self.put(self.whole.at[slot, p.core], slot, p.core, p.mate, at)
                at += 1

    def finish(self):
        p = self.p
        for k in range(0, p.n_z):
            for m in range(0, p.n_dp):
                self.landed(p.dp_of(m) * p.n_z + p.z_of(k), 1 - p.core)
        for at in range(self.sends(p.n_dp, p.n_z)):
            pltpu.make_async_copy(self.own, self.own, self.send.at[at]).wait()

    @staticmethod
    def sends(n_dp, n_z):
        return 2 * n_dp * n_z - 1


def attention_kernel(mesh_sizes, gathers, groups, lengths, x_ref, *refs):
    n_dp, n_z = mesh_sizes
    if gathers:
        (qkv_s, wo_s, wu_s, wd_s, gains_s, biases_s, upb_s,
         qkv_ref, probs_ref, ct_ref, r1_ref, a1_ref, early_ref, wo_ref, wu_ref, wd_ref,
         wqkv_t, wo_t, xt_s, normed_s, early, wo, early_own, wo_own, wu_own, wd_own, small, sems, rems, local) = refs
    else:
        (early_in, wo_in,
         qkv_ref, probs_ref, ct_ref, r1_ref, a1_ref,
         wqkv_t, wo_t, xt_s, normed_s, early, wo) = refs
    step = pl.program_id(0)
    group = lax.rem(step, groups)
    many, seq, d = x_ref.shape
    half = d // 2
    head = d // HEADS
    scale = head**-0.5

    if gathers:
        place = Place(n_dp, n_z)
        first = Gather(place, early_own, early, sems.at[0], rems.at[0])
        out = Gather(place, wo_own, wo, sems.at[1], rems.at[1])
        up = Gather(place, wu_own, wu_ref, sems.at[2], rems.at[2])
        down = Gather(place, wd_own, wd_ref, sems.at[3], rems.at[3])
        here = (place.slot, place.core)
        copies = [
            pltpu.make_async_copy(wu_own, wu_ref.at[here], local.at[0]),
            pltpu.make_async_copy(wd_own, wd_ref.at[here], local.at[1]),
            pltpu.make_async_copy(early, early_ref, local.at[2]),
            pltpu.make_async_copy(wo, wo_ref, local.at[3]),
        ]

        @pl.when(step == 0)
        def _():
            rows = qkv_s.shape[0]
            small[...] = jnp.zeros_like(small)
            small[0:2, :rows] = gains_s[...]
            small[2:8, :rows] = biases_s[...]
            for r in range(upb_s.shape[1] // rows):
                small[8 + r : 9 + r, :rows] = upb_s[:, r * rows : (r + 1) * rows]
            early_own[:, : 3 * d] = qkv_s[...].astype(BF)
            early_own[:, 3 * d :] = small[...].T[:rows].astype(BF)
            place.greet()
            first.start()
            wo_own[...] = wo_s[...].astype(BF)
            out.start()
            early[here] = early_own[...]
            wo[here] = wo_own[...]
            wu_own[...] = wu_s[...].astype(BF)
            wd_own[...] = wd_s[...].astype(BF)
            for copy in copies[:2]:
                copy.start()

        plan = {
            1: [first.along_z, out.along_z],
            2: [first.over_dp, out.over_dp],
            3: [up.start, down.start],
            4: [first.finish, out.finish, copies[2].start, copies[3].start],
            5: [up.along_z, down.along_z],
            6: [up.over_dp, down.over_dp],
        }
        for at, actions in plan.items():

            @pl.when(step == at)
            def _(actions=actions):
                for action in actions:
                    action()

    else:

        @pl.when(step == 0)
        def _():
            early[...] = early_in[...].reshape(early.shape)
            wo[...] = wo_in[...].reshape(wo.shape)

    @pl.when(step == groups)
    def _():
        whole = early[...].reshape(d, 3 * d + LANES)
        for hb in range(2):
            for part in range(3):
                to = (hb * 3 + part) * half
                at = part * d + hb * half
                wqkv_t[to : to + half] = whole[:, at : at + half].T
        wo_t[...] = wo[...].reshape(d, d).T

    @pl.when(step < groups)
    def _():
        for s in range(many):
            xt = x_ref[s].T
            xt_s[group, :, seq * s : seq * (s + 1)] = xt
            normed, _ = normalize(xt.astype(F32))
            normed_s[group, :, seq * s : seq * (s + 1)] = normed

    @pl.when(step >= groups)
    def _():
        column = early[..., 3 * d :].reshape(d, LANES).astype(F32)
        a1 = (normed_s[group] * column[:, 0:1] + column[:, 2:3]).astype(BF)
        a1_ref[...] = a1
        for hb in range(2):
            at, rows = hb * 3 * half, slice(hb * half, (hb + 1) * half)
            query = (dot(wqkv_t[at : at + half], a1) + column[rows, 3:4]).astype(BF)
            qkv_ref[at : at + half] = (query.astype(F32) * scale).astype(BF)
            at += half
            qkv_ref[at : at + half] = dot(wqkv_t[at : at + half], a1).astype(BF)
            at += half
            qkv_ref[at : at + half] = (dot(wqkv_t[at : at + half], a1) + column[rows, 4:5]).astype(BF)
        row = lax.broadcasted_iota(jnp.int32, (seq, seq), 0)
        valid = [row < lengths[group * many + s] for s in range(many)]
        items = [(s, h) for s in range(many) for h in range(HEADS)]

        def place_of(s, h, part):
            at = (h // (HEADS // 2) * 3 + part) * half + h % (HEADS // 2) * head
            return slice(at, at + head), slice(seq * s, seq * (s + 1))

        def score(s, h):
            return dot(qkv_ref[place_of(s, h, 1)], qkv_ref[place_of(s, h, 0)], TN)

        def soften(s, scores):
            scores = jnp.where(valid[s], scores, -1e30)
            exponent = jnp.exp(scores - jnp.max(scores, 0, keepdims=True))
            return (exponent * (1.0 / jnp.sum(exponent, 0, keepdims=True))).astype(BF)

        def mix(s, h, probs):
            probs_ref[s, h] = probs
            ct_ref[h * head : (h + 1) * head, seq * s : seq * (s + 1)] = dot(
                qkv_ref[place_of(s, h, 2)], probs
            ).astype(BF)

        def attended(s):
            at = slice(seq * s, seq * (s + 1))
            r1_ref[:, at] = (
                xt_s[group, :, at].astype(F32) + dot(wo_t[...], ct_ref[:, at]) + column[:, 5:6]
            )

        scores, probs = score(*items[0]), None
        for at, (s, h) in enumerate(items):
            ahead = score(*items[at + 1]) if at + 1 < len(items) else None
            if at:
                mix(*items[at - 1], probs)
            if s and h == 2:
                attended(s - 1)
            probs, scores = soften(s, scores), ahead
        mix(*items[-1], probs)

        attended(many - 1)

    if gathers:

        @pl.when(step == 2 * groups - 1)
        def _():
            up.finish()
            down.finish()
            for copy in copies:
                copy.wait()


def forward_kernel(
    r1_first, g_first, r1_next, g_next, column_ref, wu_ref, wd_ref,
    out_ref, dr1_ref, dwu_ref, dwd_ref, small_ref,
    wu_t, wd_t, gt, gt_next, a2, a2_next, normed, inverse, total_out, total_a2, total_wu, total_wd,
    u_s, dh_s, h_s, du_s, sums, sums_up, up_bias, *, block,
):
    step = pl.program_id(0)
    d, tokens = dr1_ref.shape
    hidden = wd_ref.shape[0]
    n_dev = dwd_ref.shape[0] * 2
    rows = d // n_dev
    seqs, seq = g_next.shape[:2]
    column = column_ref[...].astype(F32)
    blocks = hidden // block

    def prepare(r1_ref, g_ref, gt_to, a2_to):
        for s in range(seqs):
            gt_to[:, seq * s : seq * (s + 1)] = g_ref[s].T
        r1 = r1_ref[...]
        n, inv = normalize(r1)
        a2_to[...] = (n * column[:, 1:2] + column[:, 6:7]).astype(BF)
        normed[...] = n
        inverse[...] = jnp.broadcast_to(inv, inverse.shape)
        total_out[...] = r1 + column[:, 7:8]

    @pl.when(step == 0)
    def _():
        wu_t[...] = wu_ref[...].T
        wd_t[...] = wd_ref[...].T
        total_wu[...] = jnp.zeros_like(total_wu)
        total_wd[...] = jnp.zeros_like(total_wd)
        sums[...] = jnp.zeros_like(sums)
        sums_up[...] = jnp.zeros_like(sums_up)
        for r in range(hidden // d):
            up_bias[:, r * rows : (r + 1) * rows, :] = jnp.broadcast_to(
                column[:, 8 + r : 9 + r].reshape(n_dev, rows, 1), (n_dev, rows, LANES)
            )
        prepare(r1_first, g_first, gt, a2)

    per = block // (hidden // n_dev)

    def span(j):
        return slice(j * block, (j + 1) * block)

    def enter(j):
        bias = up_bias[j * per : (j + 1) * per].reshape(block, LANES)[:, 0:1]
        u_s[j % 2] = dot(wu_t[span(j)], a2[...]) + bias
        dh_s[j % 2] = dot(wd_ref[span(j)], gt[...])

    def bend(j):
        u = u_s[j % 2]
        square = u * u
        part = 0.5 + 0.5 * jnp.tanh(u * (C0 + C1 * square))
        h = u * part
        h_s[j] = h.astype(BF)
        slope = part + h * (1.0 - part) * (2 * C0 + 6 * C1 * square)
        du = (dh_s[j % 2] * slope).astype(BF)
        du_s[j] = du
        sums_up[span(j)] += lane_sums(du.astype(F32))

    def leave(j):
        total_out[...] += dot(wd_t[:, span(j)], h_s[j])
        term = dot(wu_ref[:, span(j)], du_s[j])
        total_a2[...] = term if j == 0 else total_a2[...] + term

    def weights(j):
        total_wd[span(j)] += dot(h_s[j], gt[...], NT)
        total_wu[:, span(j)] += dot(a2[...], du_s[j], NT)

    def close():
        for s in range(seqs):
            out_ref[s] = total_out[:, seq * s : seq * (s + 1)].astype(BF).T
        da2, n, g = total_a2[...], normed[...], gt[...].astype(F32)
        dr1_ref[...] = g + normalize_back(da2, n, inverse[0:1], column[:, 1:2])
        sums[0] += lane_sums(da2 * n)
        sums[1] += lane_sums(da2)
        sums[2] += lane_sums(g)

    enter(0)
    for j in range(blocks):
        if j + 1 < blocks:
            enter(j + 1)
        if j:
            leave(j - 1)
        bend(j)
        if 0 < j < blocks - 1:
            weights(j - 1)
    leave(blocks - 1)
    weights(blocks - 2)
    close()
    weights(blocks - 1)
    prepare(r1_next, g_next, gt_next, a2_next)
    gt[...] = gt_next[...]
    a2[...] = a2_next[...]

    @pl.when(step == pl.num_programs(0) - 1)
    def _():
        dwu_ref[...] = total_wu[...].astype(BF).reshape(dwu_ref.shape)
        dwd_ref[...] = total_wd[...].astype(BF).reshape(dwd_ref.shape)
        lane = lax.broadcasted_iota(jnp.int32, (d, LANES), 1)
        small = jnp.zeros((d, LANES), F32)
        for s, at in ((0, 1), (1, 6), (2, 7)):
            small = jnp.where(lane == at, jnp.sum(sums[s], 1, keepdims=True), small)
        up = jnp.sum(sums_up[...], 1, keepdims=True).reshape(n_dev, hidden // n_dev, 1)
        for r in range(hidden // d):
            part = up[:, r * rows : (r + 1) * rows].reshape(d, 1)
            small = jnp.where(lane == 8 + r, part, small)
        small_ref[...] = small


class Scatter:
    def __init__(self, place, part, result, bufs, send, recv):
        self.p, self.part, self.result = place, part, result
        self.mine, self.got1, self.sum1, self.got2, self.sum2, self.got3 = bufs
        self.send, self.recv = send, recv

    @staticmethod
    def scratch(n_dp, n_z, rows, width, kind):
        return [
            pltpu.VMEM((n_dp * n_z, rows, width), kind),
            pltpu.VMEM((n_dp * n_z, rows, width), kind),
            pltpu.VMEM((n_dp * n_z, rows, width), kind),
            pltpu.VMEM((n_dp - 1, n_z, rows, width), kind),
            pltpu.VMEM((n_z, rows, width), kind),
            pltpu.VMEM((n_z - 1, rows, width), kind),
        ]

    @staticmethod
    def sems(n_dp, n_z):
        return n_dp + n_z

    def copy(self, src, dst, at, peer):
        return pltpu.make_async_remote_copy(
            src_ref=src,
            dst_ref=dst,
            send_sem=self.send.at[at],
            recv_sem=self.recv.at[at],
            device_id=peer,
            device_id_type=MESH,
        )

    def to_mate(self):
        p = self.p
        return self.copy(self.part.at[:, 1 - p.core], self.got1, 0, p.mate)

    def own(self):
        p = self.p
        return pltpu.make_async_copy(
            self.part.at[:, p.core], self.mine, self.send.at[p.n_dp + p.n_z - 1]
        )

    def over_dp(self):
        p = self.p
        return [
            self.copy(
                self.sum1.at[pl.ds(p.dp_of(k) * p.n_z, p.n_z)], self.got2.at[k - 1], k, p.dp_peer(k)
            )
            for k in range(1, p.n_dp)
        ]

    def along_z(self):
        p = self.p
        return [
            self.copy(
                self.sum2.at[p.z_of(k)], self.got3.at[k - 1], p.n_dp - 1 + k, p.z_peer(k)
            )
            for k in range(1, p.n_z)
        ]

    def step1(self):
        self.to_mate().start()
        self.own().start()

    def step2(self):
        self.own().wait()
        self.to_mate().wait()

        def add(s, _):
            self.sum1[s] = (self.mine[s].astype(F32) + self.got1[s].astype(F32)).astype(
                self.sum1.dtype
            )
            return 0

        lax.fori_loop(0, self.p.n_dp * self.p.n_z, add, 0)
        for copy in self.over_dp():
            copy.start()

    def step3(self):
        for copy in self.over_dp():
            copy.wait()

        def add(s, _):
            total = self.sum1[self.p.dp * self.p.n_z + s].astype(F32)
            for k in range(self.p.n_dp - 1):
                total = total + self.got2[k, s].astype(F32)
            self.sum2[s] = total.astype(self.sum2.dtype)
            return 0

        lax.fori_loop(0, self.p.n_z, add, 0)
        for copy in self.along_z():
            copy.start()

    def step4(self):
        for copy in self.along_z():
            copy.wait()
        total = self.sum2[self.p.z].astype(F32)
        for k in range(self.p.n_z - 1):
            total = total + self.got3[k].astype(F32)
        self.result[...] = total


def backward_kernel(mesh_sizes, scatters, groups, *refs):
    n_dp, n_z = mesh_sizes
    (dr1_ref, ct_ref, qkv_ref, probs_ref, a1_ref, x_ref, early_ref, wo_ref, part_ref) = refs[:9]
    refs = refs[9:]
    if scatters:
        (dwu_ref, dwd_ref, tg_ref, gqkv_ref, gout_ref, gup_ref, gdown_ref, gsmall_ref,
         dp_s, wqkv, total_qkv, total_out, dc_s, sums, part_qkv, part_out, part_small, gqkv_half) = refs[:18]
        buffers, (send, recv) = refs[18:-2], refs[-2:]
    else:
        (tg_ref, gqkv_ref, gout_ref, gsmall_ref, dp_s, wqkv, total_qkv, total_out, dc_s, sums) = refs
    step = pl.program_id(0)
    last = pl.num_programs(0) - 1
    stage, group = step // groups, lax.rem(step, groups)
    d = dr1_ref.shape[0]
    many, seq = x_ref.shape[:2]
    half, head = d // 2, d // HEADS
    scale = head**-0.5
    column = early_ref[:, 3 * d :].astype(F32)

    @pl.when(step == 0)
    def _():
        sums[...] = jnp.zeros_like(sums)
        for hb in range(2):
            for part in range(3):
                at = part * d + hb * half
                wqkv[hb, :, part * half : (part + 1) * half] = early_ref[:, at : at + half]

    if scatters:
        place = Place(n_dp, n_z)
        down, up, qkv0, qkv1, out, small_piece = [
            Scatter(place, part, result, buffers[6 * i : 6 * i + 6], send.at[i], recv.at[i])
            for i, (part, result) in enumerate(
                (
                    (dwd_ref, gdown_ref),
                    (dwu_ref, gup_ref),
                    (part_qkv.at[0], gqkv_half.at[0]),
                    (part_qkv.at[1], gqkv_half.at[1]),
                    (part_out, gout_ref),
                    (part_small, gsmall_ref),
                )
            )
        ]

        def pack(hb):
            part_qkv[hb] = total_qkv[hb].astype(BF).reshape(part_qkv.shape[1:])

        def pack_out():
            part_out[...] = total_out[...].astype(BF).reshape(part_out.shape)

        plan = {
            0: [place.greet, down.step1, up.step1],
            1: [down.step2],
            2: [up.step2],
            4: [lambda: pack(0), qkv0.step1],
            5: [qkv0.step2, down.step3],
            7: [up.step3],
            8: [lambda: pack(1), qkv1.step1, pack_out, out.step1, down.step4],
            9: [qkv1.step2, out.step2, qkv0.step3],
            10: [up.step4],
            11: [qkv0.step4, qkv1.step3, out.step3],
        }
        for at, actions in plan.items():

            @pl.when(step == at)
            def _(actions=actions):
                for action in actions:
                    action()

    @pl.when(stage < 2)
    def _():
        do = dr1_ref[...].astype(BF)
        mine = pl.ds(pl.multiple_of(stage * half, half), half)
        dc_s[...] = dot(wo_ref[mine, :], do).astype(BF)
        to = dp_s.at[stage, group]
        items = [(s, h) for s in range(many) for h in range(HEADS // 2)]

        def place_of(s, h, part):
            at = part * half + h * head
            return slice(at, at + head), slice(seq * s, seq * (s + 1))

        def grad_probs(s, h):
            return dot(qkv_ref[place_of(s, h, 2)], dc_s[place_of(s, h, 0)], TN)

        def grad_scores(s, h, term):
            at = place_of(s, h, 0)
            delta = jnp.sum(dc_s[at].astype(F32) * ct_ref[at].astype(F32), 0, keepdims=True)
            return (probs_ref[s, h].astype(F32) * (term - delta)).astype(BF)

        def finish(s, h, ds):
            q, k, v = (place_of(s, h, part) for part in range(3))
            to[v] = dot(dc_s[q], probs_ref[s, h], NT).astype(BF)
            to[k] = dot(qkv_ref[q], ds, NT).astype(BF)
            to[q] = (dot(qkv_ref[k], ds) * scale).astype(BF)

        term, ds = grad_probs(*items[0]), None
        for at, item in enumerate(items):
            ahead = grad_probs(*items[at + 1]) if at + 1 < len(items) else None
            if at:
                finish(*items[at - 1], ds)
            ds, term = grad_scores(*item, term), ahead
        opening = group == 0
        term = dot(ct_ref[...], do, NT)
        total_out[mine, :] = jnp.where(opening, term, total_out[mine, :] + term)
        finish(*items[-1], ds)
        term = dot(a1_ref[...], to[...], NT)
        total_qkv[stage] = jnp.where(opening, term, total_qkv[stage] + term)
        sums[2, mine, :] += lane_sums(to[0:half].astype(F32))
        sums[3, mine, :] += lane_sums(to[2 * half :].astype(F32))
        sums[4, mine, :] += lane_sums(dr1_ref[mine, :].astype(BF).astype(F32))

    @pl.when(stage == 2)
    def _():
        def product(s):
            at = slice(seq * s, seq * (s + 1))
            return dot(wqkv[0], dp_s[0, group, :, at]) + dot(wqkv[1], dp_s[1, group, :, at])

        def finish(s, da1):
            normed, inverse = normalize(x_ref[s].T.astype(F32))
            dv = normalize_back(da1, normed, inverse, column[:, 0:1])
            tg_ref[s] = (dr1_ref[:, seq * s : seq * (s + 1)] + dv).astype(BF).T
            sums[0] += lane_sums(da1 * normed)
            sums[1] += lane_sums(da1)

        da1 = product(0)
        for s in range(many):
            ahead = product(s + 1) if s + 1 < many else None
            finish(s, da1)
            da1 = ahead

    @pl.when(step == last)
    def _():
        lane = lax.broadcasted_iota(jnp.int32, (d, LANES), 1)
        small = part_ref[...]
        for s, at in enumerate((0, 2, 3, 4, 5)):
            small = jnp.where(lane == at, jnp.sum(sums[s], 1, keepdims=True), small)
        if not scatters:
            for hb in range(2):
                for part in range(3):
                    at = part * d + hb * half
                    gqkv_ref[:, at : at + half] = total_qkv[hb, :, part * half : (part + 1) * half]
            gout_ref[...] = total_out[...]
            gsmall_ref[...] = small
            return
        part_small[...] = small.reshape(part_small.shape)
        small_piece.step1()
        qkv1.step4()
        small_piece.step2()
        out.step4()
        small_piece.step3()
        for hb in range(2):
            for part in range(3):
                at = part * d + hb * half
                gqkv_ref[:, at : at + half] = gqkv_half[hb, :, part * half : (part + 1) * half]
        small_piece.step4()


def finish_kernel(tg, qkv, out, up, down, small, tg_to, qkv_to, out_to, up_to, down_to, gains, biases, upb, turn, sems):
    copies = [
        pltpu.make_async_copy(tg.at[s], tg_to.at[s], sems.at[s]) for s in range(tg.shape[0])
    ]
    pairs = ((qkv, qkv_to), (out, out_to), (up, up_to), (down, down_to))
    copies += [
        pltpu.make_async_copy(a, b, sems.at[tg.shape[0] + i]) for i, (a, b) in enumerate(pairs)
    ]
    for copy in copies:
        copy.start()
    rows = small.shape[0]
    turn[...] = jnp.zeros_like(turn)
    turn[:rows] = small[...]
    turned = turn[...].T
    gains[...] = turned[0:2, :rows]
    biases[...] = turned[2:8, :rows]
    for r in range(upb.shape[1] // rows):
        upb[:, r * rows : (r + 1) * rows] = turned[8 + r : 9 + r, :rows]
    for copy in copies:
        copy.wait()


def per_device(n_dp, n_fsdp, tokens, lengths, cotangent, qkv_w, out_w, up_w, down_w, gains, biases, up_bias):
    seqs, seq, d = tokens.shape
    n_z, n_dev = n_fsdp // 2, n_dp * n_fsdp
    rows, rows_down = qkv_w.shape[0], down_w.shape[0]
    hidden = up_w.shape[1]
    half = d // 2
    slots = n_dp * n_z
    count = seqs * seq
    wide = 3 * d + LANES
    axes = ("dp", "fsdp")
    direct = rows % 16 == 0
    cut = n_dev if direct else 32
    quarter = hidden // d
    many = next(m for m in (3, 2, 1) if seqs % m == 0)
    groups, width = seqs // many, many * seq

    def whole(shape):
        return pl.BlockSpec(shape, lambda i: (0,) * len(shape), pipeline_mode=pl.Buffered(1))

    def shape(dims, kind):
        return jax.ShapeDtypeStruct(dims, kind)

    anywhere = pl.BlockSpec(memory_space=pl.ANY)
    smem = pl.BlockSpec(memory_space=pltpu.SMEM)

    def norms(i):
        return jnp.minimum(i, groups - 1)

    def heads(i):
        return jnp.maximum(i - groups, 0)

    def lanes(height):
        return pl.BlockSpec((height, width), lambda i: (0, heads(i)))

    acts_specs = [
        lanes(3 * d),
        pl.BlockSpec((many, HEADS, seq, seq), lambda i: (heads(i), 0, 0, 0)),
        lanes(d),
        lanes(d),
        lanes(d),
    ]
    acts_shapes = [
        shape((3 * d, count), BF),
        shape((seqs, HEADS, seq, seq), BF),
        shape((d, count), BF),
        shape((d, count), F32),
        shape((d, count), BF),
    ]
    in_specs = [smem, pl.BlockSpec((many, seq, d), lambda i: (norms(i), 0, 0))]
    grid_shape = (slots, 2, rows) if direct else (d,)
    scratch = [
        pltpu.VMEM((3 * d, d), BF),
        pltpu.VMEM((d, d), BF),
        pltpu.VMEM((groups, d, width), BF),
        pltpu.VMEM((groups, d, width), F32),
        pltpu.VMEM((*grid_shape, wide), BF),
        pltpu.VMEM((*grid_shape, d), BF),
    ]
    if direct:
        n_sends = Gather.sends(n_dp, n_z)
        shards = (qkv_w, out_w, up_w, down_w, gains, biases, up_bias.reshape(1, -1))
        qkv, probs, ct, r1, a1, early, wo, wu, wd = pl.pallas_call(
            functools.partial(attention_kernel, (n_dp, n_z), True, groups),
            grid=(2 * groups,),
            in_specs=in_specs + [whole(s.shape) for s in shards],
            out_specs=acts_specs + [anywhere] * 4,
            out_shape=acts_shapes
            + [
                shape((slots, 2, rows, wide), BF),
                shape((slots, 2, rows, d), BF),
                shape((slots, 2, rows, hidden), BF),
                shape((slots, 2, rows_down, d), BF),
            ],
            scratch_shapes=scratch
            + [
                pltpu.VMEM((rows, wide), BF),
                pltpu.VMEM((rows, d), BF),
                pltpu.VMEM((rows, hidden), BF),
                pltpu.VMEM((rows_down, d), BF),
                pltpu.VMEM((LANES, LANES), F32),
                pltpu.SemaphoreType.DMA((4, n_sends)),
                pltpu.SemaphoreType.DMA((4, slots, 2)),
                pltpu.SemaphoreType.DMA((4,)),
            ],
            compiler_params=pltpu.CompilerParams(
                vmem_limit_bytes=VMEM_LIMIT, collective_id=0, has_side_effects=True
            ),
            name="attention_forward",
        )(lengths, tokens, *shards)
        early, wo = early.reshape(d, wide), wo.reshape(d, d)
        wu, wd = wu.reshape(d, hidden), wd.reshape(hidden, d)
    else:
        early = jnp.concatenate([qkv_w, gains.T, biases.T], 1).astype(BF)
        early = lax.all_gather(early, axes, axis=0, tiled=True)
        up_all = lax.all_gather(up_bias.astype(BF), axes, axis=0, tiled=True)
        up_all = up_all.reshape(cut, quarter, d // cut).swapaxes(1, 2).reshape(d, quarter)
        early = jnp.concatenate([early, up_all], 1)
        early = jnp.pad(early, ((0, 0), (0, wide - early.shape[1])))
        wo = lax.all_gather(out_w.astype(BF), axes, axis=0, tiled=True)
        wu = lax.all_gather(up_w.astype(BF), axes, axis=0, tiled=True)
        wd = lax.all_gather(down_w.astype(BF), axes, axis=0, tiled=True)
        qkv, probs, ct, r1, a1 = pl.pallas_call(
            functools.partial(attention_kernel, (n_dp, n_z), False, groups),
            grid=(2 * groups,),
            in_specs=in_specs + [whole(early.shape), whole(wo.shape)],
            out_specs=acts_specs,
            out_shape=acts_shapes,
            scratch_shapes=scratch,
            compiler_params=pltpu.CompilerParams(vmem_limit_bytes=VMEM_LIMIT),
            name="attention_forward",
        )(lengths, tokens, early, wo)

    pair = 2 if seqs % 2 == 0 else 1
    chunk = pair * seq
    chunks = seqs // pair
    block = d
    tail = 3 * d // LANES

    def following(i):
        return jnp.minimum(i + 1, chunks - 1)

    out, dr1, dwu, dwd, small = pl.pallas_call(
        functools.partial(forward_kernel, block=block),
        grid=(chunks,),
        in_specs=[
            whole((d, chunk)),
            whole((pair, seq, d)),
            pl.BlockSpec((d, chunk), lambda i: (0, following(i))),
            pl.BlockSpec((pair, seq, d), lambda i: (following(i), 0, 0)),
            pl.BlockSpec((d, LANES), lambda i: (0, tail), pipeline_mode=pl.Buffered(1)),
            whole((d, hidden)),
            whole((hidden, d)),
        ],
        out_specs=[
            pl.BlockSpec((pair, seq, d), lambda i: (i, 0, 0)),
            pl.BlockSpec((d, chunk), lambda i: (0, i)),
            whole((cut // 2, 2, d // cut, hidden)),
            whole((cut // 2, 2, hidden // cut, d)),
            whole((d, LANES)),
        ],
        out_shape=[
            shape(tokens.shape, BF),
            shape((d, count), F32),
            shape((cut // 2, 2, d // cut, hidden), BF),
            shape((cut // 2, 2, hidden // cut, d), BF),
            shape((d, LANES), F32),
        ],
        scratch_shapes=[pltpu.VMEM((hidden, d), BF), pltpu.VMEM((d, hidden), BF)]
        + [pltpu.VMEM((d, chunk), BF)] * 4
        + [pltpu.VMEM((d, chunk), F32), pltpu.VMEM((8, chunk), F32)]
        + [pltpu.VMEM((d, chunk), F32)] * 2
        + [pltpu.VMEM((d, hidden), F32), pltpu.VMEM((hidden, d), F32)]
        + [pltpu.VMEM((2, block, chunk), F32)] * 2
        + [pltpu.VMEM((hidden // block, block, chunk), BF)] * 2
        + [
            pltpu.VMEM((3, d, LANES), F32),
            pltpu.VMEM((hidden, LANES), F32),
            pltpu.VMEM((cut, hidden // cut, LANES), F32),
        ],
        compiler_params=pltpu.CompilerParams(vmem_limit_bytes=VMEM_LIMIT),
        name="feed_forward",
    )(r1, cotangent, r1, cotangent, early, wu, wd)

    def turn(i):
        return lax.rem(i, groups)

    def hold(i):
        return jnp.where(i < 2 * groups, turn(i), groups - 1)

    def side(i):
        return jnp.minimum(i // groups, 1)

    def late(i):
        return jnp.where(i < 2 * groups, 0, turn(i))

    seq_block = pl.BlockSpec((many, seq, d), lambda i: (late(i), 0, 0))
    acts_in = [
        pl.BlockSpec((d, width), lambda i: (0, turn(i))),
        pl.BlockSpec((half, width), lambda i: (side(i), hold(i))),
        pl.BlockSpec((3 * half, width), lambda i: (side(i), hold(i))),
        pl.BlockSpec((many, HEADS // 2, seq, seq), lambda i: (hold(i), side(i), 0, 0)),
        pl.BlockSpec((d, width), lambda i: (0, hold(i))),
        seq_block,
        whole((d, wide)),
        whole((d, d)),
        whole((d, LANES)),
    ]
    base = [
        pltpu.VMEM((2, groups, 3 * half, width), BF),
        pltpu.VMEM((2, d, 3 * half), BF),
        pltpu.VMEM((2, d, 3 * half), F32),
        pltpu.VMEM((d, d), F32),
        pltpu.VMEM((half, width), BF),
        pltpu.VMEM((5, d, LANES), F32),
    ]
    acts = (dr1, ct, qkv, probs, a1, tokens, early, wo, small)
    if direct:
        n_sems = Scatter.sems(n_dp, n_z)
        plan = ((rows_down, d, BF), (rows, hidden, BF), (rows, 3 * half, BF), (rows, 3 * half, BF), (rows, d, BF), (rows, LANES, F32))
        outs = [(rows, 3 * d), (rows, d), (rows, hidden), (rows_down, d), (rows, LANES)]
        scratch = base + [
            pltpu.VMEM((2, slots, 2, rows, 3 * half), BF),
            pltpu.VMEM((slots, 2, rows, d), BF),
            pltpu.VMEM((slots, 2, rows, LANES), F32),
            pltpu.VMEM((2, rows, 3 * half), F32),
        ]
        for height, across, kind in plan:
            scratch += Scatter.scratch(n_dp, n_z, height, across, kind)
        scratch += [pltpu.SemaphoreType.DMA((len(plan), n_sems))] * 2
        grads = pl.pallas_call(
            functools.partial(backward_kernel, (n_dp, n_z), True, groups),
            grid=(3 * groups,),
            in_specs=acts_in + [anywhere, anywhere],
            out_specs=[seq_block] + [whole(o) for o in outs],
            out_shape=[shape(tokens.shape, BF)] + [shape(o, F32) for o in outs],
            scratch_shapes=scratch,
            compiler_params=pltpu.CompilerParams(
                vmem_limit_bytes=VMEM_LIMIT, collective_id=1, has_side_effects=True
            ),
            name="attention_backward",
        )(*acts, dwu, dwd)
        ends = [shape(tokens.shape, BF)] + [shape(o, F32) for o in outs[:4]]
        vectors = [shape(v, F32) for v in (gains.shape, biases.shape, (1, quarter * rows))]
        vmem = pl.BlockSpec(memory_space=pltpu.VMEM)
        token_grad, gqkv, gout, gup, gdown, ggains, gbiases, gupb = pl.pallas_call(
            finish_kernel,
            in_specs=[anywhere] * 5 + [vmem],
            out_specs=[anywhere] * 5 + [vmem] * 3,
            out_shape=ends + vectors,
            scratch_shapes=[
                pltpu.VMEM((LANES, LANES), F32),
                pltpu.SemaphoreType.DMA((seqs + 4,)),
            ],
            name="hand_over",
        )(*grads)
        return out, token_grad, gqkv, gout, gup, gdown, ggains, gbiases, gupb.reshape(-1)

    token_grad, gqkv, gout, gsmall = pl.pallas_call(
        functools.partial(backward_kernel, (n_dp, n_z), False, groups),
        grid=(3 * groups,),
        in_specs=acts_in,
        out_specs=[seq_block, whole((d, 3 * d)), whole((d, d)), whole((d, LANES))],
        out_shape=[shape(tokens.shape, BF), shape((d, 3 * d), F32), shape((d, d), F32), shape((d, LANES), F32)],
        scratch_shapes=base,
        compiler_params=pltpu.CompilerParams(vmem_limit_bytes=VMEM_LIMIT),
        name="attention_backward",
    )(*acts)

    def scatter(term):
        return lax.psum_scatter(term.astype(F32), axes, scatter_dimension=0, tiled=True)

    up_sums = gsmall[:, 8 : 8 + quarter].reshape(cut, d // cut, quarter).swapaxes(1, 2)
    gsmall = scatter(gsmall[:, :8]).T
    return (
        out,
        token_grad,
        scatter(gqkv),
        scatter(gout),
        scatter(dwu.reshape(d, hidden)),
        scatter(dwd.reshape(hidden, d)),
        gsmall[:2],
        gsmall[2:8],
        scatter(up_sums.reshape(hidden)),
    )


def solution(mesh):
    axes = ("dp", "fsdp")
    rows, cols, flat = P(axes, None), P(None, axes), P(axes)
    data = P(axes, None, None)
    return jax.shard_map(
        functools.partial(per_device, mesh.shape["dp"], mesh.shape["fsdp"]),
        mesh=mesh,
        in_specs=(data, flat, data, rows, rows, rows, rows, cols, cols, flat),
        out_specs=(data, data, rows, rows, rows, rows, cols, cols, flat),
        check_vma=False,
    )
```

time: 250 us -> 301 us (1.20)
  Pallas kernels: 239 us -> 300 us
  local copies, waits for them, and re-layouts: 10.1 us -> 0 us
    pallas_call x3 -> x4, Pallas kernels: 239 us -> 300 us  [the longest x1 110 us: per_device(): pl.pallas_call(finish_kernel, in_specs=[anywhere] * 5 + [vmem], out_specs...]
    unnamed x19 -> x0, local copies, waits for them, and re-layouts: 7.55 us -> none
where the time goes in v2:
time: 301 us
  Pallas kernels  300 us (100%)
    pallas_call x1, Pallas kernels, per_device(): pl.pallas_call(finish_kernel, in_specs=[anywhere] * 5 + [vmem], out_specs...  110 us
    pallas_call x1, Pallas kernels, per_device(): pl.pallas_call(functools.partial(backward_kernel, (n_dp, n_z), True, grou...  65.6 us
    pallas_call x1, Pallas kernels, per_device(): pl.pallas_call(functools.partial(attention_kernel, (n_dp, n_z), True, gro...  65.4 us
    pallas_call x1, Pallas kernels, per_device(): pl.pallas_call(functools.partial(forward_kernel, block=block), grid=(chun...  59.3 us

profile of v2, /device:TPU:0, one launch (start us, length us, event | category | flops | bytes accessed | tf_op | source)
XLA Modules:
  0.0 300.8 jit_solution(6198078557353802709)
XLA Ops:
  0.6 65.4 %attention_forward.1 = (bf16[1536,3072]{1,0:T(8,128)(2,1)}, bf16[12,8,256,256]{3,2,1,0:T(8,128)(2,1)}, bf16[512,3072]{1,0:T(8,128)(2,1)}, f32[512,3072]{1,0:T(8,...) custom-call(s32[12]{0:T(128)} %lengths.1, ...), custom_call_target="tpu_custom_call" | custom-call | tf_op jit(solution)/shard_map/attention_forward/pallas_call | solution.py:744
  66.1 59.3 %feed_forward.1 = (bf16[12,256,512]{2,1,0:T(8,128)(2,1)}, f32[512,3072]{1,0:T(8,128)}, bf16[16,2,16,2048]{3,2,1,0:T(8,128)(2,1)}, bf16[16,2,64,512]{3,2,1,0:T(8,128)(2,1)}, f32[512,128]{1,0:T(8,128)}) custom-call(f32[512,3072]{1,0:T(8,128)} %get-tuple-element.37.r1_first.r1_next, bf16[12,256,512]{2,1,0:T(8,128)(2,1)} %g_next.1, ...), custom_call_target="tpu_custom_call" | custom-call | tf_op jit(solution)/shard_map/feed_forward/pallas_call | solution.py:804
  125.3 65.6 %attention_backward.1 = (bf16[12,256,512]{2,1,0:T(8,128)(2,1)}, f32[16,1536]{1,0:T(8,128)}, f32[16,512]{1,0:T(8,128)}, f32[16,2048]{1,0:T(8,128)}, f32[64,512]{1,0:T(8,128)}, /*index=5*/f32[16,128]{1,0:T(8,128)}) custom-call(f32[512,3072]{1,0:T(8,128)} %get-tuple-element.42.refs_0_, bf16[512,3072]{1,0:T(8,128)(2,1)} %get-tuple-element.43.refs_1_, ...), custom_call_target="tpu_custom_call" | custom-call | tf_op jit(solution)/shard_map/attention_backward/pallas_call | solution.py:892
  190.9 109.7 %hand_over.1 = (bf16[12,256,512]{2,1,0:T(8,128)(2,1)}, f32[16,1536]{1,0:T(8,128)}, f32[16,512]{1,0:T(8,128)}, f32[16,2048]{1,0:T(8,128)}, f32[64,512]{1,0:T(8,12...) custom-call(bf16[12,256,512]{2,1,0:T(8,128)(2,1)} %get-tuple-element.51.tg, ...), custom_call_target="tpu_custom_call" | custom-call | tf_op jit(solution)/shard_map/hand_over/pallas_call | solution.py:907

commit v3 on v2

--- a/solution.py
+++ b/solution.py
@@ -67,26 +67,43 @@
     def dp_peer(self, k):
         return (self.dp_of(k), self.fsdp)
 
-    def greet(self):
+    def others(self):
+        n_fsdp = 2 * self.n_z
+        return [
+            (self.dp_of(m), lax.rem(self.fsdp + k, n_fsdp))
+            for m in range(self.n_dp)
+            for k in range(n_fsdp)
+            if m or k
+        ]
+
+    def greet(self, everyone=False):
         barrier = pltpu.get_barrier_semaphore()
         peers = [self.mate]
         peers += [self.z_peer(k) for k in range(1, self.n_z)]
         peers += [self.dp_peer(k) for k in range(1, self.n_dp)]
+        if everyone:
+            peers = self.others()
         for peer in peers:
             pl.semaphore_signal(barrier, inc=1, device_id=peer, device_id_type=MESH)
         pl.semaphore_wait(barrier, len(peers))
 
 
 class Gather:
-    def __init__(self, place, own, whole, send, recv):
+    def __init__(self, place, own, whole, send, recv, flip=False):
         self.p, self.own, self.whole, self.send, self.recv = place, own, whole, send, recv
-
-    def put(self, src, slot, core, peer, at):
+        p = place
+        by_z = (p.n_z, p.z_peer, lambda near, far: p.dp_of(far) * p.n_z + p.z_of(near))
+        by_dp = (p.n_dp, p.dp_peer, lambda near, far: p.dp_of(near) * p.n_z + p.z_of(far))
+        (self.near, self.near_peer, self.slot), (self.far, self.far_peer, _) = (
+            (by_dp, by_z) if flip else (by_z, by_dp)
+        )
+
+    def put(self, src, slot, peer, at):
         pltpu.make_async_remote_copy(
             src_ref=src,
-            dst_ref=self.whole.at[slot, core],
+            dst_ref=self.whole.at[slot, self.p.core],
             send_sem=self.send.at[at],
-            recv_sem=self.recv.at[slot, core],
+            recv_sem=self.recv.at[slot, self.p.core],
             device_id=peer,
             device_id_type=MESH,
         ).start()
@@ -95,40 +112,37 @@
         there = self.whole.at[slot, core]
         pltpu.make_async_copy(there, there, self.recv.at[slot, core]).wait()
 
+    def far_peers(self):
+        return [self.far_peer(m) for m in range(1, self.far)] + [self.p.mate]
+
     def start(self):
-        p, at = self.p, 0
-        peers = [p.z_peer(k) for k in range(1, p.n_z)]
-        peers += [p.dp_peer(k) for k in range(1, p.n_dp)]
-        for peer in peers + [p.mate]:
-            self.put(self.own, p.slot, p.core, peer, at)
-            at += 1
-
-    def along_z(self):
-        p = self.p
-        at = p.n_z + p.n_dp - 1
-        for k in range(1, p.n_z):
-            slot = p.dp * p.n_z + p.z_of(k)
-            self.landed(slot, p.core)
-            for peer in [p.dp_peer(m) for m in range(1, p.n_dp)] + [p.mate]:
-                self.put(self.whole.at[slot, p.core], slot, p.core, peer, at)
+        peers = [self.near_peer(k) for k in range(1, self.near)] + self.far_peers()
+        for at, peer in enumerate(peers):
+            self.put(self.own, self.p.slot, peer, at)
+
+    def relay(self):
+        at = self.near + self.far - 1
+        for k in range(1, self.near):
+            slot = self.slot(k, 0)
+            self.landed(slot, self.p.core)
+            for peer in self.far_peers():
+                self.put(self.whole.at[slot, self.p.core], slot, peer, at)
                 at += 1
 
-    def over_dp(self):
-        p = self.p
-        at = p.n_z + p.n_dp - 1 + (p.n_z - 1) * p.n_dp
-        for k in range(0, p.n_z):
-            for m in range(1, p.n_dp):
-                slot = p.dp_of(m) * p.n_z + p.z_of(k)
-                self.landed(slot, p.core)
-                self.put(self.whole.at[slot, p.core], slot, p.core, p.mate, at)
+    def share(self):
+        at = self.near + self.far - 1 + (self.near - 1) * self.far
+        for k in range(self.near):
+            for m in range(1, self.far):
+                slot = self.slot(k, m)
+                self.landed(slot, self.p.core)
+                self.put(self.whole.at[slot, self.p.core], slot, self.p.mate, at)
                 at += 1
 
     def finish(self):
-        p = self.p
-        for k in range(0, p.n_z):
-            for m in range(0, p.n_dp):
-                self.landed(p.dp_of(m) * p.n_z + p.z_of(k), 1 - p.core)
-        for at in range(self.sends(p.n_dp, p.n_z)):
+        for k in range(self.near):
+            for m in range(self.far):
+                self.landed(self.slot(k, m), 1 - self.p.core)
+        for at in range(self.sends(self.p.n_dp, self.p.n_z)):
             pltpu.make_async_copy(self.own, self.own, self.send.at[at]).wait()
 
     @staticmethod
@@ -140,14 +154,15 @@
     n_dp, n_z = mesh_sizes
     if gathers:
         (qkv_s, wo_s, wu_s, wd_s, gains_s, biases_s, upb_s,
-         qkv_ref, probs_ref, ct_ref, r1_ref, a1_ref, early_ref, wo_ref, wu_ref, wd_ref,
-         wqkv_t, wo_t, xt_s, normed_s, early, wo, early_own, wo_own, wu_own, wd_own, small, sems, rems, local) = refs
+         qkv_ref, probs_ref, ct_ref, r1_ref, a1_ref, early_ref, late_ref, wo_ref, wu_ref, wd_ref,
+         wqkv_t, wo_t, xt_s, normed_s, a1_s, ct_s, early, late, wo,
+         early_own, late_own, wo_own, wu_own, wd_own, small, sems, rems, local) = refs
     else:
-        (early_in, wo_in,
+        (early_in, late_in, wo_in,
          qkv_ref, probs_ref, ct_ref, r1_ref, a1_ref,
-         wqkv_t, wo_t, xt_s, normed_s, early, wo) = refs
+         wqkv_t, wo_t, xt_s, normed_s, a1_s, ct_s, early, late, wo) = refs
     step = pl.program_id(0)
-    group = lax.rem(step, groups)
+    stage, group = step // groups, lax.rem(step, groups)
     many, seq, d = x_ref.shape
     half = d // 2
     head = d // HEADS
@@ -156,46 +171,45 @@
     if gathers:
         place = Place(n_dp, n_z)
         first = Gather(place, early_own, early, sems.at[0], rems.at[0])
-        out = Gather(place, wo_own, wo, sems.at[1], rems.at[1])
-        up = Gather(place, wu_own, wu_ref, sems.at[2], rems.at[2])
-        down = Gather(place, wd_own, wd_ref, sems.at[3], rems.at[3])
+        second = Gather(place, late_own, late, sems.at[1], rems.at[1])
+        out = Gather(place, wo_own, wo, sems.at[2], rems.at[2])
+        up = Gather(place, wu_own, wu_ref, sems.at[3], rems.at[3])
+        cut = wd_own.shape[0] // 2
+        down = Gather(place, wd_own.at[:cut], wd_ref.at[:, :, :cut], sems.at[4], rems.at[4])
+        down2 = Gather(place, wd_own.at[cut:], wd_ref.at[:, :, cut:], sems.at[5], rems.at[5], flip=True)
         here = (place.slot, place.core)
         copies = [
             pltpu.make_async_copy(wu_own, wu_ref.at[here], local.at[0]),
             pltpu.make_async_copy(wd_own, wd_ref.at[here], local.at[1]),
             pltpu.make_async_copy(early, early_ref, local.at[2]),
-            pltpu.make_async_copy(wo, wo_ref, local.at[3]),
+            pltpu.make_async_copy(late, late_ref, local.at[3]),
+            pltpu.make_async_copy(wo, wo_ref, local.at[4]),
         ]
 
-        @pl.when(step == 0)
-        def _():
+        def enter():
             rows = qkv_s.shape[0]
             small[...] = jnp.zeros_like(small)
             small[0:2, :rows] = gains_s[...]
             small[2:8, :rows] = biases_s[...]
             for r in range(upb_s.shape[1] // rows):
                 small[8 + r : 9 + r, :rows] = upb_s[:, r * rows : (r + 1) * rows]
-            early_own[:, : 3 * d] = qkv_s[...].astype(BF)
-            early_own[:, 3 * d :] = small[...].T[:rows].astype(BF)
+            for part in range(3):
+                at = part * d
+                early_own[:, part * half : (part + 1) * half] = qkv_s[:, at : at + half].astype(BF)
+                late_own[:, part * half : (part + 1) * half] = qkv_s[:, at + half : at + d].astype(BF)
+            early_own[:, 3 * half :] = small[...].T[:rows].astype(BF)
             place.greet()
             first.start()
             wo_own[...] = wo_s[...].astype(BF)
-            out.start()
-            early[here] = early_own[...]
-            wo[here] = wo_own[...]
             wu_own[...] = wu_s[...].astype(BF)
             wd_own[...] = wd_s[...].astype(BF)
+            early[here] = early_own[...]
+            late[here] = late_own[...]
+            wo[here] = wo_own[...]
             for copy in copies[:2]:
                 copy.start()
 
-        plan = {
-            1: [first.along_z, out.along_z],
-            2: [first.over_dp, out.over_dp],
-            3: [up.start, down.start],
-            4: [first.finish, out.finish, copies[2].start, copies[3].start],
-            5: [up.along_z, down.along_z],
-            6: [up.over_dp, down.over_dp],
-        }
+        plan = plan_forward(groups, enter, first, second, out, up, down, down2, copies)
         for at, actions in plan.items():
 
             @pl.when(step == at)
@@ -208,19 +222,13 @@
         @pl.when(step == 0)
         def _():
             early[...] = early_in[...].reshape(early.shape)
+            late[...] = late_in[...].reshape(late.shape)
             wo[...] = wo_in[...].reshape(wo.shape)
 
-    @pl.when(step == groups)
-    def _():
-        whole = early[...].reshape(d, 3 * d + LANES)
-        for hb in range(2):
-            for part in range(3):
-                to = (hb * 3 + part) * half
-                at = part * d + hb * half
-                wqkv_t[to : to + half] = whole[:, at : at + half].T
-        wo_t[...] = wo[...].reshape(d, d).T
-
-    @pl.when(step < groups)
+    def columns():
+        return early[..., 3 * half :].reshape(d, LANES).astype(F32)
+
+    @pl.when(stage == 0)
     def _():
         for s in range(many):
             xt = x_ref[s].T
@@ -228,25 +236,35 @@
             normed, _ = normalize(xt.astype(F32))
             normed_s[group, :, seq * s : seq * (s + 1)] = normed
 
-    @pl.when(step >= groups)
+    @pl.when(step == groups)
     def _():
-        column = early[..., 3 * d :].reshape(d, LANES).astype(F32)
+        wqkv_t[...] = early[..., : 3 * half].reshape(d, 3 * half).T
+
+    @pl.when(step == 2 * groups)
+    def _():
+        wqkv_t[...] = late[...].reshape(d, 3 * half).T
+        wo_t[...] = wo[...].reshape(d, d).T
+
+    @pl.when(stage == 1)
+    def _():
+        column = columns()
         a1 = (normed_s[group] * column[:, 0:1] + column[:, 2:3]).astype(BF)
+        a1_s[group] = a1
         a1_ref[...] = a1
-        for hb in range(2):
-            at, rows = hb * 3 * half, slice(hb * half, (hb + 1) * half)
-            query = (dot(wqkv_t[at : at + half], a1) + column[rows, 3:4]).astype(BF)
-            qkv_ref[at : at + half] = (query.astype(F32) * scale).astype(BF)
-            at += half
-            qkv_ref[at : at + half] = dot(wqkv_t[at : at + half], a1).astype(BF)
-            at += half
-            qkv_ref[at : at + half] = (dot(wqkv_t[at : at + half], a1) + column[rows, 4:5]).astype(BF)
+
+    def heads(hb):
+        column = columns()
+        rows = slice(hb * half, (hb + 1) * half)
+        query = (dot(wqkv_t[:half], a1_s[group]) + column[rows, 3:4]).astype(BF)
+        qkv_ref[:half] = (query.astype(F32) * scale).astype(BF)
+        qkv_ref[half : 2 * half] = dot(wqkv_t[half : 2 * half], a1_s[group]).astype(BF)
+        qkv_ref[2 * half :] = (dot(wqkv_t[2 * half :], a1_s[group]) + column[rows, 4:5]).astype(BF)
         row = lax.broadcasted_iota(jnp.int32, (seq, seq), 0)
         valid = [row < lengths[group * many + s] for s in range(many)]
-        items = [(s, h) for s in range(many) for h in range(HEADS)]
+        items = [(s, h) for s in range(many) for h in range(HEADS // 2)]
 
         def place_of(s, h, part):
-            at = (h // (HEADS // 2) * 3 + part) * half + h % (HEADS // 2) * head
+            at = part * half + h * head
             return slice(at, at + head), slice(seq * s, seq * (s + 1))
 
         def score(s, h):
@@ -259,36 +277,52 @@
 
         def mix(s, h, probs):
             probs_ref[s, h] = probs
-            ct_ref[h * head : (h + 1) * head, seq * s : seq * (s + 1)] = dot(
-                qkv_ref[place_of(s, h, 2)], probs
-            ).astype(BF)
+            ct_ref[place_of(s, h, 0)] = dot(qkv_ref[place_of(s, h, 2)], probs).astype(BF)
 
         def attended(s):
             at = slice(seq * s, seq * (s + 1))
-            r1_ref[:, at] = (
-                xt_s[group, :, at].astype(F32) + dot(wo_t[...], ct_ref[:, at]) + column[:, 5:6]
-            )
+            term = dot(wo_t[:, :half], ct_s[group, :, at]) + dot(wo_t[:, half:], ct_ref[:, at])
+            r1_ref[:, at] = xt_s[group, :, at].astype(F32) + term + column[:, 5:6]
 
         scores, probs = score(*items[0]), None
         for at, (s, h) in enumerate(items):
             ahead = score(*items[at + 1]) if at + 1 < len(items) else None
             if at:
                 mix(*items[at - 1], probs)
-            if s and h == 2:
+            if hb and s and h == 1:
                 attended(s - 1)
             probs, scores = soften(s, scores), ahead
         mix(*items[-1], probs)
-
-        attended(many - 1)
+        if hb:
+            attended(many - 1)
+        else:
+            ct_s[group] = ct_ref[...]
+
+    pl.when(stage == 1)(lambda: heads(0))
+    pl.when(stage == 2)(lambda: heads(1))
 
     if gathers:
 
-        @pl.when(step == 2 * groups - 1)
+        @pl.when(step == 3 * groups - 1)
         def _():
-            up.finish()
-            down.finish()
+            for each in (up, down, down2):
+                each.finish()
             for copy in copies:
                 copy.wait()
+
+
+def plan_forward(groups, enter, first, second, out, up, down, down2, copies):
+    return {
+        0: [enter],
+        1: [second.start, out.start],
+        2: [first.relay],
+        3: [first.share, up.start, down.start, down2.start],
+        4: [first.finish, copies[2].start, second.relay, out.relay],
+        5: [up.relay, second.share, out.share],
+        6: [down2.relay, down.relay],
+        8: [second.finish, out.finish, copies[3].start, copies[4].start, up.share],
+        9: [down2.share, down.share],
+    }
 
 
 def forward_kernel(
@@ -320,8 +354,6 @@
     def _():
         wu_t[...] = wu_ref[...].T
         wd_t[...] = wd_ref[...].T
-        total_wu[...] = jnp.zeros_like(total_wu)
-        total_wd[...] = jnp.zeros_like(total_wd)
         sums[...] = jnp.zeros_like(sums)
         sums_up[...] = jnp.zeros_like(sums_up)
         for r in range(hidden // d):
@@ -357,8 +389,10 @@
         total_a2[...] = term if j == 0 else total_a2[...] + term
 
     def weights(j):
-        total_wd[span(j)] += dot(h_s[j], gt[...], NT)
-        total_wu[:, span(j)] += dot(a2[...], du_s[j], NT)
+        term = dot(h_s[j], gt[...], NT)
+        total_wd[span(j)] = jnp.where(step == 0, term, total_wd[span(j)] + term)
+        term = dot(a2[...], du_s[j], NT)
+        total_wu[:, span(j)] = jnp.where(step == 0, term, total_wu[:, span(j)] + term)
 
     def close():
         for s in range(seqs):
@@ -402,25 +436,32 @@
 
 
 class Scatter:
-    def __init__(self, place, part, result, bufs, send, recv):
+    def __init__(self, place, part, result, bufs, send, recv, flip=False):
         self.p, self.part, self.result = place, part, result
         self.mine, self.got1, self.sum1, self.got2, self.sum2, self.got3 = bufs
         self.send, self.recv = send, recv
+        p = place
+        by_z = (p.n_z, p.z_peer, lambda far, near: p.dp_of(near) * p.n_z + p.z_of(far))
+        by_dp = (p.n_dp, p.dp_peer, lambda far, near: p.dp_of(far) * p.n_z + p.z_of(near))
+        (self.far, self.far_peer, self.slot), (self.near, self.near_peer, _) = (
+            (by_z, by_dp) if flip else (by_dp, by_z)
+        )
 
     @staticmethod
-    def scratch(n_dp, n_z, rows, width, kind):
+    def scratch(n_dp, n_z, rows, width, kind, flip=False):
+        far, near = (n_z, n_dp) if flip else (n_dp, n_z)
         return [
             pltpu.VMEM((n_dp * n_z, rows, width), kind),
             pltpu.VMEM((n_dp * n_z, rows, width), kind),
             pltpu.VMEM((n_dp * n_z, rows, width), kind),
-            pltpu.VMEM((n_dp - 1, n_z, rows, width), kind),
-            pltpu.VMEM((n_z, rows, width), kind),
-            pltpu.VMEM((n_z - 1, rows, width), kind),
+            pltpu.VMEM((far - 1, near, rows, width), kind),
+            pltpu.VMEM((near, rows, width), kind),
+            pltpu.VMEM((near - 1, rows, width), kind),
         ]
 
     @staticmethod
     def sems(n_dp, n_z):
-        return n_dp + n_z
+        return 2 + (max(n_dp, n_z) - 1) * max(n_dp, n_z) + max(n_dp, n_z) - 1
 
     def copy(self, src, dst, at, peer):
         return pltpu.make_async_remote_copy(
@@ -437,27 +478,29 @@
         return self.copy(self.part.at[:, 1 - p.core], self.got1, 0, p.mate)
 
     def own(self):
-        p = self.p
-        return pltpu.make_async_copy(
-            self.part.at[:, p.core], self.mine, self.send.at[p.n_dp + p.n_z - 1]
-        )
-
-    def over_dp(self):
-        p = self.p
+        return pltpu.make_async_copy(self.part.at[:, self.p.core], self.mine, self.send.at[1])
+
+    def afar(self):
         return [
             self.copy(
-                self.sum1.at[pl.ds(p.dp_of(k) * p.n_z, p.n_z)], self.got2.at[k - 1], k, p.dp_peer(k)
+                self.sum1.at[self.slot(k, m)],
+                self.got2.at[k - 1, m],
+                2 + (k - 1) * self.near + m,
+                self.far_peer(k),
             )
-            for k in range(1, p.n_dp)
+            for k in range(1, self.far)
+            for m in range(self.near)
         ]
 
-    def along_z(self):
-        p = self.p
+    def nearby(self):
         return [
             self.copy(
-                self.sum2.at[p.z_of(k)], self.got3.at[k - 1], p.n_dp - 1 + k, p.z_peer(k)
+                self.sum2.at[m],
+                self.got3.at[m - 1],
+                2 + (self.far - 1) * self.near + m - 1,
+                self.near_peer(m),
             )
-            for k in range(1, p.n_z)
+            for m in range(1, self.near)
         ]
 
     def step1(self):
@@ -475,43 +518,39 @@
             return 0
 
         lax.fori_loop(0, self.p.n_dp * self.p.n_z, add, 0)
-        for copy in self.over_dp():
+        for copy in self.afar():
             copy.start()
 
     def step3(self):
-        for copy in self.over_dp():
+        for copy in self.afar():
             copy.wait()
-
-        def add(s, _):
-            total = self.sum1[self.p.dp * self.p.n_z + s].astype(F32)
-            for k in range(self.p.n_dp - 1):
-                total = total + self.got2[k, s].astype(F32)
-            self.sum2[s] = total.astype(self.sum2.dtype)
-            return 0
-
-        lax.fori_loop(0, self.p.n_z, add, 0)
-        for copy in self.along_z():
+        for m in range(self.near):
+            total = self.sum1[self.slot(0, m)].astype(F32)
+            for k in range(self.far - 1):
+                total = total + self.got2[k, m].astype(F32)
+            self.sum2[m] = total.astype(self.sum2.dtype)
+        for copy in self.nearby():
             copy.start()
 
     def step4(self):
-        for copy in self.along_z():
+        for copy in self.nearby():
             copy.wait()
-        total = self.sum2[self.p.z].astype(F32)
-        for k in range(self.p.n_z - 1):
-            total = total + self.got3[k].astype(F32)
+        total = self.sum2[0].astype(F32)
+        for m in range(self.near - 1):
+            total = total + self.got3[m].astype(F32)
         self.result[...] = total
 
 
 def backward_kernel(mesh_sizes, scatters, groups, *refs):
     n_dp, n_z = mesh_sizes
-    (dr1_ref, ct_ref, qkv_ref, probs_ref, a1_ref, x_ref, early_ref, wo_ref, part_ref) = refs[:9]
-    refs = refs[9:]
+    (dr1_ref, ct_ref, qkv_ref, probs_ref, a1_ref, x_ref, early_ref, late_ref, wo_ref, part_ref) = refs[:10]
+    refs = refs[10:]
     if scatters:
         (dwu_ref, dwd_ref, tg_ref, gqkv_ref, gout_ref, gup_ref, gdown_ref, gsmall_ref,
-         dp_s, wqkv, total_qkv, total_out, dc_s, sums, part_qkv, part_out, part_small, gqkv_half) = refs[:18]
-        buffers, (send, recv) = refs[18:-2], refs[-2:]
+         dp_s, total_qkv, total_out, dc_s, sums, part_qkv, part_out, part_small, got_small, gqkv_half) = refs[:18]
+        buffers, (send, recv, small_send, small_recv) = refs[18:-4], refs[-4:]
     else:
-        (tg_ref, gqkv_ref, gout_ref, gsmall_ref, dp_s, wqkv, total_qkv, total_out, dc_s, sums) = refs
+        tg_ref, gqkv_ref, gout_ref, gsmall_ref, dp_s, total_qkv, total_out, dc_s, sums = refs
     step = pl.program_id(0)
     last = pl.num_programs(0) - 1
     stage, group = step // groups, lax.rem(step, groups)
@@ -519,30 +558,26 @@
     many, seq = x_ref.shape[:2]
     half, head = d // 2, d // HEADS
     scale = head**-0.5
-    column = early_ref[:, 3 * d :].astype(F32)
+    column = early_ref[:, 3 * half :].astype(F32)
 
     @pl.when(step == 0)
     def _():
         sums[...] = jnp.zeros_like(sums)
-        for hb in range(2):
-            for part in range(3):
-                at = part * d + hb * half
-                wqkv[hb, :, part * half : (part + 1) * half] = early_ref[:, at : at + half]
 
     if scatters:
         place = Place(n_dp, n_z)
-        down, up, qkv0, qkv1, out, small_piece = [
-            Scatter(place, part, result, buffers[6 * i : 6 * i + 6], send.at[i], recv.at[i])
-            for i, (part, result) in enumerate(
-                (
-                    (dwd_ref, gdown_ref),
-                    (dwu_ref, gup_ref),
-                    (part_qkv.at[0], gqkv_half.at[0]),
-                    (part_qkv.at[1], gqkv_half.at[1]),
-                    (part_out, gout_ref),
-                    (part_small, gsmall_ref),
-                )
-            )
+        cut = dwd_ref.shape[2] // 2
+        parts = (
+            (dwu_ref, gup_ref, False),
+            (dwd_ref.at[:, :, :cut], gdown_ref.at[:cut], False),
+            (dwd_ref.at[:, :, cut:], gdown_ref.at[cut:], True),
+            (part_qkv.at[0], gqkv_half.at[0], False),
+            (part_qkv.at[1], gqkv_half.at[1], False),
+            (part_out, gout_ref, False),
+        )
+        up, down, down2, qkv0, qkv1, out = [
+            Scatter(place, part, result, buffers[6 * i : 6 * i + 6], send.at[i], recv.at[i], flip)
+            for i, (part, result, flip) in enumerate(parts)
         ]
 
         def pack(hb):
@@ -551,18 +586,10 @@
         def pack_out():
             part_out[...] = total_out[...].astype(BF).reshape(part_out.shape)
 
-        plan = {
-            0: [place.greet, down.step1, up.step1],
-            1: [down.step2],
-            2: [up.step2],
-            4: [lambda: pack(0), qkv0.step1],
-            5: [qkv0.step2, down.step3],
-            7: [up.step3],
-            8: [lambda: pack(1), qkv1.step1, pack_out, out.step1, down.step4],
-            9: [qkv1.step2, out.step2, qkv0.step3],
-            10: [up.step4],
-            11: [qkv0.step4, qkv1.step3, out.step3],
-        }
+        plan = plan_backward(
+            lambda: place.greet(True), up, down, down2, qkv0, qkv1, out,
+            lambda: pack(0), lambda: pack(1), pack_out,
+        )
         for at, actions in plan.items():
 
             @pl.when(step == at)
@@ -586,8 +613,10 @@
             return dot(qkv_ref[place_of(s, h, 2)], dc_s[place_of(s, h, 0)], TN)
 
         def grad_scores(s, h, term):
-            at = place_of(s, h, 0)
-            delta = jnp.sum(dc_s[at].astype(F32) * ct_ref[at].astype(F32), 0, keepdims=True)
+            rows, at = place_of(s, h, 0)
+            there = pl.ds(pl.multiple_of(stage * half + h * head, head), head)
+            delta = dc_s[rows, at].astype(F32) * ct_ref[there, at].astype(F32)
+            delta = jnp.sum(delta, 0, keepdims=True)
             return (probs_ref[s, h].astype(F32) * (term - delta)).astype(BF)
 
         def finish(s, h, ds):
@@ -603,8 +632,12 @@
                 finish(*items[at - 1], ds)
             ds, term = grad_scores(*item, term), ahead
         opening = group == 0
-        term = dot(ct_ref[...], do, NT)
-        total_out[mine, :] = jnp.where(opening, term, total_out[mine, :] + term)
+
+        @pl.when(stage == 0)
+        def _():
+            term = dot(ct_ref[...], dr1_ref[...].astype(BF), NT)
+            total_out[...] = jnp.where(opening, term, total_out[...] + term)
+
         finish(*items[-1], ds)
         term = dot(a1_ref[...], to[...], NT)
         total_qkv[stage] = jnp.where(opening, term, total_qkv[stage] + term)
@@ -616,7 +649,9 @@
     def _():
         def product(s):
             at = slice(seq * s, seq * (s + 1))
-            return dot(wqkv[0], dp_s[0, group, :, at]) + dot(wqkv[1], dp_s[1, group, :, at])
+            return dot(early_ref[:, : 3 * half], dp_s[0, group, :, at]) + dot(
+                late_ref[...], dp_s[1, group, :, at]
+            )
 
         def finish(s, da1):
             normed, inverse = normalize(x_ref[s].T.astype(F32))
@@ -646,38 +681,62 @@
             gsmall_ref[...] = small
             return
         part_small[...] = small.reshape(part_small.shape)
-        small_piece.step1()
+
+        def exchange(at, peer):
+            dp, fsdp = peer
+            return pltpu.make_async_remote_copy(
+                src_ref=part_small.at[dp * n_z + fsdp // 2, fsdp % 2],
+                dst_ref=got_small.at[at],
+                send_sem=small_send.at[at],
+                recv_sem=small_recv.at[at],
+                device_id=peer,
+                device_id_type=MESH,
+            )
+
+        swaps = [exchange(at, peer) for at, peer in enumerate(place.others())]
+        for swap in swaps:
+            swap.start()
         qkv1.step4()
-        small_piece.step2()
-        out.step4()
-        small_piece.step3()
         for hb in range(2):
             for part in range(3):
                 at = part * d + hb * half
                 gqkv_ref[:, at : at + half] = gqkv_half[hb, :, part * half : (part + 1) * half]
-        small_piece.step4()
-
-
-def finish_kernel(tg, qkv, out, up, down, small, tg_to, qkv_to, out_to, up_to, down_to, gains, biases, upb, turn, sems):
-    copies = [
-        pltpu.make_async_copy(tg.at[s], tg_to.at[s], sems.at[s]) for s in range(tg.shape[0])
-    ]
-    pairs = ((qkv, qkv_to), (out, out_to), (up, up_to), (down, down_to))
-    copies += [
-        pltpu.make_async_copy(a, b, sems.at[tg.shape[0] + i]) for i, (a, b) in enumerate(pairs)
-    ]
-    for copy in copies:
-        copy.start()
-    rows = small.shape[0]
-    turn[...] = jnp.zeros_like(turn)
-    turn[:rows] = small[...]
-    turned = turn[...].T
-    gains[...] = turned[0:2, :rows]
-    biases[...] = turned[2:8, :rows]
-    for r in range(upb.shape[1] // rows):
-        upb[:, r * rows : (r + 1) * rows] = turned[8 + r : 9 + r, :rows]
-    for copy in copies:
-        copy.wait()
+        total = part_small[place.slot, place.core]
+        for at, swap in enumerate(swaps):
+            swap.wait()
+            total = total + got_small[at]
+        gsmall_ref[...] = total
+
+
+def plan_backward(greet, up, down, down2, qkv0, qkv1, out, pack0, pack1, pack_out):
+    return {
+        0: [greet, up.step1, down2.step1, down.step1],
+        1: [up.step2, down2.step2, down.step2],
+        4: [pack0, qkv0.step1, pack_out, out.step1],
+        5: [up.step3, down2.step3, qkv0.step2, out.step2],
+        7: [down.step3],
+        8: [pack1, qkv1.step1, up.step4, down2.step4],
+        9: [qkv1.step2, qkv0.step3, out.step3],
+        10: [down.step4],
+        11: [qkv1.step3, qkv0.step4, out.step4],
+    }
+
+
+def finish_kernel(tg, qkv, out, up, down, small, tg_to, qkv_to, out_to, up_to, down_to, gains, biases, upb, turn):
+    tg_to[...] = tg[...]
+
+    @pl.when(pl.program_id(0) == 0)
+    def _():
+        for source, to in ((qkv, qkv_to), (out, out_to), (up, up_to), (down, down_to)):
+            to[...] = source[...]
+        rows = small.shape[0]
+        turn[...] = jnp.zeros_like(turn)
+        turn[:rows] = small[...]
+        turned = turn[...].T
+        gains[...] = turned[0:2, :rows]
+        biases[...] = turned[2:8, :rows]
+        for r in range(upb.shape[1] // rows):
+            upb[:, r * rows : (r + 1) * rows] = turned[8 + r : 9 + r, :rows]
 
 
 def per_device(n_dp, n_fsdp, tokens, lengths, cotangent, qkv_w, out_w, up_w, down_w, gains, biases, up_bias):
@@ -688,7 +747,7 @@
     half = d // 2
     slots = n_dp * n_z
     count = seqs * seq
-    wide = 3 * d + LANES
+    wide = 3 * half + LANES
     axes = ("dp", "fsdp")
     direct = rows % 16 == 0
     cut = n_dev if direct else 32
@@ -705,21 +764,27 @@
     anywhere = pl.BlockSpec(memory_space=pl.ANY)
     smem = pl.BlockSpec(memory_space=pltpu.SMEM)
 
+    def turn(i):
+        return lax.rem(i, groups)
+
     def norms(i):
         return jnp.minimum(i, groups - 1)
 
     def heads(i):
-        return jnp.maximum(i - groups, 0)
-
-    def lanes(height):
-        return pl.BlockSpec((height, width), lambda i: (0, heads(i)))
+        return jnp.where(i < groups, 0, turn(i))
+
+    def side(i):
+        return jnp.maximum(i // groups - 1, 0)
+
+    def once(i, stage):
+        return jnp.clip(i - stage * groups, 0, groups - 1)
 
     acts_specs = [
-        lanes(3 * d),
-        pl.BlockSpec((many, HEADS, seq, seq), lambda i: (heads(i), 0, 0, 0)),
-        lanes(d),
-        lanes(d),
-        lanes(d),
+        pl.BlockSpec((3 * half, width), lambda i: (side(i), heads(i))),
+        pl.BlockSpec((many, HEADS // 2, seq, seq), lambda i: (heads(i), side(i), 0, 0)),
+        pl.BlockSpec((half, width), lambda i: (side(i), heads(i))),
+        pl.BlockSpec((d, width), lambda i: (0, once(i, 2))),
+        pl.BlockSpec((d, width), lambda i: (0, once(i, 1))),
     ]
     acts_shapes = [
         shape((3 * d, count), BF),
@@ -731,24 +796,28 @@
     in_specs = [smem, pl.BlockSpec((many, seq, d), lambda i: (norms(i), 0, 0))]
     grid_shape = (slots, 2, rows) if direct else (d,)
     scratch = [
-        pltpu.VMEM((3 * d, d), BF),
+        pltpu.VMEM((3 * half, d), BF),
         pltpu.VMEM((d, d), BF),
         pltpu.VMEM((groups, d, width), BF),
         pltpu.VMEM((groups, d, width), F32),
+        pltpu.VMEM((groups, d, width), BF),
+        pltpu.VMEM((groups, half, width), BF),
         pltpu.VMEM((*grid_shape, wide), BF),
+        pltpu.VMEM((*grid_shape, 3 * half), BF),
         pltpu.VMEM((*grid_shape, d), BF),
     ]
     if direct:
         n_sends = Gather.sends(n_dp, n_z)
         shards = (qkv_w, out_w, up_w, down_w, gains, biases, up_bias.reshape(1, -1))
-        qkv, probs, ct, r1, a1, early, wo, wu, wd = pl.pallas_call(
+        qkv, probs, ct, r1, a1, early, late, wo, wu, wd = pl.pallas_call(
             functools.partial(attention_kernel, (n_dp, n_z), True, groups),
-            grid=(2 * groups,),
+            grid=(3 * groups,),
             in_specs=in_specs + [whole(s.shape) for s in shards],
-            out_specs=acts_specs + [anywhere] * 4,
+            out_specs=acts_specs + [anywhere] * 5,
             out_shape=acts_shapes
             + [
                 shape((slots, 2, rows, wide), BF),
+                shape((slots, 2, rows, 3 * half), BF),
                 shape((slots, 2, rows, d), BF),
                 shape((slots, 2, rows, hidden), BF),
                 shape((slots, 2, rows_down, d), BF),
@@ -756,24 +825,31 @@
             scratch_shapes=scratch
             + [
                 pltpu.VMEM((rows, wide), BF),
+                pltpu.VMEM((rows, 3 * half), BF),
                 pltpu.VMEM((rows, d), BF),
                 pltpu.VMEM((rows, hidden), BF),
                 pltpu.VMEM((rows_down, d), BF),
                 pltpu.VMEM((LANES, LANES), F32),
-                pltpu.SemaphoreType.DMA((4, n_sends)),
-                pltpu.SemaphoreType.DMA((4, slots, 2)),
-                pltpu.SemaphoreType.DMA((4,)),
+                pltpu.SemaphoreType.DMA((6, n_sends)),
+                pltpu.SemaphoreType.DMA((6, slots, 2)),
+                pltpu.SemaphoreType.DMA((5,)),
             ],
             compiler_params=pltpu.CompilerParams(
                 vmem_limit_bytes=VMEM_LIMIT, collective_id=0, has_side_effects=True
             ),
             name="attention_forward",
         )(lengths, tokens, *shards)
-        early, wo = early.reshape(d, wide), wo.reshape(d, d)
+        early, late = early.reshape(d, wide), late.reshape(d, 3 * half)
+        wo = wo.reshape(d, d)
         wu, wd = wu.reshape(d, hidden), wd.reshape(hidden, d)
     else:
-        early = jnp.concatenate([qkv_w, gains.T, biases.T], 1).astype(BF)
+        sides = [
+            jnp.concatenate([qkv_w[:, p * d + hb * half :][:, :half] for p in range(3)], 1)
+            for hb in range(2)
+        ]
+        early = jnp.concatenate([sides[0], gains.T, biases.T], 1).astype(BF)
         early = lax.all_gather(early, axes, axis=0, tiled=True)
+        late = lax.all_gather(sides[1].astype(BF), axes, axis=0, tiled=True)
         up_all = lax.all_gather(up_bias.astype(BF), axes, axis=0, tiled=True)
         up_all = up_all.reshape(cut, quarter, d // cut).swapaxes(1, 2).reshape(d, quarter)
         early = jnp.concatenate([early, up_all], 1)
@@ -783,20 +859,20 @@
         wd = lax.all_gather(down_w.astype(BF), axes, axis=0, tiled=True)
         qkv, probs, ct, r1, a1 = pl.pallas_call(
             functools.partial(attention_kernel, (n_dp, n_z), False, groups),
-            grid=(2 * groups,),
-            in_specs=in_specs + [whole(early.shape), whole(wo.shape)],
+            grid=(3 * groups,),
+            in_specs=in_specs + [whole(early.shape), whole(late.shape), whole(wo.shape)],
             out_specs=acts_specs,
             out_shape=acts_shapes,
             scratch_shapes=scratch,
             compiler_params=pltpu.CompilerParams(vmem_limit_bytes=VMEM_LIMIT),
             name="attention_forward",
-        )(lengths, tokens, early, wo)
+        )(lengths, tokens, early, late, wo)
 
     pair = 2 if seqs % 2 == 0 else 1
     chunk = pair * seq
     chunks = seqs // pair
     block = d
-    tail = 3 * d // LANES
+    tail = 3 * half // LANES
 
     def following(i):
         return jnp.minimum(i + 1, chunks - 1)
@@ -843,52 +919,51 @@
         name="feed_forward",
     )(r1, cotangent, r1, cotangent, early, wu, wd)
 
-    def turn(i):
-        return lax.rem(i, groups)
-
     def hold(i):
         return jnp.where(i < 2 * groups, turn(i), groups - 1)
 
-    def side(i):
+    def back_side(i):
         return jnp.minimum(i // groups, 1)
 
-    def late(i):
+    def closing(i):
         return jnp.where(i < 2 * groups, 0, turn(i))
 
-    seq_block = pl.BlockSpec((many, seq, d), lambda i: (late(i), 0, 0))
+    seq_block = pl.BlockSpec((many, seq, d), lambda i: (closing(i), 0, 0))
     acts_in = [
         pl.BlockSpec((d, width), lambda i: (0, turn(i))),
-        pl.BlockSpec((half, width), lambda i: (side(i), hold(i))),
-        pl.BlockSpec((3 * half, width), lambda i: (side(i), hold(i))),
-        pl.BlockSpec((many, HEADS // 2, seq, seq), lambda i: (hold(i), side(i), 0, 0)),
+        pl.BlockSpec((d, width), lambda i: (0, hold(i))),
+        pl.BlockSpec((3 * half, width), lambda i: (back_side(i), hold(i))),
+        pl.BlockSpec((many, HEADS // 2, seq, seq), lambda i: (hold(i), back_side(i), 0, 0)),
         pl.BlockSpec((d, width), lambda i: (0, hold(i))),
         seq_block,
         whole((d, wide)),
+        whole((d, 3 * half)),
         whole((d, d)),
         whole((d, LANES)),
     ]
     base = [
         pltpu.VMEM((2, groups, 3 * half, width), BF),
-        pltpu.VMEM((2, d, 3 * half), BF),
         pltpu.VMEM((2, d, 3 * half), F32),
         pltpu.VMEM((d, d), F32),
         pltpu.VMEM((half, width), BF),
         pltpu.VMEM((5, d, LANES), F32),
     ]
-    acts = (dr1, ct, qkv, probs, a1, tokens, early, wo, small)
+    acts = (dr1, ct, qkv, probs, a1, tokens, early, late, wo, small)
     if direct:
         n_sems = Scatter.sems(n_dp, n_z)
-        plan = ((rows_down, d, BF), (rows, hidden, BF), (rows, 3 * half, BF), (rows, 3 * half, BF), (rows, d, BF), (rows, LANES, F32))
+        plan = ((rows, hidden, False), (rows_down // 2, d, False), (rows_down // 2, d, True), (rows, 3 * half, False), (rows, 3 * half, False), (rows, d, False))
         outs = [(rows, 3 * d), (rows, d), (rows, hidden), (rows_down, d), (rows, LANES)]
         scratch = base + [
             pltpu.VMEM((2, slots, 2, rows, 3 * half), BF),
             pltpu.VMEM((slots, 2, rows, d), BF),
             pltpu.VMEM((slots, 2, rows, LANES), F32),
+            pltpu.VMEM((n_dev - 1, rows, LANES), F32),
             pltpu.VMEM((2, rows, 3 * half), F32),
         ]
-        for height, across, kind in plan:
-            scratch += Scatter.scratch(n_dp, n_z, height, across, kind)
+        for height, across, flip in plan:
+            scratch += Scatter.scratch(n_dp, n_z, height, across, BF, flip)
         scratch += [pltpu.SemaphoreType.DMA((len(plan), n_sems))] * 2
+        scratch += [pltpu.SemaphoreType.DMA((n_dev - 1,))] * 2
         grads = pl.pallas_call(
             functools.partial(backward_kernel, (n_dp, n_z), True, groups),
             grid=(3 * groups,),
@@ -903,16 +978,15 @@
         )(*acts, dwu, dwd)
         ends = [shape(tokens.shape, BF)] + [shape(o, F32) for o in outs[:4]]
         vectors = [shape(v, F32) for v in (gains.shape, biases.shape, (1, quarter * rows))]
-        vmem = pl.BlockSpec(memory_space=pltpu.VMEM)
+        seq_block = pl.BlockSpec((many, seq, d), lambda i: (i, 0, 0))
         token_grad, gqkv, gout, gup, gdown, ggains, gbiases, gupb = pl.pallas_call(
             finish_kernel,
-            in_specs=[anywhere] * 5 + [vmem],
-            out_specs=[anywhere] * 5 + [vmem] * 3,
+            grid=(groups,),
+            in_specs=[seq_block] + [whole(o) for o in outs],
+            out_specs=[seq_block] + [whole(o.shape) for o in ends[1:] + vectors],
             out_shape=ends + vectors,
-            scratch_shapes=[
-                pltpu.VMEM((LANES, LANES), F32),
-                pltpu.SemaphoreType.DMA((seqs + 4,)),
-            ],
+            scratch_shapes=[pltpu.VMEM((LANES, LANES), F32)],
+            compiler_params=pltpu.CompilerParams(vmem_limit_bytes=VMEM_LIMIT),
             name="hand_over",
         )(*grads)
         return out, token_grad, gqkv, gout, gup, gdown, ggains, gbiases, gupb.reshape(-1)

time: 301 us -> 182 us (0.60)
  Pallas kernels: 300 us -> 181 us
    pallas_call x1, Pallas kernels: 110 us -> 4.58 us  [per_device(): pl.pallas_call(finish_kernel, grid=(groups,), in_specs=[seq_block] + [who...]
    pallas_call x1, Pallas kernels: 65.4 us -> 57.7 us  [per_device(): pl.pallas_call(functools.partial(attention_kernel, (n_dp, n_z), True, gro...]
    pallas_call x1, Pallas kernels: 65.6 us -> 60 us  [per_device(): pl.pallas_call(functools.partial(backward_kernel, (n_dp, n_z), True, grou...]
where the time goes in v3:
time: 182 us
  Pallas kernels  181 us (99%)
    pallas_call x1, Pallas kernels, per_device(): pl.pallas_call(functools.partial(backward_kernel, (n_dp, n_z), True, grou...  60 us
    pallas_call x1, Pallas kernels, per_device(): pl.pallas_call(functools.partial(forward_kernel, block=block), grid=(chun...  58.7 us
    pallas_call x1, Pallas kernels, per_device(): pl.pallas_call(functools.partial(attention_kernel, (n_dp, n_z), True, gro...  57.7 us
    pallas_call x1, Pallas kernels, per_device(): pl.pallas_call(finish_kernel, grid=(groups,), in_specs=[seq_block] + [who...  4.58 us

profile of v3, /device:TPU:0, one launch (start us, length us, event | category | flops | bytes accessed | tf_op | source)
XLA Modules:
  0.0 181.9 jit_solution(14949914970041391940)
XLA Ops:
  0.6 57.7 %attention_forward.1 = (bf16[1536,3072]{1,0:T(8,128)(2,1)}, bf16[12,8,256,256]{3,2,1,0:T(8,128)(2,1)}, bf16[512,3072]{1,0:T(8,128)(2,1)}, f32[512,3072]{1,0:T(8,...) custom-call(s32[12]{0:T(128)} %lengths.1, ...), custom_call_target="tpu_custom_call" | custom-call | tf_op jit(solution)/shard_map/attention_forward/pallas_call | solution.py:812
  58.4 58.7 %feed_forward.1 = (bf16[12,256,512]{2,1,0:T(8,128)(2,1)}, f32[512,3072]{1,0:T(8,128)}, bf16[16,2,16,2048]{3,2,1,0:T(8,128)(2,1)}, bf16[16,2,64,512]{3,2,1,0:T(8,128)(2,1)}, f32[512,128]{1,0:T(8,128)}) custom-call(f32[512,3072]{1,0:T(8,128)} %get-tuple-element.38.r1_first.r1_next, bf16[12,256,512]{2,1,0:T(8,128)(2,1)} %g_next.1, ...), custom_call_target="tpu_custom_call" | custom-call | tf_op jit(solution)/shard_map/feed_forward/pallas_call | solution.py:880
  117.1 60.0 %attention_backward.1 = (bf16[12,256,512]{2,1,0:T(8,128)(2,1)}, f32[16,1536]{1,0:T(8,128)}, f32[16,512]{1,0:T(8,128)}, f32[16,2048]{1,0:T(8,128)}, f32[64,512]{1,0:T(8,128)}, /*index=5*/f32[16,128]{1,0:T(8,128)}) custom-call(f32[512,3072]{1,0:T(8,128)} %get-tuple-element.43.refs_0_, bf16[512,3072]{1,0:T(8,128)(2,1)} %get-tuple-element.44.refs_1_, ...), custom_call_target="tpu_custom_call" | custom-call | tf_op jit(solution)/shard_map/attention_backward/pallas_call | solution.py:967
  177.1 4.6 %hand_over.1 = (bf16[12,256,512]{2,1,0:T(8,128)(2,1)}, f32[16,1536]{1,0:T(8,128)}, f32[16,512]{1,0:T(8,128)}, f32[16,2048]{1,0:T(8,128)}, f32[64,512]{1,0:T(8,12...) custom-call(bf16[12,256,512]{2,1,0:T(8,128)(2,1)} %get-tuple-element.53.tg, ...), custom_call_target="tpu_custom_call" | custom-call | tf_op jit(solution)/shard_map/hand_over/pallas_call | solution.py:982

commit v4 on v3

v4 whole, which is shorter than its diff:
```python
import functools

import jax
import jax.numpy as jnp
from jax import lax
from jax.experimental import pallas as pl
from jax.experimental.pallas import tpu as pltpu
from jax.sharding import PartitionSpec as P

F32, BF = jnp.float32, jnp.bfloat16
MESH = pl.DeviceIdType.MESH
HEADS = 8
EPS = 1e-5
C0 = 0.7978845608028654
C1 = C0 * 0.044715
LANES = 128
NN = (((1,), (0,)), ((), ()))
NT = (((1,), (1,)), ((), ()))
TN = (((0,), (0,)), ((), ()))
VMEM_FORWARD, VMEM_MIDDLE, VMEM_BACKWARD = 32, 30.5, 37
R1 = BF


def dot(a, b, dims=NN):
    return lax.dot_general(a, b, dims, preferred_element_type=F32)


def lane_sums(v):
    total = v[:, :LANES]
    for at in range(LANES, v.shape[1], LANES):
        total = total + v[:, at : at + LANES]
    return total


def normalize(v):
    center = v - jnp.mean(v, 0, keepdims=True)
    inverse = lax.rsqrt(jnp.mean(center * center, 0, keepdims=True) + EPS)
    return center * inverse, inverse


def normalize_back(grad, normed, inverse, gain):
    scaled = grad * gain
    return inverse * (
        scaled
        - jnp.mean(scaled, 0, keepdims=True)
        - normed * jnp.mean(scaled * normed, 0, keepdims=True)
    )


class Place:
    def __init__(self, n_dp, n_z):
        self.n_dp, self.n_z = n_dp, n_z
        self.dp = lax.axis_index("dp")
        fsdp = lax.axis_index("fsdp")
        self.fsdp, self.z, self.core = fsdp, fsdp // 2, fsdp % 2
        self.slot = self.dp * n_z + self.z
        self.mate = (self.dp, self.z * 2 + 1 - self.core)

    def z_of(self, k):
        return lax.rem(self.z + k, self.n_z)

    def dp_of(self, k):
        return lax.rem(self.dp + k, self.n_dp)

    def corner(self, i):
        if i == 0:
            return self.dp
        low, high = lax.rem(self.dp, 2), self.dp // 2
        if i != 2:
            low = 1 - low
        if i != 1:
            high = 1 - high
        return high * 2 + low

    def z_peer(self, k):
        return (self.dp, self.z_of(k) * 2 + self.core)

    def dp_peer(self, k):
        return (self.dp_of(k), self.fsdp)

    def others(self):
        n_fsdp = 2 * self.n_z
        return [
            (self.dp_of(m), lax.rem(self.fsdp + k, n_fsdp))
            for m in range(self.n_dp)
            for k in range(n_fsdp)
            if m or k
        ]

    def greet(self, everyone=False):
        barrier = pltpu.get_barrier_semaphore()
        peers = [self.mate]
        peers += [self.z_peer(k) for k in range(1, self.n_z)]
        peers += [self.dp_peer(k) for k in range(1, self.n_dp)]
        if everyone:
            peers = self.others()
        for peer in peers:
            pl.semaphore_signal(barrier, inc=1, device_id=peer, device_id_type=MESH)
        pl.semaphore_wait(barrier, len(peers))


class Gather:
    def __init__(self, place, own, whole, send, recv):
        self.p, self.own, self.whole, self.send, self.recv = place, own, whole, send, recv

    def put(self, src, slot, peer, at):
        pltpu.make_async_remote_copy(
            src_ref=src,
            dst_ref=self.whole.at[slot, self.p.core],
            send_sem=self.send.at[at],
            recv_sem=self.recv.at[slot, self.p.core],
            device_id=peer,
            device_id_type=MESH,
        ).start()

    def pass_on(self, slot, peers, at):
        for i, peer in enumerate(peers):
            self.put(self.whole.at[slot, self.p.core], slot, peer, at + i)

    def landed(self, slot, core):
        there = self.whole.at[slot, core]
        pltpu.make_async_copy(there, there, self.recv.at[slot, core]).wait()

    def slot(self, corner, k):
        return self.p.corner(corner) * self.p.n_z + self.p.z_of(k)

    def side_peers(self):
        return [(self.p.corner(1), self.p.fsdp), (self.p.corner(2), self.p.fsdp), self.p.mate]

    def start(self):
        for k in range(1, self.p.n_z):
            self.put(self.own, self.p.slot, self.p.z_peer(k), k - 1)

    def spread(self):
        for i, peer in enumerate(self.side_peers()):
            self.put(self.own, self.p.slot, peer, self.p.n_z - 1 + i)

    def relay(self):
        for k in range(1, self.p.n_z):
            slot = self.slot(0, k)
            self.landed(slot, self.p.core)
            self.pass_on(slot, self.side_peers(), self.p.n_z - 1 + 3 * k)

    def cross(self):
        n_z = self.p.n_z
        first, second, mate = self.side_peers()
        at = 4 * n_z - 1
        for k in range(n_z):
            for corner, other in ((1, second), (2, first)):
                slot = self.slot(corner, k)
                self.landed(slot, self.p.core)
                early = k < n_z // 2
                peers = [mate, other] if early == (corner == 1) else [mate]
                self.pass_on(slot, peers, at)
                at += len(peers)

    def share(self):
        n_z = self.p.n_z
        for k in range(n_z):
            slot = self.slot(3, k)
            self.landed(slot, self.p.core)
            self.pass_on(slot, [self.p.mate], 7 * n_z - 1 + k)

    def finish(self):
        for k in range(self.p.n_z):
            for corner in range(4):
                self.landed(self.slot(corner, k), 1 - self.p.core)
        for at in range(self.sends(self.p.n_z)):
            pltpu.make_async_copy(self.own, self.own, self.send.at[at]).wait()

    @staticmethod
    def sends(n_z):
        return 8 * n_z - 1


def pipelined(items, ahead, behind, first, second, third):
    begun, done = {}, {}
    for at in range(-ahead, len(items) + behind):
        if 0 <= at + ahead < len(items):
            begun[at + ahead] = first(*items[at + ahead])
        if 0 <= at - behind < len(items):
            third(*items[at - behind], done.pop(at - behind))
        if 0 <= at < len(items):
            done[at] = second(*items[at], begun.pop(at))


def attention_kernel(mesh_sizes, gathers, sides, groups, lengths, x_ref, *refs):
    n_dp, n_z = mesh_sizes
    if gathers:
        (qkv_s, wo_s, wu_s, wd_s, gains_s, biases_s, upb_s,
         qkv_ref, probs_ref, inv_ref, ct_ref, r1_ref, n1_ref, inv1_ref,
         early_ref, late_ref, wo_ref, wu_ref, wd_ref,
         wqkv_t, wo_t, xt_s, normed_s, a1_s, early, late, wo, wu, wd,
         early_own, late_own, wo_own, wu_own, wd_own, small, sems, rems) = refs
    else:
        (early, late, wo,
         qkv_ref, probs_ref, inv_ref, ct_ref, r1_ref, n1_ref, inv1_ref,
         wqkv_t, wo_t, xt_s, normed_s, a1_s) = refs
    step = pl.program_id(0)
    stage, group = step // groups, lax.rem(step, groups)
    many, seq, d = x_ref.shape
    head = d // HEADS
    side_rows, side_heads = d // sides, HEADS // sides
    cols = 3 * side_rows
    scale = head**-0.5

    if gathers:
        place = Place(n_dp, n_z)
        pairs = [(early_own, early)] + [(late_own.at[i], late.at[i]) for i in range(sides - 1)]
        pairs += [(wo_own, wo), (wu_own, wu), (wd_own, wd)]
        first, *rest, out, up, down = [
            Gather(place, own, whole, sems.at[i], rems.at[i])
            for i, (own, whole) in enumerate(pairs)
        ]
        here = (place.slot, place.core)

        def enter():
            rows = qkv_s.shape[0]
            small[...] = jnp.zeros_like(small)
            small[0:2, :rows] = gains_s[...]
            small[2:8, :rows] = biases_s[...]
            for r in range(upb_s.shape[1] // rows):
                small[8 + r : 9 + r, :rows] = upb_s[:, r * rows : (r + 1) * rows]
            for side in range(sides):
                own = late_own.at[side - 1] if side else early_own
                for part in range(3):
                    at = part * d + side * side_rows
                    own[:, part * side_rows : (part + 1) * side_rows] = qkv_s[:, at : at + side_rows].astype(BF)
            early_own[:, cols:] = small[...].T[:rows].astype(BF)
            place.greet()
            first.start()
            first.spread()
            wo_own[...] = wo_s[...].astype(BF)
            wu_own[...] = wu_s[...].astype(BF)
            wd_own[...] = wd_s[...].astype(BF)
            early[here] = early_own[...]
            for i in range(sides - 1):
                late[(i, *here)] = late_own[i]
            wo[here] = wo_own[...]
            wu[here] = wu_own[...]
            wd[here] = wd_own[...]

        plan, after = plan_forward(enter, first, rest[0], out, up, down)
        for at, actions in plan.items():

            @pl.when(step == at)
            def _(actions=actions):
                for action in actions:
                    action()

    def columns():
        return early[..., cols:].reshape(d, LANES).astype(F32)

    @pl.when(stage == 0)
    def _():
        tail = lax.broadcasted_iota(jnp.int32, (16, many * seq), 0)
        n1_ref[group, d:] = jnp.where(tail == 0, 1.0, 0.0).astype(BF)
        for s in range(many):
            at = slice(seq * s, seq * (s + 1))
            xt = x_ref[s].T
            xt_s[group, :, at] = xt
            normed, inverse = normalize(xt.astype(F32))
            normed_s[group, :, at] = normed
            n1_ref[group, :d, at] = normed.astype(BF)
            inv1_ref[group, :, at] = jnp.broadcast_to(inverse, (8, seq))

    for side in range(sides):

        @pl.when(step == (side + 1) * groups)
        def _(side=side):
            if side:
                wqkv_t[...] = late[side - 1].reshape(d, cols).T
            else:
                wqkv_t[...] = early[..., :cols].reshape(d, cols).T
            if side == sides - 1:
                wo_t[...] = wo[...].reshape(d, d).T

    @pl.when(stage == 1)
    def _():
        column = columns()
        a1_s[group] = (normed_s[group] * column[:, 0:1] + column[:, 2:3]).astype(BF)

    def heads(side, last):
        mine = pl.ds(pl.multiple_of(side * side_rows, side_rows), side_rows)
        qkv = qkv_ref.at[0]
        small = early[..., cols:].reshape(d, LANES)
        if sides > 1:
            sides_small = early[pl.ds(side * (early.shape[0] // sides), early.shape[0] // sides), :, :, cols:] if len(early.shape) == 4 else early[mine, cols:]
            bias = sides_small.reshape(side_rows, LANES).astype(F32)
        else:
            bias = small.astype(F32)
        query = (dot(wqkv_t[:side_rows], a1_s[group]) + bias[:, 3:4]).astype(BF)
        qkv[:side_rows] = (query.astype(F32) * scale).astype(BF)
        qkv[side_rows : 2 * side_rows] = dot(wqkv_t[side_rows : 2 * side_rows], a1_s[group]).astype(BF)
        qkv[2 * side_rows :] = (dot(wqkv_t[2 * side_rows :], a1_s[group]) + bias[:, 4:5]).astype(BF)
        row = lax.broadcasted_iota(jnp.int32, (16, seq), 0)
        key = lax.broadcasted_iota(jnp.int32, (16, seq), 1)
        one = jnp.where(row == 0, 1.0, 0.0).astype(BF)
        masks = [
            jnp.where((row == 0) & (key >= lengths[group * many + s]), -1e30, 0.0).astype(BF)
            for s in range(many)
        ]
        items = [(s, h) for s in range(many) for h in range(side_heads)]

        def place_of(s, h, part):
            at = part * side_rows + h * head
            return slice(at, at + head), slice(seq * s, seq * (s + 1))

        def score(s, h):
            keys = jnp.concatenate([qkv[place_of(s, h, 1)], masks[s]], 0)
            queries = jnp.concatenate([qkv[place_of(s, h, 0)], one], 0)
            return dot(keys, queries, TN)

        def soften(s, h, scores):
            return jnp.exp(scores - jnp.max(scores, 0, keepdims=True)).astype(BF)

        def mix(s, h, exponent):
            probs_ref[0, s, h] = exponent
            values = jnp.concatenate([qkv[place_of(s, h, 2)], one], 0)
            mixed = dot(values, exponent)
            inverse = 1.0 / mixed[head : head + 1]
            inv_ref[side, group, pl.ds(s * side_heads + h, 1), :] = inverse
            to = pl.ds(pl.multiple_of(side * side_rows + h * head, head), head)
            ct_ref[group, to, seq * s : seq * (s + 1)] = (mixed[:head] * inverse).astype(BF)
            if last and h == side_heads - 1:
                at = slice(seq * s, seq * (s + 1))
                term = dot(wo_t[...], ct_ref[group, :, at]) + small[:, 5:6].astype(F32)
                r1_ref[group, :, at] = (xt_s[group, :, at].astype(F32) + term).astype(r1_ref.dtype)

        pipelined(items, 3, 2, score, soften, mix)

    pl.when((stage > 0) & (stage < sides))(lambda: heads(stage - 1, False))
    pl.when(stage == sides)(lambda: heads(sides - 1, True))


    if gathers:

        @pl.when(step == pl.num_programs(0) - 1)
        def _():
            for whole, to in ((early, early_ref), (late, late_ref), (wo, wo_ref)):
                to[...] = whole[...]
            for action in after:
                action()
            for whole, to in ((wu, wu_ref), (wd, wd_ref)):
                to[...] = whole[...]


def plan_forward(enter, first, late, out, up, down):
    plan = {
        0: [enter],
        2: [first.relay, late.start, out.start, up.start],
        3: [late.spread, out.spread],
        4: [first.cross, late.relay, first.share, out.relay, up.spread, down.start, first.finish],
        5: [late.cross, out.cross, up.relay, down.spread],
        6: [late.share, out.share],
        7: [down.relay, up.cross],
        8: [late.finish, out.finish],
        9: [down.cross, up.share],
        11: [down.share],
    }
    return plan, [up.finish, down.finish]


def forward_kernel(
    r1_ref, g_first, g_next, early_ref, wu_ref, wd_ref,
    out_ref, do_ref, dwu_ref, dwd_ref, small_ref,
    wu_t, wd_t, total_wu, total_wd, gt, gt_next, a2, a2_next, normed, inverse, total_out, total_a2,
    u_s, dh_s, h_s, du_s, sums, sums_up, up_bias, *, block,
):
    step = pl.program_id(0)
    groups, d, width = r1_ref.shape
    hidden = wu_t.shape[0]
    n_dev = dwd_ref.shape[0] * 2
    rows = d // n_dev
    seqs, seq = g_next.shape[:2]
    many = width // seq
    cols = early_ref.shape[-1] - LANES
    column = early_ref[..., cols:].reshape(d, LANES).astype(F32)
    blocks = hidden // block
    slots = h_s.shape[0]

    def at_of(chunk, s):
        which = chunk * seqs + s
        lane = pl.multiple_of(lax.rem(which, many) * seq, seq)
        return which // many, slice(None), pl.ds(lane, seq)

    def prepare(chunk, g_ref, gt_to, a2_to):
        for s in range(seqs):
            at = slice(seq * s, seq * (s + 1))
            gt_to[:, at] = g_ref[s].T
            r1 = r1_ref[at_of(chunk, s)].astype(F32)
            n, inv = normalize(r1)
            a2_to[:, at] = (n * column[:, 1:2] + column[:, 6:7]).astype(BF)
            normed[:, at] = n
            inverse[:, at] = jnp.broadcast_to(inv, (8, seq))
            total_out[:, at] = r1 + column[:, 7:8]

    @pl.when(step == 0)
    def _():
        wu_t[...] = wu_ref[...].reshape(d, hidden).T
        wd_t[...] = wd_ref[...].reshape(hidden, d).T
        sums[...] = jnp.zeros_like(sums)
        sums_up[...] = jnp.zeros_like(sums_up)
        for r in range(hidden // d):
            up_bias[:, r * rows : (r + 1) * rows, :] = jnp.broadcast_to(
                column[:, 8 + r : 9 + r].reshape(n_dev, rows, 1), (n_dev, rows, LANES)
            )
        prepare(0, g_first, gt, a2)

    per = block // (hidden // n_dev)

    def span(j):
        return slice(j * block, (j + 1) * block)

    def down_rows(j):
        if len(wd_ref.shape) == 2:
            return wd_ref[span(j)]
        unit = block // (2 * wd_ref.shape[2])
        return wd_ref[j * unit : (j + 1) * unit].reshape(block, d)

    def enter(j):
        bias = up_bias[j * per : (j + 1) * per].reshape(block, LANES)[:, 0:1]
        u_s[j % 2] = dot(wu_t[span(j)], a2[...]) + bias
        dh_s[j % 2] = dot(down_rows(j), gt[...])

    def bend(j):
        u = u_s[j % 2]
        square = u * u
        part = 0.5 + 0.5 * jnp.tanh(u * (C0 + C1 * square))
        h = u * part
        h_s[j % slots] = h.astype(BF)
        slope = part + h * (1.0 - part) * (2 * C0 + 6 * C1 * square)
        du = (dh_s[j % 2] * slope).astype(BF)
        du_s[j % slots] = du
        sums_up[span(j)] += lane_sums(du.astype(F32))

    def leave(j):
        total_out[...] += dot(wd_t[:, span(j)], h_s[j % slots])
        term = dot(wu_ref[..., span(j)].reshape(d, block), du_s[j % slots])
        total_a2[...] = term if j == 0 else total_a2[...] + term

    def weights(j):
        unit = block // (2 * dwd_ref.shape[2])
        at = slice(j * unit, (j + 1) * unit)
        term = dot(h_s[j % slots], gt[...], NT)
        term = jnp.where(step == 0, term, total_wd[span(j)] + term)
        total_wd[span(j)] = term
        dwd_ref[at] = term.astype(BF).reshape(unit, *dwd_ref.shape[1:])
        term = dot(a2[...], du_s[j % slots], NT)
        term = jnp.where(step == 0, term, total_wu[:, span(j)] + term)
        total_wu[:, span(j)] = term
        dwu_ref[..., span(j)] = term.astype(BF).reshape(*dwu_ref.shape[:3], block)

    def close():
        da2, n, g = total_a2[...], normed[...], gt[...].astype(F32)
        dr1 = (g + normalize_back(da2, n, inverse[0:1], column[:, 1:2])).astype(BF)
        for s in range(seqs):
            at = slice(seq * s, seq * (s + 1))
            out_ref[s] = total_out[:, at].astype(BF).T
            do_ref[at_of(step, s)] = dr1[:, at]
        sums[0] += lane_sums(da2 * n)
        sums[1] += lane_sums(da2)
        sums[2] += lane_sums(g)

    enter(0)
    for j in range(blocks):
        if j + 1 < blocks:
            enter(j + 1)
        if j:
            leave(j - 1)
        bend(j)
        if 0 < j < blocks - 1:
            weights(j - 1)
    leave(blocks - 1)
    weights(blocks - 2)
    close()
    weights(blocks - 1)
    prepare(jnp.minimum(step + 1, pl.num_programs(0) - 1), g_next, gt_next, a2_next)
    gt[...] = gt_next[...]
    a2[...] = a2_next[...]

    @pl.when(step == pl.num_programs(0) - 1)
    def _():
        lane = lax.broadcasted_iota(jnp.int32, (d, LANES), 1)
        small = jnp.zeros((d, LANES), F32)
        for s, at in ((0, 1), (1, 6), (2, 7)):
            small = jnp.where(lane == at, jnp.sum(sums[s], 1, keepdims=True), small)
        up = jnp.sum(sums_up[...], 1, keepdims=True).reshape(n_dev, hidden // n_dev, 1)
        for r in range(hidden // d):
            part = up[:, r * rows : (r + 1) * rows].reshape(d, 1)
            small = jnp.where(lane == 8 + r, part, small)
        small_ref[...] = small


class Scatter:
    def __init__(self, place, part, result, bufs, send, recv, flip=False):
        self.p, self.part, self.result = place, part, result
        self.sum1, self.got1, self.got2, self.sum2, self.got3 = bufs
        self.send, self.recv = send, recv
        p = place
        by_z = (p.n_z, p.z_peer, lambda far, near: p.dp_of(near) * p.n_z + p.z_of(far))
        by_dp = (p.n_dp, p.dp_peer, lambda far, near: p.dp_of(far) * p.n_z + p.z_of(near))
        (self.far, self.far_peer, self.slot), (self.near, self.near_peer, _) = (
            (by_z, by_dp) if flip else (by_dp, by_z)
        )

    @staticmethod
    def scratch(n_dp, n_z, rows, width, kind, flip=False):
        far, near = (n_z, n_dp) if flip else (n_dp, n_z)
        return [
            pltpu.VMEM((n_dp * n_z, rows, width), kind),
            pltpu.VMEM((n_dp * n_z, rows, width), kind),
            pltpu.VMEM((far - 1, near, rows, width), kind),
            pltpu.VMEM((near, rows, width), kind),
            pltpu.VMEM((near - 1, rows, width), kind),
        ]

    @staticmethod
    def sems(n_dp, n_z):
        return 1 + (max(n_dp, n_z) - 1) * max(n_dp, n_z) + max(n_dp, n_z) - 1

    def copy(self, src, dst, at, peer):
        return pltpu.make_async_remote_copy(
            src_ref=src,
            dst_ref=dst,
            send_sem=self.send.at[at],
            recv_sem=self.recv.at[at],
            device_id=peer,
            device_id_type=MESH,
        )

    def to_mate(self):
        return self.copy(self.sum1, self.got1, 0, self.p.mate)

    def afar(self):
        return [
            self.copy(
                self.sum1.at[self.slot(k, m)],
                self.got2.at[k - 1, m],
                1 + (k - 1) * self.near + m,
                self.far_peer(k),
            )
            for k in range(1, self.far)
            for m in range(self.near)
        ]

    def nearby(self):
        return [
            self.copy(
                self.sum2.at[m],
                self.got3.at[m - 1],
                1 + (self.far - 1) * self.near + m - 1,
                self.near_peer(m),
            )
            for m in range(1, self.near)
        ]

    def step1(self):
        def cast(s, _):
            self.sum1[s] = self.part[s, 1 - self.p.core].astype(self.sum1.dtype)
            return 0

        lax.fori_loop(0, self.p.n_dp * self.p.n_z, cast, 0)
        self.to_mate().start()

    def step2(self):
        self.to_mate().wait()

        def add(s, _):
            total = self.part[s, self.p.core].astype(F32) + self.got1[s].astype(F32)
            self.sum1[s] = total.astype(self.sum1.dtype)
            return 0

        lax.fori_loop(0, self.p.n_dp * self.p.n_z, add, 0)
        for copy in self.afar():
            copy.start()

    def step3(self):
        for copy in self.afar():
            copy.wait()
        for m in range(self.near):
            total = self.sum1[self.slot(0, m)].astype(F32)
            for k in range(self.far - 1):
                total = total + self.got2[k, m].astype(F32)
            self.sum2[m] = total.astype(self.sum2.dtype)
        for copy in self.nearby():
            copy.start()

    def step4(self):
        for copy in self.nearby():
            copy.wait()
        total = self.sum2[0].astype(F32)
        for m in range(self.near - 1):
            total = total + self.got3[m].astype(F32)
        self.result[...] = total


def backward_kernel(mesh_sizes, scatters, sides, groups, *refs):
    n_dp, n_z = mesh_sizes
    (do_ref, ct_ref, qkv_ref, probs_ref, inv_ref, n1_ref, inv1_ref,
     early_ref, late_ref, wo_ref, part_ref) = refs[:11]
    refs = refs[11:]
    if scatters:
        (dwu_ref, dwd_ref, tg_ref, gqkv_ref, gout_ref, gup_ref, gdown_ref, gsmall_ref,
         dp_s, total_qkv, total_out, sum_dp, dc_s, sums, part_small, gqkv_side) = refs[:16]
        buffers, (send, recv) = refs[16:-2], refs[-2:]
    else:
        (tg_ref, gqkv_ref, gout_ref, gsmall_ref, dp_s, total_qkv, total_out, sum_dp, dc_s, sums) = refs
    step = pl.program_id(0)
    last = pl.num_programs(0) - 1
    stage, group = step // groups, lax.rem(step, groups)
    d, width = do_ref.shape[1:]
    many, seq = tg_ref.shape[:2]
    head = d // HEADS
    side_rows, side_heads = d // sides, HEADS // sides
    cols = 3 * side_rows
    scale = head**-0.5
    opening = group == 0

    def columns():
        return early_ref[..., cols:].reshape(d, LANES).astype(F32)

    def side_weights(side):
        w = late_ref[side - 1] if side else early_ref[..., :cols]
        return w.reshape(d, cols)

    @pl.when(step == 0)
    def _():
        sums[...] = jnp.zeros_like(sums)

    def pack(side):
        n_slots, _, rows, _ = total_qkv.shape[1:]
        column, w = columns(), side_weights(side)
        row = sum_dp[side, 0:1]
        for slot in range(n_slots):
            at = slice(slot * 2 * rows, (slot + 1) * 2 * rows)
            product = total_qkv[side, slot].reshape(2 * rows, cols)
            piece = w[at].astype(F32)
            sums[0, at] += lane_sums(piece * product)
            sums[1, at] += lane_sums(piece * row)
            whole = column[at, 0:1] * product + column[at, 2:3] * row
            total_qkv[side, slot] = whole.reshape(2, rows, cols)

    def vectors():
        lane = lax.broadcasted_iota(jnp.int32, (d, LANES), 1)
        small = part_ref[...]
        for s, at in enumerate((0, 2, 3, 4, 5)):
            small = jnp.where(lane == at, jnp.sum(sums[s], 1, keepdims=True), small)
        return small

    if scatters:
        place = Place(n_dp, n_z)
        cut = dwd_ref.shape[2] // 2
        parts = [
            (dwu_ref, gup_ref, False),
            (dwd_ref.at[:, :, :cut], gdown_ref.at[:cut], False),
            (dwd_ref.at[:, :, cut:], gdown_ref.at[cut:], True),
            (total_out, gout_ref, False),
            (part_small, gsmall_ref, False),
        ]
        parts += [(total_qkv.at[i], gqkv_side.at[i], False) for i in range(sides)]
        up, down, down2, out, small, *qkvs = [
            Scatter(place, part, result, buffers[5 * i : 5 * i + 5], send.at[i], recv.at[i], flip)
            for i, (part, result, flip) in enumerate(parts)
        ]

        def pack_small():
            part_small[...] = vectors().reshape(part_small.shape)

        packs = [functools.partial(pack, i) for i in range(sides)]
        plan, after = plan_backward(place.greet, up, down, down2, out, small, qkvs, packs, pack_small)
        for at, actions in plan.items():

            @pl.when(step == at)
            def _(actions=actions):
                for action in actions:
                    action()

    @pl.when(stage == 0)
    def _():
        n_slots = total_out.shape[0]
        for part in range(2):
            at = slice(part * n_slots // 2, (part + 1) * n_slots // 2)
            term = dot(ct_ref[group, part * d // 2 : (part + 1) * d // 2], do_ref[group], NT)
            term = term.reshape(n_slots // 2, *total_out.shape[1:])
            total_out[at] = jnp.where(opening, term, total_out[at] + term)
        sums[4] += lane_sums(do_ref[group].astype(F32))

    def heads(side):
        mine = pl.ds(pl.multiple_of(side * side_rows, side_rows), side_rows)
        qkv, to = qkv_ref.at[0], dp_s.at[side, group]
        if len(wo_ref.shape) == 4:
            part = wo_ref.shape[0] // sides
            wo = wo_ref[pl.ds(side * part, part)].reshape(side_rows, d)
        else:
            wo = wo_ref[mine, :]
        dc_s[...] = dot(wo, do_ref[group])
        items = [(s, h) for s in range(many) for h in range(side_heads)]

        def place_of(s, h, part):
            at = part * side_rows + h * head
            return slice(at, at + head), slice(seq * s, seq * (s + 1))

        def grad_probs(s, h):
            inverse = inv_ref[side, group, pl.ds(s * side_heads + h, 1), :]
            dc = (dc_s[place_of(s, h, 0)] * inverse).astype(BF)
            return dc, dot(qkv[place_of(s, h, 2)], dc, TN)

        def grad_scores(s, h, begun):
            dc, term = begun
            there = pl.ds(pl.multiple_of(side * side_rows + h * head, head), head)
            delta = dc.astype(F32) * ct_ref[group, there, seq * s : seq * (s + 1)].astype(F32)
            delta = jnp.sum(delta, 0, keepdims=True)
            return dc, (probs_ref[0, s, h].astype(F32) * (term - delta)).astype(BF)

        def finish(s, h, done):
            dc, ds = done
            q, k, v = (place_of(s, h, part) for part in range(3))
            to[v] = dot(dc, probs_ref[0, s, h], NT).astype(BF)
            to[k] = dot(qkv[q], ds, NT).astype(BF)
            to[q] = (dot(qkv[k], ds) * scale).astype(BF)

        pipelined(items, 2, 1, grad_probs, grad_scores, finish)
        n_slots = total_qkv.shape[1]
        for part in range(2):
            at = slice(part * n_slots // 2, (part + 1) * n_slots // 2)
            term = dot(n1_ref[group, part * d // 2 : (d // 2, d + 16)[part]], to[...], NT)
            product = term[: d // 2].reshape(n_slots // 2, *total_qkv.shape[2:])
            total_qkv[side, at] = jnp.where(opening, product, total_qkv[side, at] + product)
        row = term[d // 2 : d // 2 + 8]
        sum_dp[side] = jnp.where(opening, row, sum_dp[side] + row)
        sums[2, mine, :] += lane_sums(to[:side_rows].astype(F32))
        sums[3, mine, :] += lane_sums(to[2 * side_rows :].astype(F32))

    pl.when(stage < sides)(lambda: heads(stage))

    @pl.when(stage == sides)
    def _():
        gain = columns()[:, 0:1]

        def product(s):
            at = slice(seq * s, seq * (s + 1))
            total = dot(side_weights(0), dp_s[0, group, :, at])
            for side in range(1, sides):
                total = total + dot(side_weights(side), dp_s[side, group, :, at])
            return total

        def finish(s, _, da1):
            at = slice(seq * s, seq * (s + 1))
            normed = n1_ref[group, :d, at].astype(F32)
            dv = normalize_back(da1, normed, inv1_ref[group, 0:1, at], gain)
            tg_ref[s] = (do_ref[group, :, at].astype(F32) + dv).astype(BF).T

        ahead = product(0)
        for s in range(many):
            da1, ahead = ahead, product(s + 1) if s + 1 < many else None
            finish(s, None, da1)

    @pl.when(step == last)
    def _():
        if scatters:
            for action in after:
                action()
            shards = gqkv_side
        else:
            for side in range(sides):
                pack(side)
            gout_ref[...] = total_out[...].reshape(d, d)
            gsmall_ref[...] = vectors()
            shards = total_qkv
        for side in range(sides):
            whole = shards[side].reshape(gqkv_ref.shape[0], cols)
            for part in range(3):
                at = part * d + side * side_rows
                gqkv_ref[:, at : at + side_rows] = whole[:, part * side_rows : (part + 1) * side_rows]


def plan_backward(greet, up, down, down2, out, small, qkvs, packs, pack_small):
    qkv0, qkv1 = qkvs
    plan = {
        0: [greet, up.step1, down2.step1, down.step1],
        1: [up.step2, down2.step2, down.step2],
        4: [packs[0], qkv0.step1, out.step1],
        5: [up.step3, down2.step3, qkv0.step2, out.step2],
        7: [down.step3],
        8: [packs[1], qkv1.step1, pack_small, small.step1, up.step4, down2.step4],
        9: [qkv1.step2, small.step2, qkv0.step3, out.step3],
        10: [down.step4],
        11: [qkv0.step4, out.step4],
    }
    return plan, [qkv1.step3, small.step3, qkv1.step4, small.step4]


def finish_kernel(tg, qkv, out, up, down, small, tg_to, qkv_to, out_to, up_to, down_to, gains, biases, upb, turn):
    tg_to[...] = tg[...]

    @pl.when(pl.program_id(0) == 0)
    def _():
        for source, to in ((qkv, qkv_to), (out, out_to), (up, up_to), (down, down_to)):
            to[...] = source[...]
        rows = small.shape[0]
        turn[...] = jnp.zeros_like(turn)
        turn[:rows] = small[...]
        turned = turn[...].T
        gains[...] = turned[0:2, :rows]
        biases[...] = turned[2:8, :rows]
        for r in range(upb.shape[1] // rows):
            upb[:, r * rows : (r + 1) * rows] = turned[8 + r : 9 + r, :rows]


def in_hbm(*arrays):
    return tuple(pltpu.with_memory_space_constraint(array, pltpu.HBM) for array in arrays)


def per_device(n_dp, n_fsdp, tokens, lengths, cotangent, qkv_w, out_w, up_w, down_w, gains, biases, up_bias):
    tokens, lengths, cotangent = in_hbm(tokens, lengths, cotangent)
    seqs, seq, d = tokens.shape
    n_z, n_dev = n_fsdp // 2, n_dp * n_fsdp
    rows, rows_down = qkv_w.shape[0], down_w.shape[0]
    hidden = up_w.shape[1]
    slots = n_dp * n_z
    axes = ("dp", "fsdp")
    direct = rows % 16 == 0 and n_dp == 4
    cut = n_dev if direct else 32
    quarter = hidden // d
    many = next(m for m in (3, 2, 1) if seqs % m == 0)
    groups, width = seqs // many, many * seq
    sides = 2
    side_rows, side_heads = d // sides, HEADS // sides
    cols = 3 * side_rows
    wide = cols + LANES

    def whole(shape):
        return pl.BlockSpec(shape, lambda i: (0,) * len(shape), pipeline_mode=pl.Buffered(1))

    def shape(dims, kind):
        return jax.ShapeDtypeStruct(dims, kind)

    anywhere = pl.BlockSpec(memory_space=pl.ANY)
    smem = pl.BlockSpec(memory_space=pltpu.SMEM)
    vmem = pl.BlockSpec(memory_space=pltpu.VMEM)
    probs_block = (1, many, side_heads, seq, seq)

    def params(mib, **more):
        return pltpu.CompilerParams(vmem_limit_bytes=int(mib * 2**20), **more)

    held = [
        pltpu.HBM((sides * groups, cols, width), BF),
        pltpu.HBM((sides * groups, *probs_block[1:]), BF),
        pltpu.VMEM((sides, groups, many * side_heads, seq), F32),
        pltpu.VMEM((groups, d, width), BF),
        pltpu.VMEM((groups, d, width), R1),
        pltpu.VMEM((groups, d + 16, width), BF),
        pltpu.VMEM((groups, 8, width), F32),
    ]
    held_specs = [vmem] * len(held)
    held_specs[0] = pl.BlockSpec((1, cols, width), lambda i: (jnp.maximum(i - groups, 0), 0, 0))
    held_specs[1] = pl.BlockSpec(
        probs_block, lambda i: (jnp.maximum(i - groups, 0), 0, 0, 0, 0)
    )
    in_specs = [
        smem,
        pl.BlockSpec((many, seq, d), lambda i: (jnp.minimum(i, groups - 1), 0, 0)),
    ]
    scratch = [
        pltpu.VMEM((cols, d), BF),
        pltpu.VMEM((d, d), BF),
        pltpu.VMEM((groups, d, width), BF),
        pltpu.VMEM((groups, d, width), F32),
        pltpu.VMEM((groups, d, width), BF),
    ]
    steps = (1 + sides) * groups
    if direct:
        n_sends = Gather.sends(n_z)
        shards = in_hbm(qkv_w, out_w, up_w, down_w, gains, biases, up_bias.reshape(1, -1))
        qkv, probs, inv, ct, r1, n1, inv1, early, late, wo, wu, wd = pl.pallas_call(
            functools.partial(attention_kernel, (n_dp, n_z), True, sides, groups),
            grid=(steps,),
            in_specs=in_specs + [whole(s.shape) for s in shards],
            out_specs=held_specs + [vmem] * 5,
            out_shape=held
            + [
                pltpu.VMEM((slots, 2, rows, wide), BF),
                pltpu.VMEM((sides - 1, slots, 2, rows, cols), BF),
                pltpu.VMEM((slots, 2, rows, d), BF),
                pltpu.VMEM((slots, 2, rows, hidden), BF),
                pltpu.VMEM((slots, 2, rows_down, d), BF),
            ],
            scratch_shapes=scratch
            + [
                pltpu.VMEM((slots, 2, rows, wide), BF),
                pltpu.VMEM((sides - 1, slots, 2, rows, cols), BF),
                pltpu.VMEM((slots, 2, rows, d), BF),
                pltpu.VMEM((slots, 2, rows, hidden), BF),
                pltpu.VMEM((slots, 2, rows_down, d), BF),
                pltpu.VMEM((rows, wide), BF),
                pltpu.VMEM((sides - 1, rows, cols), BF),
                pltpu.VMEM((rows, d), BF),
                pltpu.VMEM((rows, hidden), BF),
                pltpu.VMEM((rows_down, d), BF),
                pltpu.VMEM((LANES, LANES), F32),
                pltpu.SemaphoreType.DMA((sides + 3, n_sends)),
                pltpu.SemaphoreType.DMA((sides + 3, slots, 2)),
            ],
            compiler_params=params(VMEM_FORWARD, collective_id=0, has_side_effects=True),
            name="attention_forward",
        )(lengths, tokens, *shards)
    else:
        split = [
            jnp.concatenate([qkv_w[:, p * d + i * side_rows :][:, :side_rows] for p in range(3)], 1)
            for i in range(sides)
        ]
        early = jnp.concatenate([split[0], gains.T, biases.T], 1).astype(BF)
        early = lax.all_gather(early, axes, axis=0, tiled=True)
        up_all = lax.all_gather(up_bias.astype(BF), axes, axis=0, tiled=True)
        up_all = up_all.reshape(cut, quarter, d // cut).swapaxes(1, 2).reshape(d, quarter)
        early = jnp.concatenate([early, up_all], 1)
        early = jnp.pad(early, ((0, 0), (0, wide - early.shape[1])))
        late = lax.all_gather(jnp.stack(split[1:]).astype(BF), axes, axis=1, tiled=True)
        wo = lax.all_gather(out_w.astype(BF), axes, axis=0, tiled=True)
        wu = lax.all_gather(up_w.astype(BF), axes, axis=0, tiled=True)
        wd = lax.all_gather(down_w.astype(BF), axes, axis=0, tiled=True)
        qkv, probs, inv, ct, r1, n1, inv1 = pl.pallas_call(
            functools.partial(attention_kernel, (n_dp, n_z), False, sides, groups),
            grid=(steps,),
            in_specs=in_specs + [whole(early.shape), whole(late.shape), whole(wo.shape)],
            out_specs=held_specs,
            out_shape=held,
            scratch_shapes=scratch,
            compiler_params=params(VMEM_FORWARD),
            name="attention_forward",
        )(lengths, tokens, early, late, wo)

    def weight(array):
        return vmem if direct else whole(array.shape)

    pair = 2 if seqs % 2 == 0 else 1
    chunk = pair * seq
    chunks = seqs // pair
    block = d // 2
    lag = 4
    parts = [
        pltpu.VMEM((cut // 2, 2, d // cut, hidden), BF),
        pltpu.VMEM((cut // 2, 2, hidden // cut, d), BF),
    ]
    part_specs = [vmem] * 2
    if not direct:
        parts = [shape(part.shape, BF) for part in parts]
        part_specs = [whole(part.shape) for part in parts]
    out, do, dwu, dwd, small = pl.pallas_call(
        functools.partial(forward_kernel, block=block),
        grid=(chunks,),
        in_specs=[
            vmem,
            whole((pair, seq, d)),
            pl.BlockSpec((pair, seq, d), lambda i: (jnp.minimum(i + 1, chunks - 1), 0, 0)),
            weight(early),
            weight(wu),
            weight(wd),
        ],
        out_specs=[pl.BlockSpec((pair, seq, d), lambda i: (i, 0, 0)), vmem]
        + part_specs
        + [whole((d, LANES))],
        out_shape=[pltpu.HBM(tokens.shape, BF), pltpu.VMEM((groups, d, width), BF)]
        + parts
        + [shape((d, LANES), F32)],
        scratch_shapes=[pltpu.VMEM((hidden, d), BF), pltpu.VMEM((d, hidden), BF)]
        + [pltpu.VMEM((d, hidden), F32), pltpu.VMEM((hidden, d), F32)]
        + [pltpu.VMEM((d, chunk), BF)] * 4
        + [pltpu.VMEM((d, chunk), F32), pltpu.VMEM((8, chunk), F32)]
        + [pltpu.VMEM((d, chunk), F32)] * 2
        + [pltpu.VMEM((2, block, chunk), F32)] * 2
        + [pltpu.VMEM((lag, block, chunk), BF)] * 2
        + [
            pltpu.VMEM((3, d, LANES), F32),
            pltpu.VMEM((hidden, LANES), F32),
            pltpu.VMEM((cut, hidden // cut, LANES), F32),
        ],
        compiler_params=params(VMEM_MIDDLE if direct else VMEM_MIDDLE + 16),
        name="feed_forward",
    )(r1, cotangent, cotangent, early, wu, wd)

    seq_block = pl.BlockSpec((many, seq, d), lambda i: (jnp.maximum(i - sides * groups, 0), 0, 0))
    acts = (do, ct, qkv, probs, inv, n1, inv1, early, late, wo, small)
    acts_in = [vmem] * 7 + [weight(early), weight(late), weight(wo), whole((d, LANES))]
    acts_in[2] = pl.BlockSpec(
        (1, cols, width), lambda i: (jnp.minimum(i, sides * groups - 1), 0, 0)
    )
    acts_in[3] = pl.BlockSpec(
        probs_block, lambda i: (jnp.minimum(i, sides * groups - 1), 0, 0, 0, 0)
    )
    base = [
        pltpu.VMEM((sides, groups, cols, width), BF),
        pltpu.VMEM((sides, cut // 2, 2, d // cut, cols), F32),
        pltpu.VMEM((cut // 2, 2, d // cut, d), F32),
        pltpu.VMEM((sides, 8, cols), F32),
        pltpu.VMEM((side_rows, width), F32),
        pltpu.VMEM((5, d, LANES), F32),
    ]
    if direct:
        n_sems = Scatter.sems(n_dp, n_z)
        plan = [(rows, hidden, False), (rows_down // 2, d, False), (rows_down // 2, d, True), (rows, d, False), (rows, LANES, False)]
        plan += [(rows, cols, False)] * sides
        outs = [(rows, 3 * d), (rows, d), (rows, hidden), (rows_down, d), (rows, LANES)]
        scratch = base + [
            pltpu.VMEM((slots, 2, rows, LANES), F32),
            pltpu.VMEM((sides, rows, cols), F32),
        ]
        for height, across, flip in plan:
            scratch += Scatter.scratch(n_dp, n_z, height, across, BF, flip)
        scratch += [pltpu.SemaphoreType.DMA((len(plan), n_sems))] * 2
        grads = pl.pallas_call(
            functools.partial(backward_kernel, (n_dp, n_z), True, sides, groups),
            grid=(steps,),
            in_specs=acts_in + [vmem, vmem],
            out_specs=[seq_block] + [whole(o) for o in outs],
            out_shape=[pltpu.HBM(o, BF if i == 0 else F32) for i, o in enumerate([tokens.shape] + outs)],
            scratch_shapes=scratch,
            compiler_params=params(VMEM_BACKWARD, collective_id=1, has_side_effects=True),
            name="attention_backward",
        )(*acts, dwu, dwd)
        ends = [shape(tokens.shape, BF)] + [shape(o, F32) for o in outs[:4]]
        vectors = [shape(v, F32) for v in (gains.shape, biases.shape, (1, quarter * rows))]
        seq_block = pl.BlockSpec((many, seq, d), lambda i: (i, 0, 0))
        token_grad, gqkv, gout, gup, gdown, ggains, gbiases, gupb = pl.pallas_call(
            finish_kernel,
            grid=(groups,),
            in_specs=[seq_block] + [whole(o) for o in outs],
            out_specs=[seq_block] + [whole(o.shape) for o in ends[1:] + vectors],
            out_shape=ends + vectors,
            scratch_shapes=[pltpu.VMEM((LANES, LANES), F32)],
            compiler_params=params(60),
            name="hand_over",
        )(*grads)
        return out, token_grad, gqkv, gout, gup, gdown, ggains, gbiases, gupb.reshape(-1)

    token_grad, gqkv, gout, gsmall = pl.pallas_call(
        functools.partial(backward_kernel, (n_dp, n_z), False, sides, groups),
        grid=(steps,),
        in_specs=acts_in,
        out_specs=[seq_block, whole((d, 3 * d)), whole((d, d)), whole((d, LANES))],
        out_shape=[shape(tokens.shape, BF), shape((d, 3 * d), F32), shape((d, d), F32), shape((d, LANES), F32)],
        scratch_shapes=base,
        compiler_params=params(VMEM_BACKWARD),
        name="attention_backward",
    )(*acts)

    def scatter(term):
        return lax.psum_scatter(term.astype(F32), axes, scatter_dimension=0, tiled=True)

    up_sums = gsmall[:, 8 : 8 + quarter].reshape(cut, d // cut, quarter).swapaxes(1, 2)
    gsmall = scatter(gsmall[:, :8]).T
    return (
        out,
        token_grad,
        scatter(gqkv),
        scatter(gout),
        scatter(dwu.reshape(d, hidden)),
        scatter(dwd.reshape(hidden, d)),
        gsmall[:2],
        gsmall[2:8],
        scatter(up_sums.reshape(hidden)),
    )


def solution(mesh):
    axes = ("dp", "fsdp")
    rows, cols, flat = P(axes, None), P(None, axes), P(axes)
    data = P(axes, None, None)
    return jax.shard_map(
        functools.partial(per_device, mesh.shape["dp"], mesh.shape["fsdp"]),
        mesh=mesh,
        in_specs=(data, flat, data, rows, rows, rows, rows, cols, cols, flat),
        out_specs=(data, data, rows, rows, rows, rows, cols, cols, flat),
        check_vma=False,
    )
```

time: 182 us -> 164 us (0.901)
  Pallas kernels: 181 us -> 163 us
    pallas_call x2, Pallas kernels: 118 us -> 102 us  [the longest x1 51.3 us: per_device(): pl.pallas_call(functools.partial(attention_kernel, (n_dp, n_z), True, sid...]
    pallas_call x1, Pallas kernels: 58.7 us -> 56.6 us  [per_device(): pl.pallas_call(functools.partial(forward_kernel, block=block), grid=(chun...]
where the time goes in v4:
time: 164 us
  Pallas kernels  163 us (99%)
    pallas_call x1, Pallas kernels, per_device(): pl.pallas_call(functools.partial(forward_kernel, block=block), grid=(chun...  56.6 us
    pallas_call x1, Pallas kernels, per_device(): pl.pallas_call(functools.partial(attention_kernel, (n_dp, n_z), True, sid...  51.3 us
    pallas_call x1, Pallas kernels, per_device(): pl.pallas_call(functools.partial(backward_kernel, (n_dp, n_z), True, side...  50.7 us
    pallas_call x1, Pallas kernels, per_device(): pl.pallas_call(finish_kernel, grid=(groups,), in_specs=[seq_block] + [who...  4.58 us

profile of v4, /device:TPU:0, one launch (start us, length us, event | category | flops | bytes accessed | tf_op | source)
XLA Modules:
  0.0 164.0 jit_solution(279489950004949399)
XLA Ops:
  0.6 51.3 %attention_forward.1 = (bf16[8,768,768]{2,1,0:T(8,128)(2,1)}, bf16[8,3,4,256,256]{4,3,2,1,0:T(8,128)(2,1)}, f32[2,4,12,256]{3,2,1,0:T(8,128)S(1)}, bf16[4,512,76...) custom-call(s32[12]{0:T(128)} %lengths.1, ...), custom_call_target="tpu_custom_call" | custom-call | tf_op jit(solution)/shard_map/attention_forward/pallas_call | solution.py:876
  52.0 56.6 %feed_forward.1 = (bf16[12,256,512]{2,1,0:T(8,128)(2,1)}, bf16[4,512,768]{2,1,0:T(8,128)(2,1)S(1)}, bf16[16,2,16,2048]{3,2,1,0:T(8,128)(2,1)S(1)}, bf16[16,2,64,512]{3,2,1,0:T(8,128)(2,1)S(1)}, f32[512,128]{1,0:T(8,128)S(1)}) custom-call(bf16[4,512,768]{2,1,0:T(8,128)(2,1)S(1)} %get-tuple-element.40.r1_ref, bf16[12,256,512]{2,1,0:T(8,128)(2,1)} %g_next.1, ...), custom_call_target="tpu_custom_call" | custom-call | tf_op jit(solution)/shard_map/feed_forward/pallas_call | solution.py:950
  108.6 50.7 %attention_backward.1 = (bf16[12,256,512]{2,1,0:T(8,128)(2,1)}, f32[16,1536]{1,0:T(8,128)}, f32[16,512]{1,0:T(8,128)}, f32[16,2048]{1,0:T(8,128)}, f32[64,512]{1,0:T(8,128)}, /*index=5*/f32[16,128]{1,0:T(8,128)}) custom-call(bf16[4,512,768]{2,1,0:T(8,128)(2,1)S(1)} %get-tuple-element.45.refs_0_, bf16[4,512,768]{2,1,0:T(8,128)(2,1)S(1)} %get-tuple-element.46.refs_1_, ...), custom_call_target="tpu_custom_call" | custom-call | tf_op jit(solution)/shard_map/attention_backward/pallas_call | solution.py:1012
  159.2 4.6 %hand_over.1 = (bf16[12,256,512]{2,1,0:T(8,128)(2,1)}, f32[16,1536]{1,0:T(8,128)}, f32[16,512]{1,0:T(8,128)}, f32[16,2048]{1,0:T(8,128)}, f32[64,512]{1,0:T(8,12...) custom-call(bf16[12,256,512]{2,1,0:T(8,128)(2,1)} %get-tuple-element.57.tg, ...), custom_call_target="tpu_custom_call" | custom-call | tf_op jit(solution)/shard_map/hand_over/pallas_call | solution.py:1025

commit v5 on v4

--- a/solution.py
+++ b/solution.py
@@ -17,8 +17,7 @@
 NN = (((1,), (0,)), ((), ()))
 NT = (((1,), (1,)), ((), ()))
 TN = (((0,), (0,)), ((), ()))
-VMEM_FORWARD, VMEM_MIDDLE, VMEM_BACKWARD = 32, 30.5, 37
-R1 = BF
+VMEM_FORWARD, VMEM_MIDDLE, VMEM_BACKWARD = 40, 36, 36
 
 
 def dot(a, b, dims=NN):
@@ -32,9 +31,15 @@
     return total
 
 
+def center_of(v):
+    mean = jnp.mean(v, 0, keepdims=True)
+    center = v - mean
+    inverse = lax.rsqrt(jnp.mean(center * center, 0, keepdims=True) + EPS)
+    return center, inverse, mean
+
+
 def normalize(v):
-    center = v - jnp.mean(v, 0, keepdims=True)
-    inverse = lax.rsqrt(jnp.mean(center * center, 0, keepdims=True) + EPS)
+    center, inverse, _ = center_of(v)
     return center * inverse, inverse
 
 
@@ -173,6 +178,31 @@
         return 8 * n_z - 1
 
 
+class ShortGather(Gather):
+    def side_peers(self):
+        p = self.p
+        return [(p.corner(i), p.fsdp) for i in (1, 2, 3)] + [p.mate]
+
+    def relay(self):
+        for k in range(1, self.p.n_z):
+            slot = self.slot(0, k)
+            self.landed(slot, self.p.core)
+            self.pass_on(slot, self.side_peers(), self.p.n_z - 1 + 4 * k)
+
+    def cross(self):
+        n_z = self.p.n_z
+        at = 5 * n_z - 1
+        for k in range(n_z):
+            for corner in (1, 2, 3):
+                slot = self.slot(corner, k)
+                self.landed(slot, self.p.core)
+                self.pass_on(slot, [self.p.mate], at)
+                at += 1
+
+    def share(self):
+        pass
+
+
 def pipelined(items, ahead, behind, first, second, third):
     begun, done = {}, {}
     for at in range(-ahead, len(items) + behind):
@@ -184,17 +214,17 @@
             done[at] = second(*items[at], begun.pop(at))
 
 
-def attention_kernel(mesh_sizes, gathers, sides, groups, lengths, x_ref, *refs):
+def attention_kernel(mesh_sizes, gathers, sides, groups, lengths, x_ref, g_ref, *refs):
     n_dp, n_z = mesh_sizes
     if gathers:
         (qkv_s, wo_s, wu_s, wd_s, gains_s, biases_s, upb_s,
-         qkv_ref, probs_ref, inv_ref, ct_ref, r1_ref, n1_ref, inv1_ref,
+         qkv_ref, probs_ref, inv_ref, ct_ref, n1_ref, inv1_ref, r1_ref, a2_ref, gt_ref, norm2_ref, gsum_ref,
          early_ref, late_ref, wo_ref, wu_ref, wd_ref,
          wqkv_t, wo_t, xt_s, normed_s, a1_s, early, late, wo, wu, wd,
          early_own, late_own, wo_own, wu_own, wd_own, small, sems, rems) = refs
     else:
         (early, late, wo,
-         qkv_ref, probs_ref, inv_ref, ct_ref, r1_ref, n1_ref, inv1_ref,
+         qkv_ref, probs_ref, inv_ref, ct_ref, n1_ref, inv1_ref, r1_ref, a2_ref, gt_ref, norm2_ref, gsum_ref,
          wqkv_t, wo_t, xt_s, normed_s, a1_s) = refs
     step = pl.program_id(0)
     stage, group = step // groups, lax.rem(step, groups)
@@ -209,7 +239,7 @@
         pairs = [(early_own, early)] + [(late_own.at[i], late.at[i]) for i in range(sides - 1)]
         pairs += [(wo_own, wo), (wu_own, wu), (wd_own, wd)]
         first, *rest, out, up, down = [
-            Gather(place, own, whole, sems.at[i], rems.at[i])
+            (Gather if i else ShortGather)(place, own, whole, sems.at[i], rems.at[i])
             for i, (own, whole) in enumerate(pairs)
         ]
         here = (place.slot, place.core)
@@ -254,15 +284,19 @@
     @pl.when(stage == 0)
     def _():
         tail = lax.broadcasted_iota(jnp.int32, (16, many * seq), 0)
-        n1_ref[group, d:] = jnp.where(tail == 0, 1.0, 0.0).astype(BF)
+        n1_ref[0, d:] = jnp.where(tail == 0, 1.0, 0.0).astype(BF)
         for s in range(many):
             at = slice(seq * s, seq * (s + 1))
             xt = x_ref[s].T
             xt_s[group, :, at] = xt
             normed, inverse = normalize(xt.astype(F32))
             normed_s[group, :, at] = normed
-            n1_ref[group, :d, at] = normed.astype(BF)
+            n1_ref[0, :d, at] = normed.astype(BF)
             inv1_ref[group, :, at] = jnp.broadcast_to(inverse, (8, seq))
+            gt = g_ref[s].T
+            gt_ref[0, :, at] = gt
+            term = lane_sums(gt.astype(F32))
+            gsum_ref[...] = jnp.where((step == 0) & (s == 0), term, gsum_ref[...] + term)
 
     for side in range(sides):
 
@@ -280,15 +314,26 @@
         column = columns()
         a1_s[group] = (normed_s[group] * column[:, 0:1] + column[:, 2:3]).astype(BF)
 
+    def attended(group, s):
+        at = slice(seq * s, seq * (s + 1))
+        small = columns()
+        term = dot(wo_t[...], ct_ref[group, :, at]) + small[:, 5:6]
+        r1 = (xt_s[group, :, at].astype(F32) + term).astype(BF)
+        r1_ref[0, :, at] = r1
+        center, inverse, mean = center_of(r1.astype(F32))
+        a2_ref[0, :, at] = (center * inverse * small[:, 1:2] + small[:, 6:7]).astype(BF)
+        norm2_ref[group, :8, at] = jnp.broadcast_to(mean, (8, seq))
+        norm2_ref[group, 8:, at] = jnp.broadcast_to(inverse, (8, seq))
+
     def heads(side, last):
         mine = pl.ds(pl.multiple_of(side * side_rows, side_rows), side_rows)
         qkv = qkv_ref.at[0]
-        small = early[..., cols:].reshape(d, LANES)
-        if sides > 1:
-            sides_small = early[pl.ds(side * (early.shape[0] // sides), early.shape[0] // sides), :, :, cols:] if len(early.shape) == 4 else early[mine, cols:]
-            bias = sides_small.reshape(side_rows, LANES).astype(F32)
+        if early.ndim == 4:
+            part = early.shape[0] // sides
+            bias = early[pl.ds(side * part, part), :, :, cols:].reshape(side_rows, LANES)
         else:
-            bias = small.astype(F32)
+            bias = early[mine, cols:]
+        bias = bias.astype(F32)
         query = (dot(wqkv_t[:side_rows], a1_s[group]) + bias[:, 3:4]).astype(BF)
         qkv[:side_rows] = (query.astype(F32) * scale).astype(BF)
         qkv[side_rows : 2 * side_rows] = dot(wqkv_t[side_rows : 2 * side_rows], a1_s[group]).astype(BF)
@@ -322,15 +367,18 @@
             inv_ref[side, group, pl.ds(s * side_heads + h, 1), :] = inverse
             to = pl.ds(pl.multiple_of(side * side_rows + h * head, head), head)
             ct_ref[group, to, seq * s : seq * (s + 1)] = (mixed[:head] * inverse).astype(BF)
-            if last and h == side_heads - 1:
-                at = slice(seq * s, seq * (s + 1))
-                term = dot(wo_t[...], ct_ref[group, :, at]) + small[:, 5:6].astype(F32)
-                r1_ref[group, :, at] = (xt_s[group, :, at].astype(F32) + term).astype(r1_ref.dtype)
+            if last and h == 0:
+                attended(jnp.maximum(group - 1, 0), s)
 
         pipelined(items, 3, 2, score, soften, mix)
 
     pl.when((stage > 0) & (stage < sides))(lambda: heads(stage - 1, False))
     pl.when(stage == sides)(lambda: heads(sides - 1, True))
+
+    @pl.when(stage > sides)
+    def _():
+        for s in range(many):
+            attended(groups - 1, s)
 
 
     if gathers:
@@ -348,52 +396,35 @@
 def plan_forward(enter, first, late, out, up, down):
     plan = {
         0: [enter],
-        2: [first.relay, late.start, out.start, up.start],
+        2: [first.relay, late.start, out.start],
         3: [late.spread, out.spread],
-        4: [first.cross, late.relay, first.share, out.relay, up.spread, down.start, first.finish],
-        5: [late.cross, out.cross, up.relay, down.spread],
-        6: [late.share, out.share],
-        7: [down.relay, up.cross],
-        8: [late.finish, out.finish],
-        9: [down.cross, up.share],
+        4: [first.cross, late.relay, first.share, out.relay, up.start, first.finish],
+        5: [late.cross, out.cross, up.spread, down.start],
+        6: [late.share, out.share, down.spread, up.relay],
+        8: [late.finish, out.finish, down.relay],
+        9: [up.cross],
+        10: [down.cross, up.share],
         11: [down.share],
     }
     return plan, [up.finish, down.finish]
 
 
 def forward_kernel(
-    r1_ref, g_first, g_next, early_ref, wu_ref, wd_ref,
+    r1_ref, a2_ref, gt_ref, norm2_ref, gsum_ref, early_ref, wu_ref, wd_ref,
     out_ref, do_ref, dwu_ref, dwd_ref, small_ref,
-    wu_t, wd_t, total_wu, total_wd, gt, gt_next, a2, a2_next, normed, inverse, total_out, total_a2,
-    u_s, dh_s, h_s, du_s, sums, sums_up, up_bias, *, block,
+    wu_t, wd_t, total_wu, total_wd, total_out, total_a2, u_s, dh_s, h_s, du_s, sums, sums_up, up_bias, *, block,
 ):
     step = pl.program_id(0)
-    groups, d, width = r1_ref.shape
+    d, tokens = r1_ref.shape[1:]
     hidden = wu_t.shape[0]
     n_dev = dwd_ref.shape[0] * 2
     rows = d // n_dev
-    seqs, seq = g_next.shape[:2]
-    many = width // seq
+    seqs, seq = out_ref.shape[:2]
     cols = early_ref.shape[-1] - LANES
     column = early_ref[..., cols:].reshape(d, LANES).astype(F32)
     blocks = hidden // block
     slots = h_s.shape[0]
-
-    def at_of(chunk, s):
-        which = chunk * seqs + s
-        lane = pl.multiple_of(lax.rem(which, many) * seq, seq)
-        return which // many, slice(None), pl.ds(lane, seq)
-
-    def prepare(chunk, g_ref, gt_to, a2_to):
-        for s in range(seqs):
-            at = slice(seq * s, seq * (s + 1))
-            gt_to[:, at] = g_ref[s].T
-            r1 = r1_ref[at_of(chunk, s)].astype(F32)
-            n, inv = normalize(r1)
-            a2_to[:, at] = (n * column[:, 1:2] + column[:, 6:7]).astype(BF)
-            normed[:, at] = n
-            inverse[:, at] = jnp.broadcast_to(inv, (8, seq))
-            total_out[:, at] = r1 + column[:, 7:8]
+    a2, gt = a2_ref.at[0], gt_ref.at[0]
 
     @pl.when(step == 0)
     def _():
@@ -405,7 +436,6 @@
             up_bias[:, r * rows : (r + 1) * rows, :] = jnp.broadcast_to(
                 column[:, 8 + r : 9 + r].reshape(n_dev, rows, 1), (n_dev, rows, LANES)
             )
-        prepare(0, g_first, gt, a2)
 
     per = block // (hidden // n_dev)
 
@@ -435,7 +465,8 @@
         sums_up[span(j)] += lane_sums(du.astype(F32))
 
     def leave(j):
-        total_out[...] += dot(wd_t[:, span(j)], h_s[j % slots])
+        term = dot(wd_t[:, span(j)], h_s[j % slots])
+        total_out[...] = term if j == 0 else total_out[...] + term
         term = dot(wu_ref[..., span(j)].reshape(d, block), du_s[j % slots])
         total_a2[...] = term if j == 0 else total_a2[...] + term
 
@@ -452,15 +483,16 @@
         dwu_ref[..., span(j)] = term.astype(BF).reshape(*dwu_ref.shape[:3], block)
 
     def close():
-        da2, n, g = total_a2[...], normed[...], gt[...].astype(F32)
-        dr1 = (g + normalize_back(da2, n, inverse[0:1], column[:, 1:2])).astype(BF)
         for s in range(seqs):
             at = slice(seq * s, seq * (s + 1))
-            out_ref[s] = total_out[:, at].astype(BF).T
-            do_ref[at_of(step, s)] = dr1[:, at]
-        sums[0] += lane_sums(da2 * n)
-        sums[1] += lane_sums(da2)
-        sums[2] += lane_sums(g)
+            r1, g = r1_ref[0, :, at].astype(F32), gt[:, at].astype(F32)
+            out_ref[s] = (r1 + total_out[:, at] + column[:, 7:8]).astype(BF).T
+            da2, inverse = total_a2[:, at], norm2_ref[step, 8:9, at]
+            n = (r1 - norm2_ref[step, 0:1, at]) * inverse
+            dr1 = g + normalize_back(da2, n, inverse, column[:, 1:2])
+            do_ref[step, :, at] = dr1.astype(BF)
+            sums[0] += lane_sums(da2 * n)
+            sums[1] += lane_sums(da2)
 
     enter(0)
     for j in range(blocks):
@@ -475,16 +507,13 @@
     weights(blocks - 2)
     close()
     weights(blocks - 1)
-    prepare(jnp.minimum(step + 1, pl.num_programs(0) - 1), g_next, gt_next, a2_next)
-    gt[...] = gt_next[...]
-    a2[...] = a2_next[...]
 
     @pl.when(step == pl.num_programs(0) - 1)
     def _():
         lane = lax.broadcasted_iota(jnp.int32, (d, LANES), 1)
         small = jnp.zeros((d, LANES), F32)
-        for s, at in ((0, 1), (1, 6), (2, 7)):
-            small = jnp.where(lane == at, jnp.sum(sums[s], 1, keepdims=True), small)
+        for total, at in ((sums[0], 1), (sums[1], 6), (gsum_ref[...], 7)):
+            small = jnp.where(lane == at, jnp.sum(total, 1, keepdims=True), small)
         up = jnp.sum(sums_up[...], 1, keepdims=True).reshape(n_dev, hidden // n_dev, 1)
         for r in range(hidden // d):
             part = up[:, r * rows : (r + 1) * rows].reshape(d, 1)
@@ -724,7 +753,7 @@
         n_slots = total_qkv.shape[1]
         for part in range(2):
             at = slice(part * n_slots // 2, (part + 1) * n_slots // 2)
-            term = dot(n1_ref[group, part * d // 2 : (d // 2, d + 16)[part]], to[...], NT)
+            term = dot(n1_ref[0, part * d // 2 : (d // 2, d + 16)[part]], to[...], NT)
             product = term[: d // 2].reshape(n_slots // 2, *total_qkv.shape[2:])
             total_qkv[side, at] = jnp.where(opening, product, total_qkv[side, at] + product)
         row = term[d // 2 : d // 2 + 8]
@@ -747,7 +776,7 @@
 
         def finish(s, _, da1):
             at = slice(seq * s, seq * (s + 1))
-            normed = n1_ref[group, :d, at].astype(F32)
+            normed = n1_ref[0, :d, at].astype(F32)
             dv = normalize_back(da1, normed, inv1_ref[group, 0:1, at], gain)
             tg_ref[s] = (do_ref[group, :, at].astype(F32) + dv).astype(BF).T
 
@@ -791,21 +820,27 @@
     return plan, [qkv1.step3, small.step3, qkv1.step4, small.step4]
 
 
-def finish_kernel(tg, qkv, out, up, down, small, tg_to, qkv_to, out_to, up_to, down_to, gains, biases, upb, turn):
-    tg_to[...] = tg[...]
-
-    @pl.when(pl.program_id(0) == 0)
-    def _():
-        for source, to in ((qkv, qkv_to), (out, out_to), (up, up_to), (down, down_to)):
-            to[...] = source[...]
-        rows = small.shape[0]
-        turn[...] = jnp.zeros_like(turn)
-        turn[:rows] = small[...]
-        turned = turn[...].T
-        gains[...] = turned[0:2, :rows]
-        biases[...] = turned[2:8, :rows]
-        for r in range(upb.shape[1] // rows):
-            upb[:, r * rows : (r + 1) * rows] = turned[8 + r : 9 + r, :rows]
+def finish_kernel(tg, qkv, out, up, down, small, tg_to, qkv_to, out_to, up_to, down_to, gains, biases, upb, held, turn, sems):
+    pieces = range(tg.shape[0])
+    inward = [pltpu.make_async_copy(tg.at[s], held.at[s], sems.at[0, s]) for s in pieces]
+    outward = [pltpu.make_async_copy(held.at[s], tg_to.at[s], sems.at[1, s]) for s in pieces]
+    for copy in inward:
+        copy.start()
+    for source, to in ((qkv, qkv_to), (out, out_to), (up, up_to), (down, down_to)):
+        to[...] = source[...]
+    rows = small.shape[0]
+    turn[...] = jnp.zeros_like(turn)
+    turn[:rows] = small[...]
+    turned = turn[...].T
+    gains[...] = turned[0:2, :rows]
+    biases[...] = turned[2:8, :rows]
+    for r in range(upb.shape[1] // rows):
+        upb[:, r * rows : (r + 1) * rows] = turned[8 + r : 9 + r, :rows]
+    for copy, then in zip(inward, outward):
+        copy.wait()
+        then.start()
+    for copy in outward:
+        copy.wait()
 
 
 def in_hbm(*arrays):
@@ -849,19 +884,33 @@
         pltpu.HBM((sides * groups, *probs_block[1:]), BF),
         pltpu.VMEM((sides, groups, many * side_heads, seq), F32),
         pltpu.VMEM((groups, d, width), BF),
-        pltpu.VMEM((groups, d, width), R1),
-        pltpu.VMEM((groups, d + 16, width), BF),
+        pltpu.HBM((groups, d + 16, width), BF),
         pltpu.VMEM((groups, 8, width), F32),
+        pltpu.HBM((groups, d, width), BF),
+        pltpu.HBM((groups, d, width), BF),
+        pltpu.HBM((groups, d, width), BF),
+        pltpu.VMEM((groups, 16, width), F32),
+        pltpu.VMEM((d, LANES), F32),
     ]
     held_specs = [vmem] * len(held)
-    held_specs[0] = pl.BlockSpec((1, cols, width), lambda i: (jnp.maximum(i - groups, 0), 0, 0))
+    def working(i):
+        return jnp.clip(i - groups, 0, sides * groups - 1)
+
+    held_specs[0] = pl.BlockSpec((1, cols, width), lambda i: (working(i), 0, 0))
+    held_specs[4] = pl.BlockSpec(
+        (1, d + 16, width), lambda i: (jnp.minimum(i, groups - 1), 0, 0)
+    )
+    closing = pl.BlockSpec(
+        (1, d, width), lambda i: (jnp.maximum(i - sides * groups - 1, 0), 0, 0)
+    )
+    held_specs[6] = held_specs[7] = closing
+    held_specs[8] = pl.BlockSpec((1, d, width), lambda i: (jnp.minimum(i, groups - 1), 0, 0))
     held_specs[1] = pl.BlockSpec(
-        probs_block, lambda i: (jnp.maximum(i - groups, 0), 0, 0, 0, 0)
+        probs_block, lambda i: (working(i), 0, 0, 0, 0)
     )
     in_specs = [
         smem,
-        pl.BlockSpec((many, seq, d), lambda i: (jnp.minimum(i, groups - 1), 0, 0)),
-    ]
+    ] + [pl.BlockSpec((many, seq, d), lambda i: (jnp.minimum(i, groups - 1), 0, 0))] * 2
     scratch = [
         pltpu.VMEM((cols, d), BF),
         pltpu.VMEM((d, d), BF),
@@ -873,9 +922,9 @@
     if direct:
         n_sends = Gather.sends(n_z)
         shards = in_hbm(qkv_w, out_w, up_w, down_w, gains, biases, up_bias.reshape(1, -1))
-        qkv, probs, inv, ct, r1, n1, inv1, early, late, wo, wu, wd = pl.pallas_call(
+        qkv, probs, inv, ct, n1, inv1, r1, a2, gt, norm2, gsum, early, late, wo, wu, wd = pl.pallas_call(
             functools.partial(attention_kernel, (n_dp, n_z), True, sides, groups),
-            grid=(steps,),
+            grid=(steps + 1,),
             in_specs=in_specs + [whole(s.shape) for s in shards],
             out_specs=held_specs + [vmem] * 5,
             out_shape=held
@@ -904,7 +953,7 @@
             ],
             compiler_params=params(VMEM_FORWARD, collective_id=0, has_side_effects=True),
             name="attention_forward",
-        )(lengths, tokens, *shards)
+        )(lengths, tokens, cotangent, *shards)
     else:
         split = [
             jnp.concatenate([qkv_w[:, p * d + i * side_rows :][:, :side_rows] for p in range(3)], 1)
@@ -920,25 +969,24 @@
         wo = lax.all_gather(out_w.astype(BF), axes, axis=0, tiled=True)
         wu = lax.all_gather(up_w.astype(BF), axes, axis=0, tiled=True)
         wd = lax.all_gather(down_w.astype(BF), axes, axis=0, tiled=True)
-        qkv, probs, inv, ct, r1, n1, inv1 = pl.pallas_call(
+        qkv, probs, inv, ct, n1, inv1, r1, a2, gt, norm2, gsum = pl.pallas_call(
             functools.partial(attention_kernel, (n_dp, n_z), False, sides, groups),
-            grid=(steps,),
+            grid=(steps + 1,),
             in_specs=in_specs + [whole(early.shape), whole(late.shape), whole(wo.shape)],
             out_specs=held_specs,
             out_shape=held,
             scratch_shapes=scratch,
             compiler_params=params(VMEM_FORWARD),
             name="attention_forward",
-        )(lengths, tokens, early, late, wo)
+        )(lengths, tokens, cotangent, early, late, wo)
+
+    r1, a2, gt, n1, qkv, probs = in_hbm(r1, a2, gt, n1, qkv, probs)
 
     def weight(array):
         return vmem if direct else whole(array.shape)
 
-    pair = 2 if seqs % 2 == 0 else 1
-    chunk = pair * seq
-    chunks = seqs // pair
-    block = d // 2
-    lag = 4
+    block = d
+    lag = 2
     parts = [
         pltpu.VMEM((cut // 2, 2, d // cut, hidden), BF),
         pltpu.VMEM((cut // 2, 2, hidden // cut, d), BF),
@@ -949,16 +997,11 @@
         part_specs = [whole(part.shape) for part in parts]
     out, do, dwu, dwd, small = pl.pallas_call(
         functools.partial(forward_kernel, block=block),
-        grid=(chunks,),
-        in_specs=[
-            vmem,
-            whole((pair, seq, d)),
-            pl.BlockSpec((pair, seq, d), lambda i: (jnp.minimum(i + 1, chunks - 1), 0, 0)),
-            weight(early),
-            weight(wu),
-            weight(wd),
-        ],
-        out_specs=[pl.BlockSpec((pair, seq, d), lambda i: (i, 0, 0)), vmem]
+        grid=(groups,),
+        in_specs=[pl.BlockSpec((1, d, width), lambda i: (i, 0, 0))] * 3
+        + [vmem] * 2
+        + [weight(early), weight(wu), weight(wd)],
+        out_specs=[pl.BlockSpec((many, seq, d), lambda i: (i, 0, 0)), vmem]
         + part_specs
         + [whole((d, LANES))],
         out_shape=[pltpu.HBM(tokens.shape, BF), pltpu.VMEM((groups, d, width), BF)]
@@ -966,23 +1009,22 @@
         + [shape((d, LANES), F32)],
         scratch_shapes=[pltpu.VMEM((hidden, d), BF), pltpu.VMEM((d, hidden), BF)]
         + [pltpu.VMEM((d, hidden), F32), pltpu.VMEM((hidden, d), F32)]
-        + [pltpu.VMEM((d, chunk), BF)] * 4
-        + [pltpu.VMEM((d, chunk), F32), pltpu.VMEM((8, chunk), F32)]
-        + [pltpu.VMEM((d, chunk), F32)] * 2
-        + [pltpu.VMEM((2, block, chunk), F32)] * 2
-        + [pltpu.VMEM((lag, block, chunk), BF)] * 2
+        + [pltpu.VMEM((d, width), F32)] * 2
+        + [pltpu.VMEM((2, block, width), F32)] * 2
+        + [pltpu.VMEM((lag, block, width), BF)] * 2
         + [
-            pltpu.VMEM((3, d, LANES), F32),
+            pltpu.VMEM((2, d, LANES), F32),
             pltpu.VMEM((hidden, LANES), F32),
             pltpu.VMEM((cut, hidden // cut, LANES), F32),
         ],
         compiler_params=params(VMEM_MIDDLE if direct else VMEM_MIDDLE + 16),
         name="feed_forward",
-    )(r1, cotangent, cotangent, early, wu, wd)
+    )(r1, a2, gt, norm2, gsum, early, wu, wd)
 
     seq_block = pl.BlockSpec((many, seq, d), lambda i: (jnp.maximum(i - sides * groups, 0), 0, 0))
     acts = (do, ct, qkv, probs, inv, n1, inv1, early, late, wo, small)
     acts_in = [vmem] * 7 + [weight(early), weight(late), weight(wo), whole((d, LANES))]
+    acts_in[5] = pl.BlockSpec((1, d + 16, width), lambda i: (lax.rem(i, groups), 0, 0))
     acts_in[2] = pl.BlockSpec(
         (1, cols, width), lambda i: (jnp.minimum(i, sides * groups - 1), 0, 0)
     )
@@ -1021,14 +1063,16 @@
         )(*acts, dwu, dwd)
         ends = [shape(tokens.shape, BF)] + [shape(o, F32) for o in outs[:4]]
         vectors = [shape(v, F32) for v in (gains.shape, biases.shape, (1, quarter * rows))]
-        seq_block = pl.BlockSpec((many, seq, d), lambda i: (i, 0, 0))
         token_grad, gqkv, gout, gup, gdown, ggains, gbiases, gupb = pl.pallas_call(
             finish_kernel,
-            grid=(groups,),
-            in_specs=[seq_block] + [whole(o) for o in outs],
-            out_specs=[seq_block] + [whole(o.shape) for o in ends[1:] + vectors],
+            in_specs=[anywhere] + [vmem] * 5,
+            out_specs=[anywhere] + [vmem] * 7,
             out_shape=ends + vectors,
-            scratch_shapes=[pltpu.VMEM((LANES, LANES), F32)],
+            scratch_shapes=[
+                pltpu.VMEM(tokens.shape, BF),
+                pltpu.VMEM((LANES, LANES), F32),
+                pltpu.SemaphoreType.DMA((2, seqs)),
+            ],
             compiler_params=params(60),
             name="hand_over",
         )(*grads)

time: 164 us -> 163 us (level)
    pallas_call x2, Pallas kernels: 61.2 us -> 58 us  [the longest x1 53.4 us: per_device(): pl.pallas_call(functools.partial(forward_kernel, block=block), grid=(grou...]
    pallas_call x1, Pallas kernels: 51.3 us -> 53.1 us  [per_device(): pl.pallas_call(functools.partial(attention_kernel, (n_dp, n_z), True, sid...]
where the time goes in v5:
time: 163 us
  Pallas kernels  162 us (99%)
    pallas_call x1, Pallas kernels, per_device(): pl.pallas_call(functools.partial(forward_kernel, block=block), grid=(grou...  53.4 us
    pallas_call x1, Pallas kernels, per_device(): pl.pallas_call(functools.partial(attention_kernel, (n_dp, n_z), True, sid...  53.1 us
    pallas_call x1, Pallas kernels, per_device(): pl.pallas_call(functools.partial(backward_kernel, (n_dp, n_z), True, side...  51.3 us
    pallas_call x1, Pallas kernels, per_device(): pl.pallas_call(finish_kernel, in_specs=[anywhere] + [vmem] * 5, out_specs...  4.6 us

profile of v5, /device:TPU:0, one launch (start us, length us, event | category | flops | bytes accessed | tf_op | source)
XLA Modules:
  0.0 163.2 jit_solution(13273397101881899985)
XLA Ops:
  0.6 53.1 %attention_forward.1 = (bf16[8,768,768]{2,1,0:T(8,128)(2,1)}, bf16[8,3,4,256,256]{4,3,2,1,0:T(8,128)(2,1)}, f32[2,4,12,256]{3,2,1,0:T(8,128)S(1)}, bf16[4,512,76...) custom-call(s32[12]{0:T(128)} %lengths.1, ...), custom_call_target="tpu_custom_call" | custom-call | tf_op jit(solution)/shard_map/attention_forward/pallas_call | solution.py:925
  53.7 53.4 %feed_forward.1 = (bf16[12,256,512]{2,1,0:T(8,128)(2,1)}, bf16[4,512,768]{2,1,0:T(8,128)(2,1)S(1)}, bf16[16,2,16,2048]{3,2,1,0:T(8,128)(2,1)S(1)}, bf16[16,2,64,512]{3,2,1,0:T(8,128)(2,1)S(1)}, f32[512,128]{1,0:T(8,128)S(1)}) custom-call(bf16[4,512,768]{2,1,0:T(8,128)(2,1)} %get-tuple-element.44.r1_ref, bf16[4,512,768]{2,1,0:T(8,128)(2,1)} %get-tuple-element.45.a2_ref, ...), custom_call_target="tpu_custom_call" | custom-call | tf_op jit(solution)/shard_map/feed_forward/pallas_call | solution.py:998
  107.1 51.3 %attention_backward.1 = (bf16[12,256,512]{2,1,0:T(8,128)(2,1)}, f32[16,1536]{1,0:T(8,128)}, f32[16,512]{1,0:T(8,128)}, f32[16,2048]{1,0:T(8,128)}, f32[64,512]{1,0:T(8,128)}, /*index=5*/f32[16,128]{1,0:T(8,128)}) custom-call(bf16[4,512,768]{2,1,0:T(8,128)(2,1)S(1)} %get-tuple-element.53.refs_0_, bf16[4,512,768]{2,1,0:T(8,128)(2,1)S(1)} %get-tuple-element.54.refs_1_, ...), custom_call_target="tpu_custom_call" | custom-call | tf_op jit(solution)/shard_map/attention_backward/pallas_call | solution.py:1054
  158.4 4.6 %hand_over.1 = (bf16[12,256,512]{2,1,0:T(8,128)(2,1)}, f32[16,1536]{1,0:T(8,128)}, f32[16,512]{1,0:T(8,128)}, f32[16,2048]{1,0:T(8,128)}, f32[64,512]{1,0:T(8,12...) custom-call(bf16[12,256,512]{2,1,0:T(8,128)(2,1)} %get-tuple-element.65.tg, ...), custom_call_target="tpu_custom_call" | custom-call | tf_op jit(solution)/shard_map/hand_over/pallas_call | solution.py:1066

commit v6 on v5

--- a/solution.py
+++ b/solution.py
@@ -389,7 +389,8 @@
                 to[...] = whole[...]
             for action in after:
                 action()
-            for whole, to in ((wu, wu_ref), (wd, wd_ref)):
+            for last_gather, whole, to in ((up, wu, wu_ref), (down, wd, wd_ref)):
+                last_gather.finish()
                 to[...] = whole[...]
 
 
@@ -403,10 +404,10 @@
         6: [late.share, out.share, down.spread, up.relay],
         8: [late.finish, out.finish, down.relay],
         9: [up.cross],
-        10: [down.cross, up.share],
-        11: [down.share],
+        10: [up.share, down.cross],
+        12: [down.share],
     }
-    return plan, [up.finish, down.finish]
+    return plan, []
 
 
 def forward_kernel(
@@ -457,10 +458,11 @@
         u = u_s[j % 2]
         square = u * u
         part = 0.5 + 0.5 * jnp.tanh(u * (C0 + C1 * square))
-        h = u * part
-        h_s[j % slots] = h.astype(BF)
-        slope = part + h * (1.0 - part) * (2 * C0 + 6 * C1 * square)
-        du = (dh_s[j % 2] * slope).astype(BF)
+        h = (u * part).astype(BF)
+        h_s[j % slots] = h
+        part = part.astype(BF)
+        slope = part + h * (1.0 - part) * (2 * C0 + 6 * C1 * square).astype(BF)
+        du = dh_s[j % 2].astype(BF) * slope
         du_s[j % slots] = du
         sums_up[span(j)] += lane_sums(du.astype(F32))
 
@@ -813,11 +815,10 @@
         5: [up.step3, down2.step3, qkv0.step2, out.step2],
         7: [down.step3],
         8: [packs[1], qkv1.step1, pack_small, small.step1, up.step4, down2.step4],
-        9: [qkv1.step2, small.step2, qkv0.step3, out.step3],
-        10: [down.step4],
-        11: [qkv0.step4, out.step4],
+        9: [qkv1.step2, small.step2],
+        10: [qkv0.step3, out.step3, down.step4],
     }
-    return plan, [qkv1.step3, small.step3, qkv1.step4, small.step4]
+    return plan, [qkv1.step3, small.step3, qkv0.step4, out.step4, qkv1.step4, small.step4]
 
 
 def finish_kernel(tg, qkv, out, up, down, small, tg_to, qkv_to, out_to, up_to, down_to, gains, biases, upb, held, turn, sems):

time: 163 us -> 161 us (0.988)
  Pallas kernels: 162 us -> 160 us
where the time goes in v6:
time: 161 us
  Pallas kernels  160 us (99%)
    pallas_call x1, Pallas kernels, per_device(): pl.pallas_call(functools.partial(forward_kernel, block=block), grid=(grou...  52.6 us
    pallas_call x1, Pallas kernels, per_device(): pl.pallas_call(functools.partial(attention_kernel, (n_dp, n_z), True, sid...  52.5 us
    pallas_call x1, Pallas kernels, per_device(): pl.pallas_call(functools.partial(backward_kernel, (n_dp, n_z), True, side...  50.3 us
    pallas_call x1, Pallas kernels, per_device(): pl.pallas_call(finish_kernel, in_specs=[anywhere] + [vmem] * 5, out_specs...  4.6 us

profile of v6, /device:TPU:0, one launch (start us, length us, event | category | flops | bytes accessed | tf_op | source)
XLA Modules:
  0.0 160.8 jit_solution(15604580785639376073)
XLA Ops:
  0.6 52.5 %attention_forward.1 = (bf16[8,768,768]{2,1,0:T(8,128)(2,1)}, bf16[8,3,4,256,256]{4,3,2,1,0:T(8,128)(2,1)}, f32[2,4,12,256]{3,2,1,0:T(8,128)S(1)}, bf16[4,512,76...) custom-call(s32[12]{0:T(128)} %lengths.1, ...), custom_call_target="tpu_custom_call" | custom-call | tf_op jit(solution)/shard_map/attention_forward/pallas_call | solution.py:926
  53.2 52.6 %feed_forward.1 = (bf16[12,256,512]{2,1,0:T(8,128)(2,1)}, bf16[4,512,768]{2,1,0:T(8,128)(2,1)S(1)}, bf16[16,2,16,2048]{3,2,1,0:T(8,128)(2,1)S(1)}, bf16[16,2,64,512]{3,2,1,0:T(8,128)(2,1)S(1)}, f32[512,128]{1,0:T(8,128)S(1)}) custom-call(bf16[4,512,768]{2,1,0:T(8,128)(2,1)} %get-tuple-element.44.r1_ref, bf16[4,512,768]{2,1,0:T(8,128)(2,1)} %get-tuple-element.45.a2_ref, ...), custom_call_target="tpu_custom_call" | custom-call | tf_op jit(solution)/shard_map/feed_forward/pallas_call | solution.py:999
  105.8 50.3 %attention_backward.1 = (bf16[12,256,512]{2,1,0:T(8,128)(2,1)}, f32[16,1536]{1,0:T(8,128)}, f32[16,512]{1,0:T(8,128)}, f32[16,2048]{1,0:T(8,128)}, f32[64,512]{1,0:T(8,128)}, /*index=5*/f32[16,128]{1,0:T(8,128)}) custom-call(bf16[4,512,768]{2,1,0:T(8,128)(2,1)S(1)} %get-tuple-element.53.refs_0_, bf16[4,512,768]{2,1,0:T(8,128)(2,1)S(1)} %get-tuple-element.54.refs_1_, ...), custom_call_target="tpu_custom_call" | custom-call | tf_op jit(solution)/shard_map/attention_backward/pallas_call | solution.py:1055
  156.1 4.6 %hand_over.1 = (bf16[12,256,512]{2,1,0:T(8,128)(2,1)}, f32[16,1536]{1,0:T(8,128)}, f32[16,512]{1,0:T(8,128)}, f32[16,2048]{1,0:T(8,128)}, f32[64,512]{1,0:T(8,12...) custom-call(bf16[12,256,512]{2,1,0:T(8,128)(2,1)} %get-tuple-element.65.tg, ...), custom_call_target="tpu_custom_call" | custom-call | tf_op jit(solution)/shard_map/hand_over/pallas_call | solution.py:1067
